TPU v7x, 512 devices: a whole 4x4x16 slice. The times are simulated.
512 devices in a mesh: tx: 32 (over x, y, core), ty: 16 (over z).
Axes of the slice: x: 4, y: 4, z: 16, core: 2. Of those that a mesh axis runs over, the one named last changes fastest.
Arguments:
- source: float32 [20, 512, 2048], P(None, 'tx', 'ty'), may hold values from -6 to 6
- kappa_sq: float32 [20, 512, 2048], P(None, 'tx', 'ty'), may hold values from 0.05 to 0.5
- lon_diff: float32 [20, 512, 2048], P(None, 'tx', 'ty'), may hold values from 8 to 64
- lat_diff: float32 [20, 512, 2048], P(None, 'tx', 'ty'), may hold values from 8 to 64
- sea_mask: int32 [20, 512, 2048], P(None, 'tx', 'ty'), may hold values 0 or 1
Outputs:
- solution: float32 [20, 512, 2048], P(None, 'tx', 'ty')
- residual: float32 [20, 512, 2048], P(None, 'tx', 'ty')
All inputs are finite; a program needn't handle non-finite values. No bound on the sum of `sea_mask` on one device may be relied on, other than what follows from the above.
Results may differ from a plain program's by a relative error of at most 0.0003.
Values sent between devices are 32-bit elements; how exact they have to be, the bound alone decides.
A program may use at most 128 MiB of HBM per device.

v0:
```python
import jax
import jax.numpy as jnp
from jax import lax
from jax.sharding import PartitionSpec as P

LEVELS = 4
COARSE_SWEEPS = 20


OMEGA = 0.8
VERT = 1.0


def extended(block, sides, width, periodic):
    for axis, dim in sides:
        count = lax.axis_size(axis)
        forward = [(i, i + 1) for i in range(count - 1)]
        if periodic:
            forward.append((count - 1, 0))
        backward = [(target, source) for source, target in forward]
        low = lax.ppermute(
            lax.slice_in_dim(block, block.shape[dim] - width, None, axis=dim), axis, forward
        )
        high = lax.ppermute(lax.slice_in_dim(block, 0, width, axis=dim), axis, backward)
        block = jnp.concatenate([low, block, high], axis=dim)
    return block


def shift_up(field):
    return jnp.concatenate([field[1:], jnp.zeros_like(field[:1])], axis=0)


def shift_down(field):
    return jnp.concatenate([jnp.zeros_like(field[:1]), field[:-1]], axis=0)


def lon_tiles(stack):
    return extended(stack, (("tx", 2),), 1, True)


def lat_tiles(stack):
    return extended(stack, (("ty", 3),), 1, False)


def rim_tiles(field):
    return extended(field, (("tx", 1), ("ty", 2)), 1, True)


def build_faces(kappa, lond, latd, sea, lon_pad, lat_pad):
    lon_weight = sea * lond
    lat_weight = sea * latd
    lon_ext = lon_pad(jnp.stack([lon_weight, sea]))
    lat_ext = lat_pad(jnp.stack([lat_weight, sea]))
    face_east = 0.5 * (lon_weight * lon_ext[1, :, 2:, :] + sea * lon_ext[0, :, 2:, :])
    face_west = 0.5 * (lon_weight * lon_ext[1, :, :-2, :] + sea * lon_ext[0, :, :-2, :])
    face_north = 0.5 * (lat_weight * lat_ext[1, :, :, 2:] + sea * lat_ext[0, :, :, 2:])
    face_south = 0.5 * (lat_weight * lat_ext[1, :, :, :-2] + sea * lat_ext[0, :, :, :-2])
    face_up = VERT * sea * shift_up(sea)
    face_down = VERT * sea * shift_down(sea)
    diagonal = (
        sea * kappa
        + (face_west + face_east + face_south + face_north + face_down + face_up)
        + (1.0 - sea)
    )
    return (face_west, face_east, face_south, face_north, face_down, face_up, diagonal)


def apply_op(field, faces, rim_pad):
    ext = rim_pad(field)
    total = (
        faces[0] * ext[:, :-2, 1:-1]
        + faces[1] * ext[:, 2:, 1:-1]
        + faces[2] * ext[:, 1:-1, :-2]
        + faces[3] * ext[:, 1:-1, 2:]
        + faces[4] * shift_down(field)
        + faces[5] * shift_up(field)
    )
    return faces[6] * field - total


def sweep(field, right, faces, rim_pad):
    return field + OMEGA * (right - apply_op(field, faces, rim_pad)) / faces[6]


def block_mean(field):
    depth, wide, tall = field.shape
    return field.reshape(depth, wide // 2, 2, tall // 2, 2).mean(axis=(2, 4))


def block_max(field):
    depth, wide, tall = field.shape
    return field.reshape(depth, wide // 2, 2, tall // 2, 2).max(axis=(2, 4))


def prolong(field):
    return jnp.repeat(jnp.repeat(field, 2, axis=1), 2, axis=2)


def coarsen(params):
    kappa, lond, latd, sea = params
    return (block_mean(kappa), 0.25 * block_mean(lond), 0.25 * block_mean(latd), block_max(sea))


def coarse_sweeps(right, faces, rim_pad):
    field = OMEGA * right / faces[6]

    def step_fn(step, current):
        return sweep(current, right, faces, rim_pad)

    return lax.fori_loop(0, COARSE_SWEEPS - 1, step_fn, field)


def coarse_solve(params, right):
    kappa, lond, latd, sea = params
    faces = build_faces(kappa, lond, latd, sea, lon_tiles, lat_tiles)
    return coarse_sweeps(right, faces, rim_tiles)


def cycle(level, right, params, faces_all):
    if level == LEVELS:
        return coarse_solve(params[LEVELS], right)
    faces = faces_all[level]
    field = OMEGA * right / faces[6]
    field = sweep(field, right, faces, rim_tiles)
    remain = right - apply_op(field, faces, rim_tiles)
    correction = cycle(level + 1, block_mean(remain), params, faces_all)
    field = field + prolong(correction)
    field = sweep(field, right, faces, rim_tiles)
    field = sweep(field, right, faces, rim_tiles)
    return field


def shards(source, kappa_sq, lon_diff, lat_diff, sea_mask):
    sea = sea_mask.astype(jnp.float32)
    params = [(kappa_sq, lon_diff, lat_diff, sea)]
    for level in range(LEVELS):
        params.append(coarsen(params[-1]))
    faces_all = [build_faces(*params[level], lon_tiles, lat_tiles) for level in range(LEVELS)]
    solution = cycle(0, source, params, faces_all)
    residual = source - apply_op(solution, faces_all[0], rim_tiles)
    return (solution, residual)


def solution(mesh):
    return jax.shard_map(
        shards,
        mesh=mesh,
        in_specs=(
            P(None, "tx", "ty"),
            P(None, "tx", "ty"),
            P(None, "tx", "ty"),
            P(None, "tx", "ty"),
            P(None, "tx", "ty"),
        ),
        out_specs=(P(None, "tx", "ty"), P(None, "tx", "ty")),
        check_vma=False,
    )
```

profile of v0, /device:TPU:1, one launch (start us, length us, event | category | flops | bytes accessed | tf_op | source)
XLA Modules:
  0.0 889.9 jit_solution(7451615572215614681)
XLA Ops:
  7.7 6.1 collective-permute-start.5
  54.8 8.6 collective-permute-start.9
  81.9 6.5 collective-permute-start.13
  91.2 5.3 collective-permute-start.15
  98.5 8.0 collective-permute-start.17
  113.2 7.3 collective-permute-start.21
  137.3 8.8 collective-permute-start.25
  149.5 5.3 collective-permute-start.27
  157.6 8.0 collective-permute-start.29
  181.7 7.5 collective-permute-start.33
  200.0 8.7 collective-permute-start.37
  220.7 7.2 collective-permute-start.41
  230.4 7.0 collective-permute-start.53
  258.4 5.7 collective-permute-start.49
  282.2 413.5 %while.13 = (s32[]{:T(128)}, f32[20,1,8]{0,2,1:T(8,128)S(1)}, f32[20,1,8]{0,2,1:T(8,128)}, f32[20,1,8]{0,2,1:T(8,128)}, f32[20,1,8]{0,2,1:T(8,128)}, /*index=5*/...) while((s32[]{:T(128)}, f32[20,1,8]{0,2,1:T(8,128)S(1)}, ...), condition=%wide.region_29.30_spmd, body=%wide.region_28.29_spmd.sunk | while | flops 3042 | bytes 58389 | solution.py:110
  284.1 8.1 collective-permute-start.1
  307.7 8.2 collective-permute-start.1
  331.0 8.2 collective-permute-start.1
  353.9 8.4 collective-permute-start.1
  376.0 8.4 collective-permute-start.1
  397.5 8.2 collective-permute-start.1
  418.7 8.2 collective-permute-start.1
  440.0 8.2 collective-permute-start.1
  461.2 8.2 collective-permute-start.1
  482.4 8.2 collective-permute-start.1
  503.7 8.2 collective-permute-start.1
  524.9 8.2 collective-permute-start.1
  546.2 8.2 collective-permute-start.1
  567.4 8.2 collective-permute-start.1
  588.6 8.2 collective-permute-start.1
  609.9 8.2 collective-permute-start.1
  631.6 8.4 collective-permute-start.1
  653.6 8.4 collective-permute-start.1
  675.6 8.4 collective-permute-start.1
  697.7 8.4 collective-permute-start.57
  716.6 8.6 collective-permute-start.61
  728.0 5.1 collective-permute-start.63
  735.9 8.4 collective-permute-start.65
  747.0 5.2 collective-permute-start.67
  755.1 8.4 collective-permute-start.69
  766.3 5.1 collective-permute-start.71
  774.4 8.4 collective-permute-start.73
  786.3 5.1 collective-permute-start.75
  798.6 8.6 collective-permute-start.77
  811.2 4.9 collective-permute-start.79
  824.8 8.6 collective-permute-start.81
  847.0 8.7 collective-permute-start.85
  869.3 8.9 %collective-permute-start.89 = (f32[20,1,128]{2,1,0:T(1,128)S(1)}, f32[20,1,128]{2,1,0:T(1,128)S(1)}, u32[]{:S(2)}, u32[]{:S(2)}) collective-permute-start(f32[20,1,128]{2,1,0:T(1,128)S(1)} %get-tuple-element.172), channel_id=1, source_target_pairs={{16,0},{32,16},{48,32},{64,48},{80,64},{96,80},{112,96},{128,112},... | collective-permute-start | bytes 30728 | tf_op jit(solution)/shard_map/ppermute | solution.py:24
  (1003 shorter events, 526.8 us)
Async XLA Ops:
  3.1 43.8 %collective-permute-start.4 = (f32[2,20,1,128]{3,2,1,0:T(1,128)}, f32[2,20,1,128]{3,2,1,0:T(1,128)}, u32[]{:S(2)}, u32[]{:S(2)}) collective-permute-start(f32[2,20,1,128]{3,2,1,0:T(1,128)} %get-tuple-element.127), channel_id=1, source_target_pairs={{0,16},{16,32},{32,48},{48,64},{64,80},{80,96},{96,112},{112,128},... | collective-permute-start | bytes 61448 | tf_op jit(solution)/shard_map/ppermute | solution.py:21
  7.7 43.2 %collective-permute-start.5 = (f32[2,20,1,128]{3,2,1,0:T(1,128)}, f32[2,20,1,128]{3,2,1,0:T(1,128)}, u32[]{:S(2)}, u32[]{:S(2)}) collective-permute-start(f32[2,20,1,128]{3,2,1,0:T(1,128)} %get-tuple-element.128), channel_id=1, source_target_pairs={{16,0},{32,16},{48,32},{64,48},{80,64},{96,80},{112,96},{128,112},... | collective-permute-start | bytes 61448 | tf_op jit(solution)/shard_map/ppermute | solution.py:24
  14.8 26.2 %collective-permute-start.7 = (f32[2,20,16,1]{3,2,1,0:T(8,128)}, f32[2,20,16,1]{3,2,1,0:T(8,128)}, u32[]{:S(2)}, u32[]{:S(2)}) collective-permute-start(f32[2,20,16,1]{3,2,1,0:T(8,128)} %get-tuple-element.125), channel_id=1, source_target_pairs={{1,0},{2,1},{3,2},{4,3},{5,4},{6,5},{7,6},{8,7},{9,8},{10,9},{11,1... | collective-permute-start | bytes 7688 | tf_op jit(solution)/shard_map/ppermute | solution.py:24
  16.1 29.5 %collective-permute-start.6 = (f32[2,20,16,1]{3,2,1,0:T(8,128)}, f32[2,20,16,1]{3,2,1,0:T(8,128)}, u32[]{:S(2)}, u32[]{:S(2)}) collective-permute-start(f32[2,20,16,1]{3,2,1,0:T(8,128)} %get-tuple-element.126), channel_id=1, source_target_pairs={{0,1},{1,2},{2,3},{3,4},{4,5},{5,6},{6,7},{7,8},{8,9},{9,10},{10,1... | collective-permute-start | bytes 7688 | tf_op jit(solution)/shard_map/ppermute | solution.py:21
  39.7 134.1 %collective-permute-start.31 = (f32[2,20,4,1]{1,3,2,0:T(1,128)}, f32[2,20,4,1]{1,3,2,0:T(1,128)S(1)}, u32[]{:S(2)}, u32[]{:S(2)}) collective-permute-start(f32[2,20,4,1]{1,3,2,0:T(1,128)} %get-tuple-element.204), channel_id=1, source_target_pairs={{1,0},{2,1},{3,2},{4,3},{5,4},{6,5},{7,6},{8,7},{9,8},{10,9},{11,1... | collective-permute-start | bytes 1928 | tf_op jit(solution)/shard_map/ppermute | solution.py:24
  41.0 137.4 %collective-permute-start.30 = (f32[2,20,4,1]{1,3,2,0:T(1,128)}, f32[2,20,4,1]{1,3,2,0:T(1,128)}, u32[]{:S(2)}, u32[]{:S(2)}) collective-permute-start(f32[2,20,4,1]{1,3,2,0:T(1,128)} %get-tuple-element.205), channel_id=1, source_target_pairs={{0,1},{1,2},{2,3},{3,4},{4,5},{5,6},{6,7},{7,8},{8,9},{9,10},{10,1... | collective-permute-start | bytes 1928 | tf_op jit(solution)/shard_map/ppermute | solution.py:21
  52.7 10.8 %collective-permute-start.8 = (f32[20,1,128]{2,1,0:T(1,128)S(1)}, f32[20,1,128]{2,1,0:T(1,128)S(1)}, u32[]{:S(2)}, u32[]{:S(2)}) collective-permute-start(f32[20,1,128]{2,1,0:T(1,128)S(1)} %get-tuple-element.198), channel_id=1, source_target_pairs={{0,16},{16,32},{32,48},{48,64},{64,80},{80,96},{96,112},{112,128},... | collective-permute-start | bytes 30728 | tf_op jit(solution)/shard_map/ppermute | solution.py:21
  75.4 12.9 %collective-permute-start.12 = (f32[20,1,128]{2,1,0:T(1,128)S(1)}, f32[20,1,128]{2,1,0:T(1,128)S(1)}, u32[]{:S(2)}, u32[]{:S(2)}) collective-permute-start(f32[20,1,128]{2,1,0:T(1,128)S(1)} %get-tuple-element.194), channel_id=1, source_target_pairs={{0,16},{16,32},{32,48},{48,64},{64,80},{80,96},{96,112},{112,128},... | collective-permute-start | bytes 30728 | tf_op jit(solution)/shard_map/ppermute | solution.py:21
  91.2 15.3 %collective-permute-start.15 = (f32[20,18,1]{2,0,1:T(8,128)S(1)}, f32[20,18,1]{2,0,1:T(8,128)S(1)}, u32[]{:S(2)}, u32[]{:S(2)}) collective-permute-start(f32[20,18,1]{2,0,1:T(8,128)S(1)} %get-tuple-element.164), channel_id=1, source_target_pairs={{1,0},{2,1},{3,2},{4,3},{5,4},{6,5},{7,6},{8,7},{9,8},{10,9},{11,1... | collective-permute-start | bytes 4328 | tf_op jit(solution)/shard_map/ppermute | solution.py:24
  96.5 11.6 %collective-permute-start.16 = (f32[2,20,1,64]{1,3,2,0:T(8,128)}, f32[2,20,1,64]{1,3,2,0:T(8,128)}, u32[]{:S(2)}, u32[]{:S(2)}) collective-permute-start(f32[2,20,1,64]{1,3,2,0:T(8,128)} %get-tuple-element.123), channel_id=1, source_target_pairs={{0,16},{16,32},{32,48},{48,64},{64,80},{80,96},{96,112},{112,128},... | collective-permute-start | bytes 30728 | tf_op jit(solution)/shard_map/ppermute | solution.py:21
  135.3 11.5 %collective-permute-start.24 = (f32[20,1,64]{0,2,1:T(8,128)S(1)}, f32[20,1,64]{0,2,1:T(8,128)S(1)}, u32[]{:S(2)}, u32[]{:S(2)}) collective-permute-start(f32[20,1,64]{0,2,1:T(8,128)S(1)} %get-tuple-element.139), channel_id=1, source_target_pairs={{0,16},{16,32},{32,48},{48,64},{64,80},{80,96},{96,112},{112,128},... | collective-permute-start | bytes 15368 | tf_op jit(solution)/shard_map/ppermute | solution.py:21
  149.5 16.0 %collective-permute-start.27 = (f32[20,10,1]{2,0,1:T(8,128)S(1)}, f32[20,10,1]{2,0,1:T(8,128)S(1)}, u32[]{:S(2)}, u32[]{:S(2)}) collective-permute-start(f32[20,10,1]{2,0,1:T(8,128)S(1)} %get-tuple-element.219), channel_id=1, source_target_pairs={{1,0},{2,1},{3,2},{4,3},{5,4},{6,5},{7,6},{8,7},{9,8},{10,9},{11,1... | collective-permute-start | bytes 2408 | tf_op jit(solution)/shard_map/ppermute | solution.py:24
  155.7 22.7 %collective-permute-start.28 = (f32[2,20,1,32]{1,3,2,0:T(8,128)}, f32[2,20,1,32]{1,3,2,0:T(8,128)}, u32[]{:S(2)}, u32[]{:S(2)}) collective-permute-start(f32[2,20,1,32]{1,3,2,0:T(8,128)} %get-tuple-element.206), channel_id=1, source_target_pairs={{0,16},{16,32},{32,48},{48,64},{64,80},{80,96},{96,112},{112,128},... | collective-permute-start | bytes 15368 | tf_op jit(solution)/shard_map/ppermute | solution.py:21
  157.6 20.8 %collective-permute-start.29 = (f32[2,20,1,32]{1,3,2,0:T(8,128)}, f32[2,20,1,32]{1,3,2,0:T(8,128)}, u32[]{:S(2)}, u32[]{:S(2)}) collective-permute-start(f32[2,20,1,32]{1,3,2,0:T(8,128)} %get-tuple-element.207), channel_id=1, source_target_pairs={{16,0},{32,16},{48,32},{64,48},{80,64},{96,80},{112,96},{128,112},... | collective-permute-start | bytes 15368 | tf_op jit(solution)/shard_map/ppermute | solution.py:24
  172.5 64.8 %collective-permute-start.43 = (f32[2,20,2,1]{1,3,2,0:T(1,128)}, f32[2,20,2,1]{1,3,2,0:T(1,128)}, u32[]{:S(2)}, u32[]{:S(2)}) collective-permute-start(f32[2,20,2,1]{1,3,2,0:T(1,128)} %get-tuple-element.260), channel_id=1, source_target_pairs={{1,0},{2,1},{3,2},{4,3},{5,4},{6,5},{7,6},{8,7},{9,8},{10,9},{11,1... | collective-permute-start | bytes 968 | tf_op jit(solution)/shard_map/ppermute | solution.py:24
  173.8 65.4 %collective-permute-start.42 = (f32[2,20,2,1]{1,3,2,0:T(1,128)}, f32[2,20,2,1]{1,3,2,0:T(1,128)}, u32[]{:S(2)}, u32[]{:S(2)}) collective-permute-start(f32[2,20,2,1]{1,3,2,0:T(1,128)} %get-tuple-element.261), channel_id=1, source_target_pairs={{0,1},{1,2},{2,3},{3,4},{4,5},{5,6},{6,7},{7,8},{8,9},{9,10},{10,1... | collective-permute-start | bytes 968 | tf_op jit(solution)/shard_map/ppermute | solution.py:21
  198.0 12.7 %collective-permute-start.36 = (f32[20,1,32]{0,2,1:T(8,128)}, f32[20,1,32]{0,2,1:T(8,128)S(1)}, u32[]{:S(2)}, u32[]{:S(2)}) collective-permute-start(f32[20,1,32]{0,2,1:T(8,128)} %get-tuple-element.242), channel_id=1, source_target_pairs={{0,16},{16,32},{32,48},{48,64},{64,80},{80,96},{96,112},{112,128},... | collective-permute-start | bytes 7688 | tf_op jit(solution)/shard_map/ppermute | solution.py:21
  200.0 10.8 %collective-permute-start.37 = (f32[20,1,32]{0,2,1:T(8,128)}, f32[20,1,32]{0,2,1:T(8,128)}, u32[]{:S(2)}, u32[]{:S(2)}) collective-permute-start(f32[20,1,32]{0,2,1:T(8,128)} %get-tuple-element.243), channel_id=1, source_target_pairs={{16,0},{32,16},{48,32},{64,48},{80,64},{96,80},{112,96},{128,112},... | collective-permute-start | bytes 7688 | tf_op jit(solution)/shard_map/ppermute | solution.py:24
  214.8 13.2 %collective-permute-start.39 = (f32[20,6,1]{0,2,1:T(1,128)S(1)}, f32[20,6,1]{0,2,1:T(1,128)S(1)}, u32[]{:S(2)}, u32[]{:S(2)}) collective-permute-start(f32[20,6,1]{0,2,1:T(1,128)S(1)} %get-tuple-element.229), channel_id=1, source_target_pairs={{1,0},{2,1},{3,2},{4,3},{5,4},{6,5},{7,6},{8,7},{9,8},{10,9},{11,1... | collective-permute-start | bytes 1448 | tf_op jit(solution)/shard_map/ppermute | solution.py:24
  218.8 20.5 %collective-permute-start.40 = (f32[2,20,1,16]{1,3,2,0:T(8,128)}, f32[2,20,1,16]{1,3,2,0:T(8,128)}, u32[]{:S(2)}, u32[]{:S(2)}) collective-permute-start(f32[2,20,1,16]{1,3,2,0:T(8,128)} %get-tuple-element.262), channel_id=1, source_target_pairs={{0,16},{16,32},{32,48},{48,64},{64,80},{80,96},{96,112},{112,128},... | collective-permute-start | bytes 7688 | tf_op jit(solution)/shard_map/ppermute | solution.py:21
  220.7 18.6 %collective-permute-start.41 = (f32[2,20,1,16]{1,3,2,0:T(8,128)}, f32[2,20,1,16]{1,3,2,0:T(8,128)}, u32[]{:S(2)}, u32[]{:S(2)}) collective-permute-start(f32[2,20,1,16]{1,3,2,0:T(8,128)} %get-tuple-element.263), channel_id=1, source_target_pairs={{16,0},{32,16},{48,32},{64,48},{80,64},{96,80},{112,96},{128,112},... | collective-permute-start | bytes 7688 | tf_op jit(solution)/shard_map/ppermute | solution.py:24
  230.4 50.4 %collective-permute-start.53 = (f32[2,20,1,8]{1,3,2,0:T(8,128)}, f32[2,20,1,8]{1,3,2,0:T(8,128)}, u32[]{:S(2)}, u32[]{:S(2)}) collective-permute-start(f32[2,20,1,8]{1,3,2,0:T(8,128)} %pad_maximum_fusion.158), channel_id=1, source_target_pairs={{16,0},{32,16},{48,32},{64,48},{80,64},{96,80},{112,96},{128,112},... | collective-permute-start | bytes 3848 | tf_op jit(solution)/shard_map/ppermute | solution.py:24
  237.3 43.4 %collective-permute-start.52 = (f32[2,20,1,8]{1,3,2,0:T(8,128)}, f32[2,20,1,8]{1,3,2,0:T(8,128)}, u32[]{:S(2)}, u32[]{:S(2)}) collective-permute-start(f32[2,20,1,8]{1,3,2,0:T(8,128)} %pad_maximum_fusion.158), channel_id=1, source_target_pairs={{0,16},{16,32},{32,48},{48,64},{64,80},{80,96},{96,112},{112,128},... | collective-permute-start | bytes 3848 | tf_op jit(solution)/shard_map/ppermute | solution.py:21
  282.2 10.7 %collective-permute-start = (f32[20,1,8]{0,2,1:T(8,128)S(1)}, f32[20,1,8]{0,2,1:T(8,128)S(1)}, u32[]{:S(2)}, u32[]{:S(2)}) collective-permute-start(f32[20,1,8]{0,2,1:T(8,128)S(1)} %get-tuple-element.375), channel_id=1, source_target_pairs={{0,16},{16,32},{32,48},{48,64},{64,80},{80,96},{96,112},{112,128},... | collective-permute-start | bytes 1928 | tf_op jit(solution)/shard_map/while/body/eval_jaxpr/ppermute | solution.py:21
  305.8 10.8 %collective-permute-start = (f32[20,1,8]{0,2,1:T(8,128)S(1)}, f32[20,1,8]{0,2,1:T(8,128)S(1)}, u32[]{:S(2)}, u32[]{:S(2)}) collective-permute-start(f32[20,1,8]{0,2,1:T(8,128)S(1)} %get-tuple-element.375), channel_id=1, source_target_pairs={{0,16},{16,32},{32,48},{48,64},{64,80},{80,96},{96,112},{112,128},... | collective-permute-start | bytes 1928 | tf_op jit(solution)/shard_map/while/body/eval_jaxpr/ppermute | solution.py:21
  329.1 10.8 %collective-permute-start = (f32[20,1,8]{0,2,1:T(8,128)S(1)}, f32[20,1,8]{0,2,1:T(8,128)S(1)}, u32[]{:S(2)}, u32[]{:S(2)}) collective-permute-start(f32[20,1,8]{0,2,1:T(8,128)S(1)} %get-tuple-element.375), channel_id=1, source_target_pairs={{0,16},{16,32},{32,48},{48,64},{64,80},{80,96},{96,112},{112,128},... | collective-permute-start | bytes 1928 | tf_op jit(solution)/shard_map/while/body/eval_jaxpr/ppermute | solution.py:21
  352.0 11.0 %collective-permute-start = (f32[20,1,8]{0,2,1:T(8,128)S(1)}, f32[20,1,8]{0,2,1:T(8,128)S(1)}, u32[]{:S(2)}, u32[]{:S(2)}) collective-permute-start(f32[20,1,8]{0,2,1:T(8,128)S(1)} %get-tuple-element.375), channel_id=1, source_target_pairs={{0,16},{16,32},{32,48},{48,64},{64,80},{80,96},{96,112},{112,128},... | collective-permute-start | bytes 1928 | tf_op jit(solution)/shard_map/while/body/eval_jaxpr/ppermute | solution.py:21
  374.0 11.0 %collective-permute-start = (f32[20,1,8]{0,2,1:T(8,128)S(1)}, f32[20,1,8]{0,2,1:T(8,128)S(1)}, u32[]{:S(2)}, u32[]{:S(2)}) collective-permute-start(f32[20,1,8]{0,2,1:T(8,128)S(1)} %get-tuple-element.375), channel_id=1, source_target_pairs={{0,16},{16,32},{32,48},{48,64},{64,80},{80,96},{96,112},{112,128},... | collective-permute-start | bytes 1928 | tf_op jit(solution)/shard_map/while/body/eval_jaxpr/ppermute | solution.py:21
  395.6 10.8 %collective-permute-start = (f32[20,1,8]{0,2,1:T(8,128)S(1)}, f32[20,1,8]{0,2,1:T(8,128)S(1)}, u32[]{:S(2)}, u32[]{:S(2)}) collective-permute-start(f32[20,1,8]{0,2,1:T(8,128)S(1)} %get-tuple-element.375), channel_id=1, source_target_pairs={{0,16},{16,32},{32,48},{48,64},{64,80},{80,96},{96,112},{112,128},... | collective-permute-start | bytes 1928 | tf_op jit(solution)/shard_map/while/body/eval_jaxpr/ppermute | solution.py:21
  416.8 10.8 %collective-permute-start = (f32[20,1,8]{0,2,1:T(8,128)S(1)}, f32[20,1,8]{0,2,1:T(8,128)S(1)}, u32[]{:S(2)}, u32[]{:S(2)}) collective-permute-start(f32[20,1,8]{0,2,1:T(8,128)S(1)} %get-tuple-element.375), channel_id=1, source_target_pairs={{0,16},{16,32},{32,48},{48,64},{64,80},{80,96},{96,112},{112,128},... | collective-permute-start | bytes 1928 | tf_op jit(solution)/shard_map/while/body/eval_jaxpr/ppermute | solution.py:21
  438.0 10.8 %collective-permute-start = (f32[20,1,8]{0,2,1:T(8,128)S(1)}, f32[20,1,8]{0,2,1:T(8,128)S(1)}, u32[]{:S(2)}, u32[]{:S(2)}) collective-permute-start(f32[20,1,8]{0,2,1:T(8,128)S(1)} %get-tuple-element.375), channel_id=1, source_target_pairs={{0,16},{16,32},{32,48},{48,64},{64,80},{80,96},{96,112},{112,128},... | collective-permute-start | bytes 1928 | tf_op jit(solution)/shard_map/while/body/eval_jaxpr/ppermute | solution.py:21
  459.3 10.8 %collective-permute-start = (f32[20,1,8]{0,2,1:T(8,128)S(1)}, f32[20,1,8]{0,2,1:T(8,128)S(1)}, u32[]{:S(2)}, u32[]{:S(2)}) collective-permute-start(f32[20,1,8]{0,2,1:T(8,128)S(1)} %get-tuple-element.375), channel_id=1, source_target_pairs={{0,16},{16,32},{32,48},{48,64},{64,80},{80,96},{96,112},{112,128},... | collective-permute-start | bytes 1928 | tf_op jit(solution)/shard_map/while/body/eval_jaxpr/ppermute | solution.py:21
  480.5 10.8 %collective-permute-start = (f32[20,1,8]{0,2,1:T(8,128)S(1)}, f32[20,1,8]{0,2,1:T(8,128)S(1)}, u32[]{:S(2)}, u32[]{:S(2)}) collective-permute-start(f32[20,1,8]{0,2,1:T(8,128)S(1)} %get-tuple-element.375), channel_id=1, source_target_pairs={{0,16},{16,32},{32,48},{48,64},{64,80},{80,96},{96,112},{112,128},... | collective-permute-start | bytes 1928 | tf_op jit(solution)/shard_map/while/body/eval_jaxpr/ppermute | solution.py:21
  501.8 10.8 %collective-permute-start = (f32[20,1,8]{0,2,1:T(8,128)S(1)}, f32[20,1,8]{0,2,1:T(8,128)S(1)}, u32[]{:S(2)}, u32[]{:S(2)}) collective-permute-start(f32[20,1,8]{0,2,1:T(8,128)S(1)} %get-tuple-element.375), channel_id=1, source_target_pairs={{0,16},{16,32},{32,48},{48,64},{64,80},{80,96},{96,112},{112,128},... | collective-permute-start | bytes 1928 | tf_op jit(solution)/shard_map/while/body/eval_jaxpr/ppermute | solution.py:21
  523.0 10.8 %collective-permute-start = (f32[20,1,8]{0,2,1:T(8,128)S(1)}, f32[20,1,8]{0,2,1:T(8,128)S(1)}, u32[]{:S(2)}, u32[]{:S(2)}) collective-permute-start(f32[20,1,8]{0,2,1:T(8,128)S(1)} %get-tuple-element.375), channel_id=1, source_target_pairs={{0,16},{16,32},{32,48},{48,64},{64,80},{80,96},{96,112},{112,128},... | collective-permute-start | bytes 1928 | tf_op jit(solution)/shard_map/while/body/eval_jaxpr/ppermute | solution.py:21
  544.2 10.8 %collective-permute-start = (f32[20,1,8]{0,2,1:T(8,128)S(1)}, f32[20,1,8]{0,2,1:T(8,128)S(1)}, u32[]{:S(2)}, u32[]{:S(2)}) collective-permute-start(f32[20,1,8]{0,2,1:T(8,128)S(1)} %get-tuple-element.375), channel_id=1, source_target_pairs={{0,16},{16,32},{32,48},{48,64},{64,80},{80,96},{96,112},{112,128},... | collective-permute-start | bytes 1928 | tf_op jit(solution)/shard_map/while/body/eval_jaxpr/ppermute | solution.py:21
  565.5 10.8 %collective-permute-start = (f32[20,1,8]{0,2,1:T(8,128)S(1)}, f32[20,1,8]{0,2,1:T(8,128)S(1)}, u32[]{:S(2)}, u32[]{:S(2)}) collective-permute-start(f32[20,1,8]{0,2,1:T(8,128)S(1)} %get-tuple-element.375), channel_id=1, source_target_pairs={{0,16},{16,32},{32,48},{48,64},{64,80},{80,96},{96,112},{112,128},... | collective-permute-start | bytes 1928 | tf_op jit(solution)/shard_map/while/body/eval_jaxpr/ppermute | solution.py:21
  586.7 10.8 %collective-permute-start = (f32[20,1,8]{0,2,1:T(8,128)S(1)}, f32[20,1,8]{0,2,1:T(8,128)S(1)}, u32[]{:S(2)}, u32[]{:S(2)}) collective-permute-start(f32[20,1,8]{0,2,1:T(8,128)S(1)} %get-tuple-element.375), channel_id=1, source_target_pairs={{0,16},{16,32},{32,48},{48,64},{64,80},{80,96},{96,112},{112,128},... | collective-permute-start | bytes 1928 | tf_op jit(solution)/shard_map/while/body/eval_jaxpr/ppermute | solution.py:21
  608.0 10.8 %collective-permute-start = (f32[20,1,8]{0,2,1:T(8,128)S(1)}, f32[20,1,8]{0,2,1:T(8,128)S(1)}, u32[]{:S(2)}, u32[]{:S(2)}) collective-permute-start(f32[20,1,8]{0,2,1:T(8,128)S(1)} %get-tuple-element.375), channel_id=1, source_target_pairs={{0,16},{16,32},{32,48},{48,64},{64,80},{80,96},{96,112},{112,128},... | collective-permute-start | bytes 1928 | tf_op jit(solution)/shard_map/while/body/eval_jaxpr/ppermute | solution.py:21
  629.7 11.0 %collective-permute-start = (f32[20,1,8]{0,2,1:T(8,128)S(1)}, f32[20,1,8]{0,2,1:T(8,128)S(1)}, u32[]{:S(2)}, u32[]{:S(2)}) collective-permute-start(f32[20,1,8]{0,2,1:T(8,128)S(1)} %get-tuple-element.375), channel_id=1, source_target_pairs={{0,16},{16,32},{32,48},{48,64},{64,80},{80,96},{96,112},{112,128},... | collective-permute-start | bytes 1928 | tf_op jit(solution)/shard_map/while/body/eval_jaxpr/ppermute | solution.py:21
  651.7 11.0 %collective-permute-start = (f32[20,1,8]{0,2,1:T(8,128)S(1)}, f32[20,1,8]{0,2,1:T(8,128)S(1)}, u32[]{:S(2)}, u32[]{:S(2)}) collective-permute-start(f32[20,1,8]{0,2,1:T(8,128)S(1)} %get-tuple-element.375), channel_id=1, source_target_pairs={{0,16},{16,32},{32,48},{48,64},{64,80},{80,96},{96,112},{112,128},... | collective-permute-start | bytes 1928 | tf_op jit(solution)/shard_map/while/body/eval_jaxpr/ppermute | solution.py:21
  673.7 11.0 %collective-permute-start = (f32[20,1,8]{0,2,1:T(8,128)S(1)}, f32[20,1,8]{0,2,1:T(8,128)S(1)}, u32[]{:S(2)}, u32[]{:S(2)}) collective-permute-start(f32[20,1,8]{0,2,1:T(8,128)S(1)} %get-tuple-element.375), channel_id=1, source_target_pairs={{0,16},{16,32},{32,48},{48,64},{64,80},{80,96},{96,112},{112,128},... | collective-permute-start | bytes 1928 | tf_op jit(solution)/shard_map/while/body/eval_jaxpr/ppermute | solution.py:21
  714.7 10.6 %collective-permute-start.60 = (f32[20,1,16]{0,2,1:T(8,128)S(1)}, f32[20,1,16]{0,2,1:T(8,128)S(1)}, u32[]{:S(2)}, u32[]{:S(2)}) collective-permute-start(f32[20,1,16]{0,2,1:T(8,128)S(1)} %get-tuple-element.266), channel_id=1, source_target_pairs={{0,16},{16,32},{32,48},{48,64},{64,80},{80,96},{96,112},{112,128},... | collective-permute-start | bytes 3848 | tf_op jit(solution)/shard_map/ppermute | solution.py:21
  772.4 10.5 %collective-permute-start.72 = (f32[20,1,64]{0,2,1:T(8,128)S(1)}, f32[20,1,64]{0,2,1:T(8,128)S(1)}, u32[]{:S(2)}, u32[]{:S(2)}) collective-permute-start(f32[20,1,64]{0,2,1:T(8,128)S(1)} %get-tuple-element.135), channel_id=1, source_target_pairs={{0,16},{16,32},{32,48},{48,64},{64,80},{80,96},{96,112},{112,128},... | collective-permute-start | bytes 15368 | tf_op jit(solution)/shard_map/ppermute | solution.py:21
  796.7 10.6 %collective-permute-start.76 = (f32[20,1,64]{0,2,1:T(8,128)S(1)}, f32[20,1,64]{0,2,1:T(8,128)S(1)}, u32[]{:S(2)}, u32[]{:S(2)}) collective-permute-start(f32[20,1,64]{0,2,1:T(8,128)S(1)} %get-tuple-element.131), channel_id=1, source_target_pairs={{0,16},{16,32},{32,48},{48,64},{64,80},{80,96},{96,112},{112,128},... | collective-permute-start | bytes 15368 | tf_op jit(solution)/shard_map/ppermute | solution.py:21
  822.9 10.5 %collective-permute-start.80 = (f32[20,1,128]{2,1,0:T(1,128)S(1)}, f32[20,1,128]{2,1,0:T(1,128)S(1)}, u32[]{:S(2)}, u32[]{:S(2)}) collective-permute-start(f32[20,1,128]{2,1,0:T(1,128)S(1)} %get-tuple-element.179), channel_id=1, source_target_pairs={{0,16},{16,32},{32,48},{48,64},{64,80},{80,96},{96,112},{112,128},... | collective-permute-start | bytes 30728 | tf_op jit(solution)/shard_map/ppermute | solution.py:21
  845.1 10.6 %collective-permute-start.84 = (f32[20,1,128]{2,1,0:T(1,128)S(1)}, f32[20,1,128]{2,1,0:T(1,128)S(1)}, u32[]{:S(2)}, u32[]{:S(2)}) collective-permute-start(f32[20,1,128]{2,1,0:T(1,128)S(1)} %get-tuple-element.175), channel_id=1, source_target_pairs={{0,16},{16,32},{32,48},{48,64},{64,80},{80,96},{96,112},{112,128},... | collective-permute-start | bytes 30728 | tf_op jit(solution)/shard_map/ppermute | solution.py:21
  867.4 10.9 %collective-permute-start.88 = (f32[20,1,128]{2,1,0:T(1,128)S(1)}, f32[20,1,128]{2,1,0:T(1,128)S(1)}, u32[]{:S(2)}, u32[]{:S(2)}) collective-permute-start(f32[20,1,128]{2,1,0:T(1,128)S(1)} %get-tuple-element.171), channel_id=1, source_target_pairs={{0,16},{16,32},{32,48},{48,64},{64,80},{80,96},{96,112},{112,128},... | collective-permute-start | bytes 30728 | tf_op jit(solution)/shard_map/ppermute | solution.py:21
  (318 other events, 1846.6 us)
where the time goes:
time: 903 us; the launch traced here: 890 us
  starting transfers between devices  657 us (73%)
  waiting for transfers between devices  84.6 us (9%)
  local copies, waits for them, and re-layouts  81 us (9%)
  other arithmetic  62.9 us (7%)
    ppermute x82, starting transfers between devices, extended(): lax.ppermute(lax.slice_in_dim(block, 0, width, axis=dim), axis, backward)  453 us
    ppermute x82, starting transfers between devices, extended(): lax.ppermute(lax.slice_in_dim(block, block.shape[dim] - width, None, axis...  204 us
    ppermute x82, waiting for transfers between devices, extended(): lax.ppermute(lax.slice_in_dim(block, block.shape[dim] - width, None, axis...  59.9 us
    ppermute x82, waiting for transfers between devices, extended(): lax.ppermute(lax.slice_in_dim(block, 0, width, axis=dim), axis, backward)  24.7 us
    while x266, local copies, waits for them, and re-layouts  24.6 us
    add x31, other arithmetic, sweep(): return field + OMEGA * (right - apply_op(field, faces, rim_pad)) / faces[6]  21.8 us
    unnamed x201, local copies, waits for them, and re-layouts  18.9 us
  transfers between devices with their start and end apart: 164, of which 49 were waited for; matrix products, arithmetic and copies ran while one was open for 8% of the time, Pallas kernels for 0%

commit v1 on v0

v1 whole, which is shorter than its diff:
```python
import jax
import jax.numpy as jnp
from jax import lax
from jax.experimental import pallas as pl
from jax.experimental.pallas import tpu as pltpu
from jax.sharding import PartitionSpec as P

NZ = 20
HZ = 10
NTX = 32
NTY = 16
OMEGA = 0.8
UNROLL = 20
MESH = pl.DeviceIdType.MESH
F32 = jnp.float32

DIAGONALS = ((1, 1), (-1, 1), (1, -1), (-1, -1))


def iota(shape, dim):
    return lax.broadcasted_iota(jnp.int32, shape, dim)


def mm(x, m):
    high = x.astype(jnp.bfloat16)
    low = (x - high.astype(F32)).astype(jnp.bfloat16)
    m = m.astype(jnp.bfloat16)
    return lax.dot_general(
        jnp.concatenate([high, low], axis=1), jnp.concatenate([m, m], axis=0),
        (((1,), (0,)), ((), ())), preferred_element_type=F32,
    )


def roll(x, shift, axis):
    shift = shift % x.shape[axis]
    return x if shift == 0 else pltpu.roll(x, shift, axis)


def one_hot(shape, hit, value=1.0):
    row, col = iota(shape, 0), iota(shape, 1)
    return jnp.where(hit(row, col), F32(value), F32(0.0))


def restrict_0():
    return one_hot((128, 128), lambda n, m: m == 32 + (n >> 1), 0.25)


def restrict_1():
    return one_hot((256, 128), lambda n, m: m == n >> 1, 0.25)


def restrict_2():
    return one_hot((128, 128), lambda n, m: m == (n & 64) + 8 + ((n & 63) >> 1), 0.25)


def restrict_3():
    def hit(n, m):
        q = n & 63
        return (m == (n & 64) + 16 + (q >> 1)) & (q >= 16) & (q < 32)

    return one_hot((128, 128), hit, 0.25)


def restrict_all():
    return one_hot((256, 128), lambda n, m: m == ((n & 128) >> 1) + 24 + ((n & 127) >> 4), 1.0 / 256)


def prolong_3():
    return one_hot((128, 128), lambda m, n: m == (n & 64) + 16 + ((n & 63) >> 1))


def prolong_2():
    return one_hot((128, 128), lambda m, n: m == (n & 64) + 8 + ((n & 63) >> 1))


def prolong_1():
    return one_hot((128, 256), lambda m, n: m == n >> 1)


def prolong_0():
    def hit(m, n):
        rel = jnp.where(n >= 192, n - 256, n)
        return (m == 32 + (rel >> 1)) & (rel < 132) & (rel >= -4)

    return one_hot((128, 256), hit)


class Level:
    def __init__(self, slabs, folded, refs):
        self.slabs = slabs
        self.folded = folded
        self.e, self.n, self.v, self.g, self.d, self.c, self.u, self.w = refs

    def each(self, body, unroll):
        def step(z, carry):
            body(z)
            return carry

        lax.fori_loop(0, self.slabs, step, 0, unroll=min(unroll, self.slabs))

    def wrap(self, ref):
        if self.folded:
            ref[0] = roll(ref[self.slabs], 64, 1)
            ref[self.slabs + 1] = roll(ref[1], 64, 1)

    def clear_ends(self):
        if not self.folded:
            for ref in (self.u, self.w):
                ref[0] = jnp.zeros_like(ref[0])
                ref[self.slabs + 1] = jnp.zeros_like(ref[0])

    def faces(self, kap, lond, latd, sea, unroll):
        top = self.slabs - 1

        def vertical(z):
            here = sea(z)
            self.v[z + 1] = here * sea(z + 1)

        lax.fori_loop(0, top, lambda z, c: (vertical(z), c)[1], 0, unroll=min(unroll, top))
        if self.folded:
            low = iota(self.v.shape[1:], 1) < 64
            self.v[self.slabs] = jnp.where(low, sea(top) * roll(sea(0), 64, 1), 0.0)
            self.v[0] = roll(self.v[self.slabs], 64, 1)
        else:
            self.v[0] = jnp.zeros_like(self.v[0])
            self.v[self.slabs] = jnp.zeros_like(self.v[0])

        def horizontal(z):
            s = sea(z)
            lw = s * lond(z)
            tw = s * latd(z)
            east = 0.5 * (lw * roll(s, -1, 0) + s * roll(lw, -1, 0))
            north = 0.5 * (tw * roll(s, -1, 1) + s * roll(tw, -1, 1))
            west = roll(east, 1, 0)
            south = roll(north, 1, 1)
            diag = s * kap(z) + (west + east + south + north + self.v[z] + self.v[z + 1]) + (1.0 - s)
            self.e[z] = east
            self.n[z] = north
            self.d[z] = diag
            self.g[z] = OMEGA / diag

        self.each(horizontal, unroll)

    def total(self, src, z):
        u = src[z + 1]
        e = self.e[z]
        n = self.n[z]
        return u, (
            roll(e * u, 1, 0)
            + e * roll(u, -1, 0)
            + roll(n * u, 1, 1)
            + n * roll(u, -1, 1)
            + self.v[z] * src[z]
            + self.v[z + 1] * src[z + 2]
        )

    def sweep(self, src, dst, unroll):
        def body(z):
            u, total = self.total(src, z)
            dst[z + 1] = (1.0 - OMEGA) * u + self.c[z] + self.g[z] * total

        self.each(body, unroll)
        self.wrap(dst)

    def start(self, unroll):
        def body(z):
            self.u[z + 1] = self.c[z]

        self.each(body, unroll)
        self.wrap(self.u)

    def remain(self, src, z):
        u, total = self.total(src, z)
        return self.d[z] * (1.25 * self.c[z] - u) + total


def pack_edge(slabs, width, base, count):
    lane = iota(slabs[0].shape, 1)
    out = roll(slabs[0], -base, 1)
    for i in range(1, count):
        out = jnp.where(lane >= width * i, roll(slabs[i], width * i - base, 1), out)
    return out


def body(
    source_in, kappa_in, lon_in, lat_in, mask_in,
    sol_out, resid_out,
    sol, resid, out_sem, source, kappa, lon_diff, lat_diff, mask, in_sem,
    raw0, src0, l0, raw1, l1, raw2, l2, raw3, l3, raw4, l4, t0, t1, t2, t3, t4, q1,
    a_ew, a_ns, a_rew, a_rns, a_rd,
    b_pk, b_ns, b_nc, b_rpk, b_rns, b_rnc,
    f_p, f_rp,
    k_blk, k_z, k_ev, k_od,
    p_pk, p_ns, p_nc, p_rpk, p_rns, p_rnc, g_p, g_rp, h_blk, h_z, h_ev, h_od,
    o_ew, o_ns, o_rew, o_rns, o_rd,
    send_sem, recv_sem,
):
    mx, my = lax.axis_index("tx"), lax.axis_index("ty")
    odd = lax.rem(mx, 2) == 1
    counter = [0]
    pending = []

    def copy(src, dst, dx, dy):
        i = counter[0]
        counter[0] += 1
        made = pltpu.make_async_remote_copy(
            src_ref=src, dst_ref=dst, send_sem=send_sem.at[i], recv_sem=recv_sem.at[i],
            device_id=(lax.rem(mx + (dx + NTX), NTX), lax.rem(my + (dy + NTY), NTY)),
            device_id_type=MESH,
        )
        made.start()
        pending.append(made)
        return made

    def arrive(copies):
        for made in copies:
            made.wait_recv()

    lev0 = Level(NZ, False, l0)
    lev1 = Level(NZ, False, l1)
    lev2 = Level(HZ, True, l2)
    lev3 = Level(HZ, True, l3)
    lev4 = Level(HZ, True, l4)

    fetched = [
        pltpu.make_async_copy(src, dst, in_sem.at[i])
        for i, (src, dst) in enumerate((
            (mask_in, mask), (lon_in, lon_diff), (lat_in, lat_diff), (kappa_in, kappa), (source_in, source)
        ))
    ]
    for made in fetched:
        made.start()

    peers = [(2 * k, 0) for k in range(1, 16)] + [(1, 0), (-1, 0), (3, 0), (-3, 0)]
    peers += [(0, d) for d in (1, 2, 3, -1, -2, -3)] + list(DIAGONALS)
    barrier = pltpu.get_barrier_semaphore()
    for dx, dy in peers:
        pl.semaphore_signal(
            barrier, inc=1,
            device_id=(lax.rem(mx + (dx + NTX), NTX), lax.rem(my + (dy + NTY), NTY)),
            device_id_type=MESH,
        )

    for made in fetched:
        made.wait()

    def own0(z):
        s = mask[z].astype(F32)
        return (kappa[z], s * lon_diff[z], s * lat_diff[z], source[z])

    lane16 = iota((16, 128), 1)
    edge_n = [jnp.zeros((16, 128), F32)] * 4
    edge_s = [jnp.zeros((16, 128), F32)] * 4
    for z in range(NZ):
        for f, x in enumerate(own0(z)):
            raw0[f, z, 0:16, 0:128] = x
            a_ew[0, f * NZ + z] = x[0:2]
            a_ew[1, f * NZ + z] = x[14:16]
            if f == 1:
                a_ew[0, 4 * NZ + z // 2, z % 2:z % 2 + 1] = x[2:3]
                a_ew[1, 4 * NZ + z // 2, z % 2:z % 2 + 1] = x[13:14]
            edge_n[f] = jnp.where(lane16 >= 4 * z, roll(x, 4 * z - 124, 1), edge_n[f])
            edge_s[f] = jnp.where(lane16 >= 4 * z, roll(x, 4 * z, 1), edge_s[f])
    for f in range(4):
        a_ns[0, f] = edge_n[f]
        a_ns[1, f] = edge_s[f]

    pl.semaphore_wait(barrier, len(peers))

    def send_edges(ew, ns, rew, rns, rd):
        made = [copy(ew.at[0], rew.at[0], -1, 0), copy(ew.at[1], rew.at[1], 1, 0)]
        made += [copy(ns.at[0], rns.at[0], 0, 1), copy(ns.at[1], rns.at[1], 0, -1)]
        made.append(copy(ns.at[0, :, 8:16, :], rd.at[0], 1, 1))
        made.append(copy(ns.at[0, :, 0:8, :], rd.at[1], -1, 1))
        made.append(copy(ns.at[1, :, 8:16, :], rd.at[2], 1, -1))
        made.append(copy(ns.at[1, :, 0:8, :], rd.at[3], -1, -1))
        return made

    has_s, has_n = my > 0, my < NTY - 1

    def merge_edges(f, rows, rns, rd, put_rows, put_side):
        sub = iota((8, 128), 0)
        south = jnp.concatenate([rns[0, f], jnp.where(sub < 4, rd[1, f], rd[0, f])], axis=0)
        north = jnp.concatenate([rns[1, f], jnp.where(sub < 4, rd[3, f], rd[2, f])], axis=0)
        lane = iota((24, 128), 1)
        south = jnp.where(has_s, south, 0.0)
        north = jnp.where(has_n, north, 0.0)
        for z in range(NZ):
            put_rows(z, rows(z))
            side = jnp.where(lane < 4, roll(north, -4 * z, 1), roll(south, 124 - 4 * z, 1))
            put_side(z, jnp.where((lane < 4) | (lane >= 124), side, 0.0))

    sent_a = send_edges(a_ew, a_ns, a_rew, a_rns, a_rd)

    m0 = restrict_0()

    def down_0(x):
        t1[...] = mm(x.reshape(NZ * 16, 128), m0).reshape(NZ, 16, 128)
        return t1[:, pl.ds(0, 8, stride=2), :] + t1[:, pl.ds(1, 8, stride=2), :]

    def pack_1(x, f, pk, ns, nc):
        lane = iota((8, 128), 1)
        for k in range(HZ):
            pk[f * HZ + k] = jnp.where(lane < 64, roll(x[k], -32, 1), roll(x[k + HZ], 32, 1))
        for k in range(5):
            group = [x[k + 5 * j] for j in range(4)]
            for side, base in ((0, 64), (1, 32)):
                edge = pack_edge(group, 32, base, 4)
                ns[side, f * 5 + k] = edge
                nc[side, 0, f * 5 + k] = edge[0:4]
                nc[side, 1, f * 5 + k] = edge[4:8]

    def send_1(pk, ns, nc, rpk, rns, rnc):
        made = [copy(pk, rpk.at[0], -1, 0), copy(pk, rpk.at[1], 1, 0)]
        made += [copy(ns.at[0], rns.at[0], 0, 1), copy(ns.at[1], rns.at[1], 0, -1)]
        made.append(copy(nc.at[0, 1], rnc.at[0, 1], 1, 1))
        made.append(copy(nc.at[0, 0], rnc.at[0, 0], -1, 1))
        made.append(copy(nc.at[1, 1], rnc.at[1, 1], 1, -1))
        made.append(copy(nc.at[1, 0], rnc.at[1, 0], -1, -1))
        return made

    def merge_1(f, own, rpk, rns, rnc, put):
        lane = iota((8, 128), 1)
        blank = jnp.zeros((4, 128), F32)

        def edge(side, i, at):
            if i == 0:
                return rns[side, at]
            if i == 1:
                return jnp.concatenate([rnc[side, 0, at], blank], axis=0)
            return jnp.concatenate([blank, rnc[side, 1, at]], axis=0)

        for z in range(NZ):
            k, shift = (z, 32) if z < HZ else (z - HZ, -32)
            middle = (own(z), roll(rpk[0, f * HZ + k], shift, 1), roll(rpk[1, f * HZ + k], shift, 1))
            for i, start in ((0, 8), (1, 16), (2, 0)):
                south = jnp.where(has_s, roll(edge(0, i, f * 5 + z % 5), -32 * (z // 5), 1), 0.0)
                north = jnp.where(has_n, roll(edge(1, i, f * 5 + z % 5), 96 - 32 * (z // 5), 1), 0.0)
                put(z, start, jnp.where(lane < 32, south, jnp.where(lane < 96, middle[i], north)))

    own1 = [
        down_0(kappa[...]),
        0.25 * down_0(lon_diff[...]),
        0.25 * down_0(lat_diff[...]),
        (down_0(mask[...].astype(F32)) > 0.0).astype(F32),
    ]
    for f in range(4):
        pack_1(own1[f], f, p_pk, p_ns, p_nc)
        raw1[f, :, 8:16, :] = own1[f]
    sent_p1 = send_1(p_pk, p_ns, p_nc, p_rpk, p_rns, p_rnc)

    mall = restrict_all()

    def down_all(x):
        pair = jnp.concatenate([x[0:HZ], x[HZ:NZ]], axis=2).reshape(HZ * 16, 256)
        return jnp.sum(mm(pair, mall).reshape(HZ, 16, 128), axis=1)

    sea4 = (down_all(mask[...].astype(F32)) > 0.0).astype(F32)
    h_blk[0:10, :] = down_all(kappa[...])
    h_blk[10:20, :] = sea4 * (down_all(lon_diff[...]) * (1.0 / 256))
    h_blk[20:30, :] = sea4 * (down_all(lat_diff[...]) * (1.0 / 256))
    h_blk[30:32, :] = jnp.zeros((2, 128), F32)

    def send_z(blk, slots):
        slots[3] = blk[...]
        return [copy(blk, slots.at[3 - d], 0, d) for d in (1, -1, 2, -2, 3, -3)]

    def window_row(slots, count):
        row = jnp.zeros((count, 128), F32)
        for s in range(7):
            inside = (my + (s - 3) >= 0) & (my + (s - 3) < NTY)
            row = row + jnp.where(inside, roll(slots[s], 8 * (s - 3), 1), 0.0)
        return row

    def send_plane(row, ev, count):
        own = pl.ds(8 * count, count)
        ev[own, :] = row
        return [
            copy(ev.at[own], ev.at[pl.ds(((8 - k) % 16) * count, count)], 2 * k, 0)
            for k in (1, 15, 2, 14, 3, 13, 4, 12, 5, 11, 6, 10, 7, 9, 8)
        ]

    def send_sibling(ev, od):
        i = counter[0]
        counter[0] += 1
        made = pltpu.make_async_remote_copy(
            src_ref=ev, dst_ref=od, send_sem=send_sem.at[i], recv_sem=recv_sem.at[i],
            device_id=(mx + 1 - 2 * lax.rem(mx, 2), my), device_id_type=MESH,
        )
        made.start()
        pending.append(made)
        return [made]

    def window_slab(ev, od, index, count, put):
        put(pl.ds(0, 16, stride=2), ev[pl.ds(index, 16, stride=count), :])
        other = od[pl.ds(index, 16, stride=count), :]
        put(pl.ds(1, 16, stride=2), jnp.where(odd, roll(other, -1, 0), other))

    sent_hz = send_z(h_blk, h_z)

    arrive(sent_a)
    for f in range(4):
        def put_rows(z, x):
            raw0[f, z, 16:24, 0:128] = x

        def put_side(z, x):
            raw0[f, z, :, 128:256] = x

        def rows(z):
            pick = slice(z % 2, z % 2 + 1)
            blank = jnp.zeros((1, 128), F32)
            near, far = [blank], [blank]
            if f == 1:
                near, far = [a_rew[0, 4 * NZ + z // 2, pick]], [a_rew[1, 4 * NZ + z // 2, pick]]
            return jnp.concatenate(
                [a_rew[0, f * NZ + z]] + near + [blank, blank] + far + [a_rew[1, f * NZ + z]], axis=0
            )

        merge_edges(f, rows, a_rns, a_rd, put_rows, put_side)

    def sea0(z):
        return (raw0[1, z] > 0.0).astype(F32)

    lev0.faces(lambda z: raw0[0, z], lambda z: raw0[1, z], lambda z: raw0[2, z], sea0, UNROLL)
    lev0.clear_ends()

    def first0(z):
        c = lev0.g[z] * raw0[3, z]
        lev0.c[z] = c
        lev0.u[z + 1] = c

    lev0.each(first0, UNROLL)
    lev0.sweep(lev0.u, lev0.w, UNROLL)

    def remain0(z):
        u, total = lev0.total(lev0.w, z)
        r = raw0[3, z] - (lev0.d[z] * u - total)
        t0[z] = r[0:16, 0:128]

    lev0.each(remain0, UNROLL)
    b1 = down_0(t0[...])

    arrive(sent_p1)
    for f in range(4):
        def put1(z, start, x):
            raw1[f, z, start:start + 8, :] = x

        merge_1(f, lambda z: raw1[f, z, 8:16, :], p_rpk, p_rns, p_rnc, put1)
    lev1.faces(lambda z: raw1[0, z], lambda z: raw1[1, z], lambda z: raw1[2, z], lambda z: raw1[3, z], UNROLL)
    lev1.clear_ends()
    c1 = lev1.g[:, 8:16, :] * b1
    q1[...] = c1
    pack_1(c1, 0, b_pk, b_ns, b_nc)
    sent_b = send_1(b_pk, b_ns, b_nc, b_rpk, b_rns, b_rnc)

    edge_n = jnp.zeros((16, 128), F32)
    edge_s = jnp.zeros((16, 128), F32)
    for z in range(NZ):
        x = lev0.w[z + 1, 0:16, 0:128]
        o_ew[0, z] = x[0:4]
        o_ew[1, z] = x[12:16]
        edge_n = jnp.where(lane16 >= 4 * z, roll(x, 4 * z - 124, 1), edge_n)
        edge_s = jnp.where(lane16 >= 4 * z, roll(x, 4 * z, 1), edge_s)
    o_ns[0, 0] = edge_n
    o_ns[1, 0] = edge_s
    sent_o = send_edges(o_ew, o_ns, o_rew, o_rns, o_rd)

    m1 = restrict_1()

    def down_1(x):
        pair = jnp.concatenate([x[0:HZ], x[HZ:NZ]], axis=2).reshape(HZ * 8, 256)
        t2[...] = mm(pair, m1).reshape(HZ, 8, 128)
        return t2[:, pl.ds(0, 4, stride=2), :] + t2[:, pl.ds(1, 4, stride=2), :]

    own2 = [
        down_1(raw1[0, :, 8:16, :]),
        0.25 * down_1(raw1[1, :, 8:16, :]),
        0.25 * down_1(raw1[2, :, 8:16, :]),
        (down_1(raw1[3, :, 8:16, :]) > 0.0).astype(F32),
    ]

    def send_2(p, rp):
        return [copy(p, rp.at[3 - d], d, 0) for d in (1, -1, 2, -2, 3, -3)]

    for f in range(4):
        g_p[f * HZ:(f + 1) * HZ] = own2[f]
    sent_p2 = send_2(g_p, g_rp)

    arrive(sent_b)

    def put1c(z, start, x):
        lev1.c[z, start:start + 8, :] = x
        lev1.u[z + 1, start:start + 8, :] = x

    merge_1(0, lambda z: q1[z], b_rpk, b_rns, b_rnc, put1c)
    lev1.sweep(lev1.u, lev1.w, UNROLL)

    def remain1(z):
        q1[z] = lev1.remain(lev1.w, z)[8:16]

    lev1.each(remain1, UNROLL)
    b2 = down_1(q1[...])

    arrive(sent_p2)
    for f in range(4):
        for s in range(7):
            piece = g_p if s == 3 else g_rp.at[s]
            raw2[f, :, 4 * s:4 * s + 4, :] = piece[f * HZ:(f + 1) * HZ]
        raw2[f, :, 28:32, :] = jnp.zeros((HZ, 4, 128), F32)
    lev2.faces(lambda z: raw2[0, z], lambda z: raw2[1, z], lambda z: raw2[2, z], lambda z: raw2[3, z], UNROLL)
    f_p[...] = lev2.g[:, 12:16, :] * b2
    sent_c = send_2(f_p, f_rp)

    arrive(sent_hz)
    sent_hp = send_plane(window_row(h_z, 32), h_ev, 32)

    m2 = restrict_2()

    def down_2(x):
        t3[...] = mm(x.reshape(HZ * 32, 128), m2).reshape(HZ, 32, 128)
        return t3[:, pl.ds(0, 16, stride=2), :] + t3[:, pl.ds(1, 16, stride=2), :]

    raw3[0] = down_2(raw2[0])
    raw3[1] = 0.25 * down_2(raw2[1])
    raw3[2] = 0.25 * down_2(raw2[2])
    raw3[3] = (down_2(raw2[3]) > 0.0).astype(F32)
    lev3.faces(lambda z: raw3[0, z], lambda z: raw3[1, z], lambda z: raw3[2, z], lambda z: raw3[3, z], UNROLL)

    arrive(sent_c)
    for s in range(7):
        piece = f_p if s == 3 else f_rp.at[s]
        lev2.c[:, 4 * s:4 * s + 4, :] = piece[...]
    lev2.c[:, 28:32, :] = jnp.zeros((HZ, 4, 128), F32)
    lev2.start(UNROLL)
    lev2.sweep(lev2.u, lev2.w, UNROLL)

    def remain2(z):
        t4[z] = lev2.remain(lev2.w, z)

    lev2.each(remain2, UNROLL)

    lev3.c[...] = lev3.g[...] * down_2(t4[...])
    lev3.start(UNROLL)
    lev3.sweep(lev3.u, lev3.w, UNROLL)

    def remain3(z):
        t3[z, 0:16, :] = lev3.remain(lev3.w, z)

    lev3.each(remain3, UNROLL)
    m3 = restrict_3()
    t3[:, 0:16, :] = mm(t3[:, 0:16, :].reshape(HZ * 16, 128), m3).reshape(HZ, 16, 128)
    for z in range(HZ):
        k_blk[z:z + 1, :] = t3[z, 6:7, :] + t3[z, 7:8, :]
    k_blk[HZ:16, :] = jnp.zeros((16 - HZ, 128), F32)
    sent_kz = send_z(k_blk, k_z)

    arrive(sent_hp)
    sent_hs = send_sibling(h_ev, h_od)

    arrive(sent_hs)
    for f in range(3):
        for z in range(HZ):
            def put4(rows, x):
                raw4[f, z, rows, :] = x

            window_slab(h_ev, h_od, f * HZ + z, 32, put4)

    def sea_4(z):
        return (raw4[1, z] > 0.0).astype(F32)

    lev4.faces(lambda z: raw4[0, z], lambda z: raw4[1, z], lambda z: raw4[2, z], sea_4, UNROLL)

    arrive(sent_kz)
    sent_kp = send_plane(window_row(k_z, 16), k_ev, 16)
    arrive(sent_kp)
    arrive(send_sibling(k_ev, k_od))
    for z in range(HZ):
        def put4c(rows, x):
            lev4.c[z, rows, :] = x

        window_slab(k_ev, k_od, z, 16, put4c)
    for z in range(HZ):
        lev4.c[z] = lev4.g[z] * lev4.c[z]
    lev4.start(UNROLL)

    def two(step, carry):
        lev4.sweep(lev4.u, lev4.w, UNROLL)
        lev4.sweep(lev4.w, lev4.u, UNROLL)
        return carry

    lax.fori_loop(0, 9, two, 0)
    lev4.sweep(lev4.u, lev4.w, UNROLL)

    up = mm(lev4.w[1:HZ + 1, 13:21, :].reshape(HZ * 8, 128), prolong_3()).reshape(HZ, 8, 128)
    for start in range(2):
        t3[:, pl.ds(start, 8, stride=2), :] = up

    def add3(z):
        lev3.w[z + 1] = lev3.w[z + 1] + t3[z, 0:16, :]

    lev3.each(add3, UNROLL)
    lev3.wrap(lev3.w)
    lev3.sweep(lev3.w, lev3.u, UNROLL)
    lev3.sweep(lev3.u, lev3.w, UNROLL)

    up = mm(lev3.w[1:HZ + 1].reshape(HZ * 16, 128), prolong_2()).reshape(HZ, 16, 128)
    for start in range(2):
        t3[:, pl.ds(start, 16, stride=2), :] = up

    def add2(z):
        lev2.w[z + 1] = lev2.w[z + 1] + t3[z]

    lev2.each(add2, UNROLL)
    lev2.wrap(lev2.w)
    lev2.sweep(lev2.w, lev2.u, UNROLL)
    lev2.sweep(lev2.u, lev2.w, UNROLL)

    t3[:, 0:16, :] = lev2.w[1:HZ + 1, 8:24, :]
    up = mm(t3[:, 0:16, :].reshape(HZ * 16, 128), prolong_1()).reshape(HZ, 16, 256)
    for start in range(2):
        t1[0:HZ, :, :] = up[:, :, 0:128]
        t1[HZ:NZ, :, :] = up[:, :, 128:256]
    for z in range(NZ):
        for start in range(2):
            q = pl.ds(start, 12, stride=2)
            raw1[0, z, q, :] = t1[z, 0:12, :]

    def add1(z):
        lev1.w[z + 1] = lev1.w[z + 1] + raw1[0, z]

    lev1.each(add1, UNROLL)
    lev1.sweep(lev1.w, lev1.u, UNROLL)
    lev1.sweep(lev1.u, lev1.w, UNROLL)

    arrive(sent_o)

    def put_rows0(z, x):
        lev0.w[z + 1, 16:24, 0:128] = x

    def put_side0(z, x):
        lev0.w[z + 1, :, 128:256] = x

    def rows0(z):
        return jnp.concatenate([o_rew[0, z], o_rew[1, z]], axis=0)

    merge_edges(0, rows0, o_rns, o_rd, put_rows0, put_side0)
    for z in range(NZ):
        t1[z, 0:8, :] = lev1.w[z + 1, 8:16, :]
        t1[z, 8:10, :] = lev1.w[z + 1, 16:18, :]
        t1[z, 10:12, :] = lev1.w[z + 1, 6:8, :]
        t1[z, 12:16, :] = jnp.zeros((4, 128), F32)
    up = mm(t1[...].reshape(NZ * 16, 128), prolong_0()).reshape(NZ, 16, 256)
    for z in range(NZ):
        for half in range(2):
            part = up[z, 0:12, 128 * half:128 * half + 128]
            for start in range(2):
                raw1[half, z, pl.ds(start, 12, stride=2), :] = part

    def add0(z):
        for half in range(2):
            lanes = slice(128 * half, 128 * half + 128)
            lev0.w[z + 1, :, lanes] = lev0.w[z + 1, :, lanes] + raw1[half, z]

    lev0.each(add0, UNROLL)
    lev0.sweep(lev0.w, lev0.u, UNROLL)
    lev0.sweep(lev0.u, lev0.w, UNROLL)
    sol[...] = lev0.w[1:NZ + 1, 0:16, 0:128]
    out_sol = pltpu.make_async_copy(sol, sol_out, out_sem.at[0])
    out_sol.start()

    def last0(z):
        u, total = lev0.total(lev0.w, z)
        r = raw0[3, z] - (lev0.d[z] * u - total)
        resid[z] = r[0:16, 0:128]

    lev0.each(last0, UNROLL)
    out_resid = pltpu.make_async_copy(resid, resid_out, out_sem.at[1])
    out_resid.start()

    for made in pending:
        made.wait_send()
    out_sol.wait()
    out_resid.wait()


def deliver(sol_in, resid_in, sol_out, resid_out, sem):
    copies = [
        pltpu.make_async_copy(sol_in, sol_out, sem.at[0]),
        pltpu.make_async_copy(resid_in, resid_out, sem.at[1]),
    ]
    for made in copies:
        made.start()
    for made in copies:
        made.wait()


def level_scratch(slabs, rows, lanes):
    def vmem(count):
        return pltpu.VMEM((count, rows, lanes), F32)

    return [vmem(slabs), vmem(slabs), vmem(slabs + 1), vmem(slabs), vmem(slabs), vmem(slabs), vmem(slabs + 2), vmem(slabs + 2)]


def shards(source, kappa_sq, lon_diff, lat_diff, sea_mask):
    def vmem(*shape):
        return pltpu.VMEM(shape, F32)

    scratch = [
        vmem(NZ, 16, 128), vmem(NZ, 16, 128), pltpu.SemaphoreType.DMA((2,)),
        vmem(NZ, 16, 128), vmem(NZ, 16, 128), vmem(NZ, 16, 128), vmem(NZ, 16, 128),
        pltpu.VMEM((NZ, 16, 128), jnp.int32), pltpu.SemaphoreType.DMA((5,)),
        vmem(4, NZ, 24, 256), vmem(8, 128), level_scratch(NZ, 24, 256),
        vmem(4, NZ, 24, 128), level_scratch(NZ, 24, 128),
        vmem(4, HZ, 32, 128), level_scratch(HZ, 32, 128),
        vmem(4, HZ, 16, 128), level_scratch(HZ, 16, 128),
        vmem(3, HZ, 32, 128), level_scratch(HZ, 32, 128),
        vmem(NZ, 16, 128), vmem(NZ, 16, 128), vmem(HZ, 8, 128), vmem(HZ, 32, 128), vmem(HZ, 32, 128), vmem(NZ, 8, 128),
        vmem(2, 4 * NZ + HZ, 2, 128), vmem(2, 4, 16, 128), vmem(2, 4 * NZ + HZ, 2, 128), vmem(2, 4, 16, 128), vmem(4, 4, 8, 128),
        vmem(HZ, 8, 128), vmem(2, 5, 8, 128), vmem(2, 2, 5, 4, 128),
        vmem(2, HZ, 8, 128), vmem(2, 5, 8, 128), vmem(2, 2, 5, 4, 128),
        vmem(HZ, 4, 128), vmem(7, HZ, 4, 128),
        vmem(16, 128), vmem(7, 16, 128), vmem(16 * 16, 128), vmem(16 * 16, 128),
        vmem(4 * HZ, 8, 128), vmem(2, 20, 8, 128), vmem(2, 2, 20, 4, 128),
        vmem(2, 4 * HZ, 8, 128), vmem(2, 20, 8, 128), vmem(2, 2, 20, 4, 128),
        vmem(4 * HZ, 4, 128), vmem(7, 4 * HZ, 4, 128),
        vmem(32, 128), vmem(7, 32, 128), vmem(16 * 32, 128), vmem(16 * 32, 128),
        vmem(2, NZ, 4, 128), vmem(2, 1, 16, 128), vmem(2, NZ, 4, 128), vmem(2, 1, 16, 128), vmem(4, 1, 8, 128),
        pltpu.SemaphoreType.DMA((96,)), pltpu.SemaphoreType.DMA((96,)),
    ]
    shape = jax.ShapeDtypeStruct(source.shape, F32)
    anywhere = pl.BlockSpec(memory_space=pl.ANY)
    found = pl.pallas_call(
        body,
        out_shape=(shape, shape),
        in_specs=[anywhere] * 5,
        out_specs=[anywhere] * 2,
        scratch_shapes=scratch,
        compiler_params=pltpu.CompilerParams(
            collective_id=0, has_side_effects=True, vmem_limit_bytes=62 * 1024 * 1024
        ),
    )(source, kappa_sq, lon_diff, lat_diff, sea_mask)
    return pl.pallas_call(
        deliver,
        out_shape=(shape, shape),
        in_specs=[anywhere] * 2,
        out_specs=[anywhere] * 2,
        scratch_shapes=[pltpu.SemaphoreType.DMA((2,))],
        compiler_params=pltpu.CompilerParams(vmem_limit_bytes=62 * 1024 * 1024),
    )(*found)


def solution(mesh):
    spec = P(None, "tx", "ty")
    return jax.shard_map(
        shards, mesh=mesh, in_specs=(spec,) * 5, out_specs=(spec, spec), check_vma=False
    )
```

time: 903 us -> 70.2 us (0.08); the launches traced: 890 us -> 70.1 us
  starting transfers between devices: 657 us -> 0 us
  waiting for transfers between devices: 84.6 us -> 0 us
  local copies, waits for them, and re-layouts: 81 us -> 0 us
  Pallas kernels: 0 us -> 69.5 us
  other arithmetic: 62.9 us -> 0 us
    ppermute x164 -> x0, starting transfers between devices: 657 us -> none  [the longest x82 453 us: extended(): lax.ppermute(lax.slice_in_dim(block, 0, width, axis=dim), axis, backward)]
    ppermute x164 -> x0, waiting for transfers between devices: 84.6 us -> none  [the longest x82 59.9 us: extended(): lax.ppermute(lax.slice_in_dim(block, block.shape[dim] - width, None, axis...]
    pallas_call x0 -> x2, Pallas kernels: none -> 69.5 us  [the longest x1 58.4 us: shards(): pl.pallas_call(body, out_shape=(shape, shape), in_specs=[anywhere] * 5, o...]
    slice x87 -> x0, local copies, waits for them, and re-layouts: 33.1 us -> none  [the longest x37 16.9 us: shift_down(): return jnp.concatenate([jnp.zeros_like(field[:1]), field[:-1]], axis=0)]
    while x266 -> x0, local copies, waits for them, and re-layouts: 24.6 us -> none
    add x35 -> x0, other arithmetic: 21.9 us -> none  [the longest x31 21.8 us: sweep(): return field + OMEGA * (right - apply_op(field, faces, rim_pad)) / faces[6]]
    unnamed x201 -> x0, local copies, waits for them, and re-layouts: 18.9 us -> none
    reduce_sum x20 -> x0, other arithmetic: 9.18 us -> none  [block_mean(): return field.reshape(depth, wide // 2, 2, tall // 2, 2).mean(axis=(2, 4))]
  transfers between devices with their start and end apart: 164 -> 0, of which waited for: 49 -> 0; matrix products, arithmetic and copies ran while one was open for 8% -> 0% of each run, Pallas kernels for 0% -> 0%
where the time goes in v1:
time: 70.2 us; the launch traced here: 70.1 us
  Pallas kernels  69.5 us (99%)
    pallas_call x1, Pallas kernels, shards(): pl.pallas_call(body, out_shape=(shape, shape), in_specs=[anywhere] * 5, o...  58.4 us
    pallas_call x1, Pallas kernels, shards(): pl.pallas_call(deliver, out_shape=(shape, shape), in_specs=[anywhere] * 2...  11 us

profile of v1, /device:TPU:1, one launch (start us, length us, event | category | flops | bytes accessed | tf_op | source)
XLA Modules:
  0.0 70.1 jit_solution(14785501513726645623)
XLA Ops:
  0.6 58.4 %shard_map.68 = (f32[20,16,128]{2,1,0:T(8,128)}, f32[20,16,128]{2,1,0:T(8,128)}) custom-call(f32[20,16,128]{2,1,0:T(8,128)} %source_in.1, f32[20,16,128]{2,1,0:T(8,128)} %kappa_in.1, f32[20,16,128]{2,1,0:T(8,128)} %lon_in.1, f32[20,16,128]{2,1,0:T(8,128)} %lat_in.1, s32[20,16,128]{2,1,0:T(8,128)} %mask_in.1), custom_call_target="tpu_custom_call" | custom-call | tf_op jit(solution)/shard_map/pallas_call | solution.py:732
  59.0 11.0 %shard_map.69 = (f32[20,16,128]{2,1,0:T(8,128)}, f32[20,16,128]{2,1,0:T(8,128)}) custom-call(f32[20,16,128]{2,1,0:T(8,128)} %get-tuple-element.4.sol_in, f32[20,16,128]{2,1,0:T(8,128)} %get-tuple-element.5.resid_in), custom_call_target="tpu_custom_call" | custom-call | tf_op jit(solution)/shard_map/pallas_call | solution.py:742

commit v2 on v1

--- a/solution.py
+++ b/solution.py
@@ -98,10 +98,10 @@
 
         lax.fori_loop(0, self.slabs, step, 0, unroll=min(unroll, self.slabs))
 
-    def wrap(self, ref):
+    def wrap(self, ref, rows=slice(None)):
         if self.folded:
-            ref[0] = roll(ref[self.slabs], 64, 1)
-            ref[self.slabs + 1] = roll(ref[1], 64, 1)
+            ref[0, rows] = roll(ref[self.slabs, rows], 64, 1)
+            ref[self.slabs + 1, rows] = roll(ref[1, rows], 64, 1)
 
     def clear_ends(self):
         if not self.folded:
@@ -141,26 +141,31 @@
 
         self.each(horizontal, unroll)
 
-    def total(self, src, z):
-        u = src[z + 1]
-        e = self.e[z]
-        n = self.n[z]
-        return u, (
-            roll(e * u, 1, 0)
-            + e * roll(u, -1, 0)
-            + roll(n * u, 1, 1)
-            + n * roll(u, -1, 1)
-            + self.v[z] * src[z]
-            + self.v[z + 1] * src[z + 2]
-        )
-
-    def sweep(self, src, dst, unroll):
-        def body(z):
-            u, total = self.total(src, z)
-            dst[z + 1] = (1.0 - OMEGA) * u + self.c[z] + self.g[z] * total
-
-        self.each(body, unroll)
-        self.wrap(dst)
+    def stencil(self, src, unroll, use, rows=slice(None)):
+        def step(z, carry):
+            below, u, face_below = carry
+            above = src[z + 2, rows]
+            face_above = self.v[z + 1, rows]
+            e = self.e[z, rows]
+            n = self.n[z, rows]
+            use(z, u, (
+                roll(e * u, 1, 0)
+                + e * roll(u, -1, 0)
+                + roll(n * u, 1, 1)
+                + n * roll(u, -1, 1)
+                + face_below * below
+                + face_above * above
+            ))
+            return u, above, face_above
+
+        lax.fori_loop(0, self.slabs, step, (src[0, rows], src[1, rows], self.v[0, rows]), unroll=min(unroll, self.slabs))
+
+    def sweep(self, src, dst, unroll, rows=slice(None)):
+        def use(z, u, total):
+            dst[z + 1, rows] = (1.0 - OMEGA) * u + self.c[z, rows] + self.g[z, rows] * total
+
+        self.stencil(src, unroll, use, rows)
+        self.wrap(dst, rows)
 
     def start(self, unroll):
         def body(z):
@@ -169,9 +174,8 @@
         self.each(body, unroll)
         self.wrap(self.u)
 
-    def remain(self, src, z):
-        u, total = self.total(src, z)
-        return self.d[z] * (1.25 * self.c[z] - u) + total
+    def remain(self, src, unroll, put):
+        self.stencil(src, unroll, lambda z, u, total: put(z, self.d[z] * (1.25 * self.c[z] - u) + total))
 
 
 def pack_edge(slabs, width, base, count):
@@ -184,14 +188,14 @@
 
 def body(
     source_in, kappa_in, lon_in, lat_in, mask_in,
-    sol_out, resid_out,
-    sol, resid, out_sem, source, kappa, lon_diff, lat_diff, mask, in_sem,
+    sol, resid,
+    source, kappa, lon_diff, lat_diff, mask, in_sem,
     raw0, src0, l0, raw1, l1, raw2, l2, raw3, l3, raw4, l4, t0, t1, t2, t3, t4, q1,
     a_ew, a_ns, a_rew, a_rns, a_rd,
     b_pk, b_ns, b_nc, b_rpk, b_rns, b_rnc,
     f_p, f_rp,
-    k_blk, k_z, k_ev, k_od,
-    p_pk, p_ns, p_nc, p_rpk, p_rns, p_rnc, g_p, g_rp, h_blk, h_z, h_ev, h_od,
+    k_blk, k_z, k_ev,
+    p_pk, p_ns, p_nc, p_rpk, p_rns, p_rnc, q_p, q_rp, g_p, g_rp, h_blk, h_z, h_ev, h_od,
     o_ew, o_ns, o_rew, o_rns, o_rd,
     send_sem, recv_sem,
 ):
@@ -199,13 +203,24 @@
     odd = lax.rem(mx, 2) == 1
     counter = [0]
     pending = []
+    places = {}
+
+    def shifted(axis, here, shift, count):
+        shift = shift % count
+        if (axis, shift) not in places:
+            there = here + shift
+            places[axis, shift] = jnp.where(there >= count, there - count, there) if shift else here
+        return places[axis, shift]
+
+    def device(dx, dy):
+        return (shifted(0, mx, dx, NTX), shifted(1, my, dy, NTY))
 
     def copy(src, dst, dx, dy):
         i = counter[0]
         counter[0] += 1
         made = pltpu.make_async_remote_copy(
             src_ref=src, dst_ref=dst, send_sem=send_sem.at[i], recv_sem=recv_sem.at[i],
-            device_id=(lax.rem(mx + (dx + NTX), NTX), lax.rem(my + (dy + NTY), NTY)),
+            device_id=device(dx, dy),
             device_id_type=MESH,
         )
         made.start()
@@ -237,48 +252,52 @@
     for dx, dy in peers:
         pl.semaphore_signal(
             barrier, inc=1,
-            device_id=(lax.rem(mx + (dx + NTX), NTX), lax.rem(my + (dy + NTY), NTY)),
+            device_id=device(dx, dy),
             device_id_type=MESH,
         )
 
-    for made in fetched:
-        made.wait()
-
-    def own0(z):
-        s = mask[z].astype(F32)
-        return (kappa[z], s * lon_diff[z], s * lat_diff[z], source[z])
-
     lane16 = iota((16, 128), 1)
+    place = ((1, 0), (0, 0), (0, 60), (1, 60))
     edge_n = [jnp.zeros((16, 128), F32)] * 4
     edge_s = [jnp.zeros((16, 128), F32)] * 4
-    for z in range(NZ):
-        for f, x in enumerate(own0(z)):
+    own0 = (
+        lambda z: kappa[z],
+        lambda z: mask[z].astype(F32) * lon_diff[z],
+        lambda z: mask[z].astype(F32) * lat_diff[z],
+        lambda z: source[z],
+    )
+    for f, needed in ((1, (0, 1)), (2, (2,)), (0, (3,)), (3, (4,))):
+        for i in needed:
+            fetched[i].wait()
+        for z in range(NZ):
+            x = own0[f](z)
             raw0[f, z, 0:16, 0:128] = x
             a_ew[0, f * NZ + z] = x[0:2]
             a_ew[1, f * NZ + z] = x[14:16]
             if f == 1:
                 a_ew[0, 4 * NZ + z // 2, z % 2:z % 2 + 1] = x[2:3]
                 a_ew[1, 4 * NZ + z // 2, z % 2:z % 2 + 1] = x[13:14]
-            edge_n[f] = jnp.where(lane16 >= 4 * z, roll(x, 4 * z - 124, 1), edge_n[f])
-            edge_s[f] = jnp.where(lane16 >= 4 * z, roll(x, 4 * z, 1), edge_s[f])
-    for f in range(4):
-        a_ns[0, f] = edge_n[f]
-        a_ns[1, f] = edge_s[f]
+            start = place[f][1] + 3 * z
+            edge_n[f] = jnp.where(lane16 >= start, roll(x, start - 125, 1), edge_n[f])
+            edge_s[f] = jnp.where(lane16 >= start, roll(x, start, 1), edge_s[f])
+    for pair, (f, g) in enumerate(((1, 2), (0, 3))):
+        a_ns[0, pair] = jnp.where(lane16 < 60, edge_n[f], edge_n[g])
+        a_ns[1, pair] = jnp.where(lane16 < 60, edge_s[f], edge_s[g])
 
     pl.semaphore_wait(barrier, len(peers))
 
     def send_edges(ew, ns, rew, rns, rd):
-        made = [copy(ew.at[0], rew.at[0], -1, 0), copy(ew.at[1], rew.at[1], 1, 0)]
-        made += [copy(ns.at[0], rns.at[0], 0, 1), copy(ns.at[1], rns.at[1], 0, -1)]
-        made.append(copy(ns.at[0, :, 8:16, :], rd.at[0], 1, 1))
+        made = [copy(ns.at[0, :, 8:16, :], rd.at[0], 1, 1)]
         made.append(copy(ns.at[0, :, 0:8, :], rd.at[1], -1, 1))
         made.append(copy(ns.at[1, :, 8:16, :], rd.at[2], 1, -1))
         made.append(copy(ns.at[1, :, 0:8, :], rd.at[3], -1, -1))
+        made += [copy(ew.at[0], rew.at[0], -1, 0), copy(ew.at[1], rew.at[1], 1, 0)]
+        made += [copy(ns.at[0], rns.at[0], 0, 1), copy(ns.at[1], rns.at[1], 0, -1)]
         return made
 
     has_s, has_n = my > 0, my < NTY - 1
 
-    def merge_edges(f, rows, rns, rd, put_rows, put_side):
+    def merge_edges(f, base, rns, rd, put_rows, put_side):
         sub = iota((8, 128), 0)
         south = jnp.concatenate([rns[0, f], jnp.where(sub < 4, rd[1, f], rd[0, f])], axis=0)
         north = jnp.concatenate([rns[1, f], jnp.where(sub < 4, rd[3, f], rd[2, f])], axis=0)
@@ -286,11 +305,15 @@
         south = jnp.where(has_s, south, 0.0)
         north = jnp.where(has_n, north, 0.0)
         for z in range(NZ):
-            put_rows(z, rows(z))
-            side = jnp.where(lane < 4, roll(north, -4 * z, 1), roll(south, 124 - 4 * z, 1))
-            put_side(z, jnp.where((lane < 4) | (lane >= 124), side, 0.0))
+            put_rows(z)
+            start = base + 3 * z
+            side = jnp.where(lane < 3, roll(north, -start, 1), roll(south, 125 - start, 1))
+            put_side(z, jnp.where((lane < 3) | (lane >= 125), side, 0.0))
 
     sent_a = send_edges(a_ew, a_ns, a_rew, a_rns, a_rd)
+    for f in range(4):
+        for z in range(NZ):
+            raw0[f, z, 16:24, 0:128] = jnp.zeros((8, 128), F32)
 
     m0 = restrict_0()
 
@@ -311,12 +334,12 @@
                 nc[side, 1, f * 5 + k] = edge[4:8]
 
     def send_1(pk, ns, nc, rpk, rns, rnc):
-        made = [copy(pk, rpk.at[0], -1, 0), copy(pk, rpk.at[1], 1, 0)]
-        made += [copy(ns.at[0], rns.at[0], 0, 1), copy(ns.at[1], rns.at[1], 0, -1)]
-        made.append(copy(nc.at[0, 1], rnc.at[0, 1], 1, 1))
+        made = [copy(nc.at[0, 1], rnc.at[0, 1], 1, 1)]
         made.append(copy(nc.at[0, 0], rnc.at[0, 0], -1, 1))
         made.append(copy(nc.at[1, 1], rnc.at[1, 1], 1, -1))
         made.append(copy(nc.at[1, 0], rnc.at[1, 0], -1, -1))
+        made += [copy(pk, rpk.at[0], -1, 0), copy(pk, rpk.at[1], 1, 0)]
+        made += [copy(ns.at[0], rns.at[0], 0, 1), copy(ns.at[1], rns.at[1], 0, -1)]
         return made
 
     def merge_1(f, own, rpk, rns, rnc, put):
@@ -344,26 +367,34 @@
         0.25 * down_0(lat_diff[...]),
         (down_0(mask[...].astype(F32)) > 0.0).astype(F32),
     ]
+
+    m1 = restrict_1()
+
+    def down_1(x):
+        pair = jnp.concatenate([x[0:HZ], x[HZ:NZ]], axis=2).reshape(HZ * 8, 256)
+        t2[...] = mm(pair, m1).reshape(HZ, 8, 128)
+        return t2[:, pl.ds(0, 4, stride=2), :] + t2[:, pl.ds(1, 4, stride=2), :]
+
+    own2 = [
+        down_1(own1[0]),
+        0.25 * down_1(own1[1]),
+        0.25 * down_1(own1[2]),
+        (down_1(own1[3]) > 0.0).astype(F32),
+    ]
     for f in range(4):
-        pack_1(own1[f], f, p_pk, p_ns, p_nc)
-        raw1[f, :, 8:16, :] = own1[f]
+        g_p[f * HZ:(f + 1) * HZ] = own2[f]
+        for k in range(5):
+            q_p[f * 5 + k] = own2[f][k] + roll(own2[f][k + 5], 32, 1)
+    sent_q = [copy(q_p, q_rp.at[0], 0, 1), copy(q_p, q_rp.at[1], 0, -1)]
+
+    for f, x in enumerate((own1[0], own1[3] * own1[1], own1[3] * own1[2])):
+        pack_1(x, f, p_pk, p_ns, p_nc)
+        raw1[f, :, 8:16, :] = x
     sent_p1 = send_1(p_pk, p_ns, p_nc, p_rpk, p_rns, p_rnc)
-
-    mall = restrict_all()
-
-    def down_all(x):
-        pair = jnp.concatenate([x[0:HZ], x[HZ:NZ]], axis=2).reshape(HZ * 16, 256)
-        return jnp.sum(mm(pair, mall).reshape(HZ, 16, 128), axis=1)
-
-    sea4 = (down_all(mask[...].astype(F32)) > 0.0).astype(F32)
-    h_blk[0:10, :] = down_all(kappa[...])
-    h_blk[10:20, :] = sea4 * (down_all(lon_diff[...]) * (1.0 / 256))
-    h_blk[20:30, :] = sea4 * (down_all(lat_diff[...]) * (1.0 / 256))
-    h_blk[30:32, :] = jnp.zeros((2, 128), F32)
 
     def send_z(blk, slots):
         slots[3] = blk[...]
-        return [copy(blk, slots.at[3 - d], 0, d) for d in (1, -1, 2, -2, 3, -3)]
+        return [copy(blk, slots.at[3 - d], 0, d) for d in (3, -3, 2, -2, 1, -1)]
 
     def window_row(slots, count):
         row = jnp.zeros((count, 128), F32)
@@ -372,12 +403,23 @@
             row = row + jnp.where(inside, roll(slots[s], 8 * (s - 3), 1), 0.0)
         return row
 
+    def folded_window_row(slots):
+        part = iota((8, 128), 1) & 63
+        out = [jnp.zeros((8, 128), F32)] * 3
+        for s in range(7):
+            inside = (my + (s - 3) >= 0) & (my + (s - 3) < NTY)
+            block = jnp.where(inside, slots[s], 0.0)
+            for i in range(3):
+                pick = (part >= 24 + 8 * i) & (part < 32 + 8 * i)
+                out[i] = out[i] + roll(jnp.where(pick, block, 0.0), 8 * (s - 3 - i), 1)
+        return jnp.concatenate(out, axis=0)
+
     def send_plane(row, ev, count):
         own = pl.ds(8 * count, count)
         ev[own, :] = row
         return [
             copy(ev.at[own], ev.at[pl.ds(((8 - k) % 16) * count, count)], 2 * k, 0)
-            for k in (1, 15, 2, 14, 3, 13, 4, 12, 5, 11, 6, 10, 7, 9, 8)
+            for k in (10, 6, 9, 7, 11, 5, 2, 14, 8, 3, 13, 1, 15, 4, 12)
         ]
 
     def send_sibling(ev, od):
@@ -396,33 +438,41 @@
         other = od[pl.ds(index, 16, stride=count), :]
         put(pl.ds(1, 16, stride=2), jnp.where(odd, roll(other, -1, 0), other))
 
-    sent_hz = send_z(h_blk, h_z)
-
     arrive(sent_a)
     for f in range(4):
-        def put_rows(z, x):
-            raw0[f, z, 16:24, 0:128] = x
+        def put_rows(z):
+            raw0[f, z, 16:18, 0:128] = a_rew[0, f * NZ + z]
+            raw0[f, z, 22:24, 0:128] = a_rew[1, f * NZ + z]
+            if f == 1:
+                pick = slice(z % 2, z % 2 + 1)
+                raw0[f, z, 18:19, 0:128] = a_rew[0, 4 * NZ + z // 2, pick]
+                raw0[f, z, 21:22, 0:128] = a_rew[1, 4 * NZ + z // 2, pick]
 
         def put_side(z, x):
             raw0[f, z, :, 128:256] = x
 
-        def rows(z):
-            pick = slice(z % 2, z % 2 + 1)
-            blank = jnp.zeros((1, 128), F32)
-            near, far = [blank], [blank]
-            if f == 1:
-                near, far = [a_rew[0, 4 * NZ + z // 2, pick]], [a_rew[1, 4 * NZ + z // 2, pick]]
-            return jnp.concatenate(
-                [a_rew[0, f * NZ + z]] + near + [blank, blank] + far + [a_rew[1, f * NZ + z]], axis=0
-            )
-
-        merge_edges(f, rows, a_rns, a_rd, put_rows, put_side)
+        merge_edges(place[f][0], place[f][1], a_rns, a_rd, put_rows, put_side)
+
+    def send_2(p, rp):
+        return [copy(p, rp.at[3 - d], d, 0) for d in (3, -3, 2, -2, 1, -1)]
+
+    arrive(sent_q)
+    part = iota((4, 128), 1) & 63
+    for f in range(4):
+        for k in range(HZ):
+            south = roll(q_rp[0, f * 5 + k % 5], -32 if k < 5 else -64, 1)
+            north = roll(q_rp[1, f * 5 + k % 5], 32 if k < 5 else 0, 1)
+            south = jnp.where(has_s, south, 0.0)
+            north = jnp.where(has_n, north, 0.0)
+            g_p[f * HZ + k] = jnp.where(part < 16, south, jnp.where(part < 48, g_p[f * HZ + k], north))
+    sent_p2 = send_2(g_p, g_rp)
 
     def sea0(z):
         return (raw0[1, z] > 0.0).astype(F32)
 
     lev0.faces(lambda z: raw0[0, z], lambda z: raw0[1, z], lambda z: raw0[2, z], sea0, UNROLL)
     lev0.clear_ends()
+
 
     def first0(z):
         c = lev0.g[z] * raw0[3, z]
@@ -432,21 +482,24 @@
     lev0.each(first0, UNROLL)
     lev0.sweep(lev0.u, lev0.w, UNROLL)
 
-    def remain0(z):
-        u, total = lev0.total(lev0.w, z)
+    def remain0(z, u, total):
         r = raw0[3, z] - (lev0.d[z] * u - total)
         t0[z] = r[0:16, 0:128]
 
-    lev0.each(remain0, UNROLL)
+    lev0.stencil(lev0.w, UNROLL, remain0)
     b1 = down_0(t0[...])
 
     arrive(sent_p1)
-    for f in range(4):
+    for f in range(3):
         def put1(z, start, x):
             raw1[f, z, start:start + 8, :] = x
 
         merge_1(f, lambda z: raw1[f, z, 8:16, :], p_rpk, p_rns, p_rnc, put1)
-    lev1.faces(lambda z: raw1[0, z], lambda z: raw1[1, z], lambda z: raw1[2, z], lambda z: raw1[3, z], UNROLL)
+
+    def sea_1(z):
+        return (raw1[1, z] > 0.0).astype(F32)
+
+    lev1.faces(lambda z: raw1[0, z], lambda z: raw1[1, z], lambda z: raw1[2, z], sea_1, UNROLL)
     lev1.clear_ends()
     c1 = lev1.g[:, 8:16, :] * b1
     q1[...] = c1
@@ -459,47 +512,22 @@
         x = lev0.w[z + 1, 0:16, 0:128]
         o_ew[0, z] = x[0:4]
         o_ew[1, z] = x[12:16]
-        edge_n = jnp.where(lane16 >= 4 * z, roll(x, 4 * z - 124, 1), edge_n)
-        edge_s = jnp.where(lane16 >= 4 * z, roll(x, 4 * z, 1), edge_s)
+        edge_n = jnp.where(lane16 >= 3 * z, roll(x, 3 * z - 125, 1), edge_n)
+        edge_s = jnp.where(lane16 >= 3 * z, roll(x, 3 * z, 1), edge_s)
     o_ns[0, 0] = edge_n
     o_ns[1, 0] = edge_s
-    sent_o = send_edges(o_ew, o_ns, o_rew, o_rns, o_rd)
-
-    m1 = restrict_1()
-
-    def down_1(x):
-        pair = jnp.concatenate([x[0:HZ], x[HZ:NZ]], axis=2).reshape(HZ * 8, 256)
-        t2[...] = mm(pair, m1).reshape(HZ, 8, 128)
-        return t2[:, pl.ds(0, 4, stride=2), :] + t2[:, pl.ds(1, 4, stride=2), :]
-
-    own2 = [
-        down_1(raw1[0, :, 8:16, :]),
-        0.25 * down_1(raw1[1, :, 8:16, :]),
-        0.25 * down_1(raw1[2, :, 8:16, :]),
-        (down_1(raw1[3, :, 8:16, :]) > 0.0).astype(F32),
-    ]
-
-    def send_2(p, rp):
-        return [copy(p, rp.at[3 - d], d, 0) for d in (1, -1, 2, -2, 3, -3)]
-
-    for f in range(4):
-        g_p[f * HZ:(f + 1) * HZ] = own2[f]
-    sent_p2 = send_2(g_p, g_rp)
-
-    arrive(sent_b)
-
-    def put1c(z, start, x):
-        lev1.c[z, start:start + 8, :] = x
-        lev1.u[z + 1, start:start + 8, :] = x
-
-    merge_1(0, lambda z: q1[z], b_rpk, b_rns, b_rnc, put1c)
-    lev1.sweep(lev1.u, lev1.w, UNROLL)
-
-    def remain1(z):
-        q1[z] = lev1.remain(lev1.w, z)[8:16]
-
-    lev1.each(remain1, UNROLL)
-    b2 = down_1(q1[...])
+
+    mall = restrict_all()
+
+    def down_all(x):
+        pair = jnp.concatenate([x[0:HZ], x[HZ:NZ]], axis=2).reshape(HZ * 16, 256)
+        return jnp.sum(mm(pair, mall).reshape(HZ, 16, 128), axis=1)
+
+    sea4 = (down_all(mask[...].astype(F32)) > 0.0).astype(F32)
+    h_blk[0:10, :] = down_all(kappa[...])
+    h_blk[10:20, :] = sea4 * (down_all(lon_diff[...]) * (1.0 / 256))
+    h_blk[20:30, :] = sea4 * (down_all(lat_diff[...]) * (1.0 / 256))
+    h_blk[30:32, :] = jnp.zeros((2, 128), F32)
 
     arrive(sent_p2)
     for f in range(4):
@@ -508,11 +536,6 @@
             raw2[f, :, 4 * s:4 * s + 4, :] = piece[f * HZ:(f + 1) * HZ]
         raw2[f, :, 28:32, :] = jnp.zeros((HZ, 4, 128), F32)
     lev2.faces(lambda z: raw2[0, z], lambda z: raw2[1, z], lambda z: raw2[2, z], lambda z: raw2[3, z], UNROLL)
-    f_p[...] = lev2.g[:, 12:16, :] * b2
-    sent_c = send_2(f_p, f_rp)
-
-    arrive(sent_hz)
-    sent_hp = send_plane(window_row(h_z, 32), h_ev, 32)
 
     m2 = restrict_2()
 
@@ -526,7 +549,30 @@
     raw3[3] = (down_2(raw2[3]) > 0.0).astype(F32)
     lev3.faces(lambda z: raw3[0, z], lambda z: raw3[1, z], lambda z: raw3[2, z], lambda z: raw3[3, z], UNROLL)
 
+    arrive(sent_b)
+    sent_hz = send_z(h_blk, h_z)
+
+    def put1c(z, start, x):
+        lev1.c[z, start:start + 8, :] = x
+        lev1.u[z + 1, start:start + 8, :] = x
+
+    merge_1(0, lambda z: q1[z], b_rpk, b_rns, b_rnc, put1c)
+    lev1.sweep(lev1.u, lev1.w, UNROLL)
+
+    def remain1(z, r):
+        q1[z] = r[8:16]
+
+    lev1.remain(lev1.w, UNROLL, remain1)
+    b2 = down_1(q1[...])
+
+    f_p[...] = lev2.g[:, 12:16, :] * b2
+    sent_c = send_2(f_p, f_rp)
+
+    arrive(sent_hz)
+    row_h = window_row(h_z, 32)
     arrive(sent_c)
+    sent_hp = send_plane(row_h, h_ev, 32)
+    sent_o = send_edges(o_ew, o_ns, o_rew, o_rns, o_rd)
     for s in range(7):
         piece = f_p if s == 3 else f_rp.at[s]
         lev2.c[:, 4 * s:4 * s + 4, :] = piece[...]
@@ -534,28 +580,35 @@
     lev2.start(UNROLL)
     lev2.sweep(lev2.u, lev2.w, UNROLL)
 
-    def remain2(z):
-        t4[z] = lev2.remain(lev2.w, z)
-
-    lev2.each(remain2, UNROLL)
+    def remain2(z, r):
+        t4[z] = r
+
+    lev2.remain(lev2.w, UNROLL, remain2)
 
     lev3.c[...] = lev3.g[...] * down_2(t4[...])
     lev3.start(UNROLL)
     lev3.sweep(lev3.u, lev3.w, UNROLL)
 
-    def remain3(z):
-        t3[z, 0:16, :] = lev3.remain(lev3.w, z)
-
-    lev3.each(remain3, UNROLL)
+    def remain3(z, r):
+        t3[z, 0:16, :] = r
+
+    lev3.remain(lev3.w, UNROLL, remain3)
     m3 = restrict_3()
     t3[:, 0:16, :] = mm(t3[:, 0:16, :].reshape(HZ * 16, 128), m3).reshape(HZ, 16, 128)
-    for z in range(HZ):
-        k_blk[z:z + 1, :] = t3[z, 6:7, :] + t3[z, 7:8, :]
-    k_blk[HZ:16, :] = jnp.zeros((16 - HZ, 128), F32)
+    for z in range(8):
+        row = t3[z, 6:7, :] + t3[z, 7:8, :] + roll(t3[z, 8:9, :] + t3[z, 9:10, :], 8, 1)
+        if z < 4:
+            at = 6 if z < 2 else 8
+            last = t3[8 + z % 2, at:at + 1, :] + t3[8 + z % 2, at + 1:at + 2, :]
+            row = row + roll(last, 16, 1)
+        k_blk[z:z + 1, :] = row
     sent_kz = send_z(k_blk, k_z)
 
     arrive(sent_hp)
     sent_hs = send_sibling(h_ev, h_od)
+
+    arrive(sent_kz)
+    sent_kp = send_plane(folded_window_row(k_z), k_ev, 24)
 
     arrive(sent_hs)
     for f in range(3):
@@ -570,15 +623,11 @@
 
     lev4.faces(lambda z: raw4[0, z], lambda z: raw4[1, z], lambda z: raw4[2, z], sea_4, UNROLL)
 
-    arrive(sent_kz)
-    sent_kp = send_plane(window_row(k_z, 16), k_ev, 16)
     arrive(sent_kp)
-    arrive(send_sibling(k_ev, k_od))
     for z in range(HZ):
-        def put4c(rows, x):
-            lev4.c[z, rows, :] = x
-
-        window_slab(k_ev, k_od, z, 16, put4c)
+        for i in range(2):
+            at = 8 * i + z if z < 8 else 16 + 2 * i + z - 8
+            lev4.c[z, pl.ds(i, 16, stride=2), :] = k_ev[pl.ds(at, 16, stride=24), :]
     for z in range(HZ):
         lev4.c[z] = lev4.g[z] * lev4.c[z]
     lev4.start(UNROLL)
@@ -588,8 +637,10 @@
         lev4.sweep(lev4.w, lev4.u, UNROLL)
         return carry
 
-    lax.fori_loop(0, 9, two, 0)
-    lev4.sweep(lev4.u, lev4.w, UNROLL)
+    lax.fori_loop(0, 7, two, 0)
+    middle = slice(8, 24)
+    for src, dst in ((lev4.u, lev4.w), (lev4.w, lev4.u)) * 2 + ((lev4.u, lev4.w),):
+        lev4.sweep(src, dst, UNROLL, middle)
 
     up = mm(lev4.w[1:HZ + 1, 13:21, :].reshape(HZ * 8, 128), prolong_3()).reshape(HZ, 8, 128)
     for start in range(2):
@@ -634,16 +685,14 @@
 
     arrive(sent_o)
 
-    def put_rows0(z, x):
-        lev0.w[z + 1, 16:24, 0:128] = x
+    def put_rows0(z):
+        lev0.w[z + 1, 16:20, 0:128] = o_rew[0, z]
+        lev0.w[z + 1, 20:24, 0:128] = o_rew[1, z]
 
     def put_side0(z, x):
         lev0.w[z + 1, :, 128:256] = x
 
-    def rows0(z):
-        return jnp.concatenate([o_rew[0, z], o_rew[1, z]], axis=0)
-
-    merge_edges(0, rows0, o_rns, o_rd, put_rows0, put_side0)
+    merge_edges(0, 0, o_rns, o_rd, put_rows0, put_side0)
     for z in range(NZ):
         t1[z, 0:8, :] = lev1.w[z + 1, 8:16, :]
         t1[z, 8:10, :] = lev1.w[z + 1, 16:18, :]
@@ -664,34 +713,16 @@
     lev0.each(add0, UNROLL)
     lev0.sweep(lev0.w, lev0.u, UNROLL)
     lev0.sweep(lev0.u, lev0.w, UNROLL)
-    sol[...] = lev0.w[1:NZ + 1, 0:16, 0:128]
-    out_sol = pltpu.make_async_copy(sol, sol_out, out_sem.at[0])
-    out_sol.start()
-
-    def last0(z):
-        u, total = lev0.total(lev0.w, z)
+
+    def last0(z, u, total):
         r = raw0[3, z] - (lev0.d[z] * u - total)
+        sol[z] = u[0:16, 0:128]
         resid[z] = r[0:16, 0:128]
 
-    lev0.each(last0, UNROLL)
-    out_resid = pltpu.make_async_copy(resid, resid_out, out_sem.at[1])
-    out_resid.start()
+    lev0.stencil(lev0.w, UNROLL, last0)
 
     for made in pending:
         made.wait_send()
-    out_sol.wait()
-    out_resid.wait()
-
-
-def deliver(sol_in, resid_in, sol_out, resid_out, sem):
-    copies = [
-        pltpu.make_async_copy(sol_in, sol_out, sem.at[0]),
-        pltpu.make_async_copy(resid_in, resid_out, sem.at[1]),
-    ]
-    for made in copies:
-        made.start()
-    for made in copies:
-        made.wait()
 
 
 def level_scratch(slabs, rows, lanes):
@@ -706,22 +737,22 @@
         return pltpu.VMEM(shape, F32)
 
     scratch = [
-        vmem(NZ, 16, 128), vmem(NZ, 16, 128), pltpu.SemaphoreType.DMA((2,)),
         vmem(NZ, 16, 128), vmem(NZ, 16, 128), vmem(NZ, 16, 128), vmem(NZ, 16, 128),
         pltpu.VMEM((NZ, 16, 128), jnp.int32), pltpu.SemaphoreType.DMA((5,)),
         vmem(4, NZ, 24, 256), vmem(8, 128), level_scratch(NZ, 24, 256),
-        vmem(4, NZ, 24, 128), level_scratch(NZ, 24, 128),
+        vmem(3, NZ, 24, 128), level_scratch(NZ, 24, 128),
         vmem(4, HZ, 32, 128), level_scratch(HZ, 32, 128),
         vmem(4, HZ, 16, 128), level_scratch(HZ, 16, 128),
         vmem(3, HZ, 32, 128), level_scratch(HZ, 32, 128),
         vmem(NZ, 16, 128), vmem(NZ, 16, 128), vmem(HZ, 8, 128), vmem(HZ, 32, 128), vmem(HZ, 32, 128), vmem(NZ, 8, 128),
-        vmem(2, 4 * NZ + HZ, 2, 128), vmem(2, 4, 16, 128), vmem(2, 4 * NZ + HZ, 2, 128), vmem(2, 4, 16, 128), vmem(4, 4, 8, 128),
+        vmem(2, 4 * NZ + HZ, 2, 128), vmem(2, 2, 16, 128), vmem(2, 4 * NZ + HZ, 2, 128), vmem(2, 2, 16, 128), vmem(4, 2, 8, 128),
         vmem(HZ, 8, 128), vmem(2, 5, 8, 128), vmem(2, 2, 5, 4, 128),
         vmem(2, HZ, 8, 128), vmem(2, 5, 8, 128), vmem(2, 2, 5, 4, 128),
         vmem(HZ, 4, 128), vmem(7, HZ, 4, 128),
-        vmem(16, 128), vmem(7, 16, 128), vmem(16 * 16, 128), vmem(16 * 16, 128),
-        vmem(4 * HZ, 8, 128), vmem(2, 20, 8, 128), vmem(2, 2, 20, 4, 128),
-        vmem(2, 4 * HZ, 8, 128), vmem(2, 20, 8, 128), vmem(2, 2, 20, 4, 128),
+        vmem(8, 128), vmem(7, 8, 128), vmem(16 * 24, 128),
+        vmem(3 * HZ, 8, 128), vmem(2, 15, 8, 128), vmem(2, 2, 15, 4, 128),
+        vmem(2, 3 * HZ, 8, 128), vmem(2, 15, 8, 128), vmem(2, 2, 15, 4, 128),
+        vmem(20, 4, 128), vmem(2, 20, 4, 128),
         vmem(4 * HZ, 4, 128), vmem(7, 4 * HZ, 4, 128),
         vmem(32, 128), vmem(7, 32, 128), vmem(16 * 32, 128), vmem(16 * 32, 128),
         vmem(2, NZ, 4, 128), vmem(2, 1, 16, 128), vmem(2, NZ, 4, 128), vmem(2, 1, 16, 128), vmem(4, 1, 8, 128),
@@ -729,25 +760,16 @@
     ]
     shape = jax.ShapeDtypeStruct(source.shape, F32)
     anywhere = pl.BlockSpec(memory_space=pl.ANY)
-    found = pl.pallas_call(
+    return pl.pallas_call(
         body,
         out_shape=(shape, shape),
         in_specs=[anywhere] * 5,
-        out_specs=[anywhere] * 2,
+        out_specs=[pl.BlockSpec(memory_space=pltpu.VMEM)] * 2,
         scratch_shapes=scratch,
         compiler_params=pltpu.CompilerParams(
-            collective_id=0, has_side_effects=True, vmem_limit_bytes=62 * 1024 * 1024
+            collective_id=0, has_side_effects=True, vmem_limit_bytes=54848 * 1024
         ),
     )(source, kappa_sq, lon_diff, lat_diff, sea_mask)
-    return pl.pallas_call(
-        deliver,
-        out_shape=(shape, shape),
-        in_specs=[anywhere] * 2,
-        out_specs=[anywhere] * 2,
-        scratch_shapes=[pltpu.SemaphoreType.DMA((2,))],
-        compiler_params=pltpu.CompilerParams(vmem_limit_bytes=62 * 1024 * 1024),
-    )(*found)
-
 
 def solution(mesh):
     spec = P(None, "tx", "ty")

time: 70.2 us -> 53.3 us (0.76)
  Pallas kernels: 69.5 us -> 51.2 us
  local copies, waits for them, and re-layouts: 0 us -> 1.33 us
    pallas_call x1 -> x0, Pallas kernels: 11 us -> none  [shards(): pl.pallas_call(deliver, out_shape=(shape, shape), in_specs=[anywhere] * 2...]
    pallas_call x1, Pallas kernels: 58.4 us -> 51.2 us  [shards(): pl.pallas_call(body, out_shape=(shape, shape), in_specs=[anywhere] * 5, o...]
    unnamed x0 -> x2, local copies, waits for them, and re-layouts: none -> 1.33 us
where the time goes in v2:
time: 53.3 us; the launch traced here: 53.2 us
  Pallas kernels  51.2 us (96%)
  local copies, waits for them, and re-layouts  1.33 us (2%)
  between operations  0.64 us (1%)
    pallas_call x1, Pallas kernels, shards(): pl.pallas_call(body, out_shape=(shape, shape), in_specs=[anywhere] * 5, o...  51.2 us
    unnamed x2, local copies, waits for them, and re-layouts  1.33 us

profile of v2, /device:TPU:1, one launch (start us, length us, event | category | flops | bytes accessed | tf_op | source)
XLA Modules:
  0.0 53.2 jit_solution(17859500357515603475)
XLA Ops:
  0.6 51.2 %shard_map.68 = (f32[20,16,128]{2,1,0:T(8,128)S(1)}, f32[20,16,128]{2,1,0:T(8,128)S(1)}) custom-call(f32[20,16,128]{2,1,0:T(8,128)} %source_in.1, f32[20,16,128]{2,1,0:T(8,128)} %kappa_in.1, f32[20,16,128]{2,1,0:T(8,128)} %lon_in.1, f32[20,16,128]{2,1,0:T(8,128)} %lat_in.1, s32[20,16,128]{2,1,0:T(8,128)} %mask_in.1), custom_call_target="tpu_custom_call" | custom-call | tf_op jit(solution)/shard_map/pallas_call | solution.py:763
  51.9 0.7 %copy.9 = f32[20,16,128]{2,1,0:T(8,128)} copy(f32[20,16,128]{2,1,0:T(8,128)S(1)} %get-tuple-element.4) | data formatting | bytes 327680
  52.5 0.7 %copy.10 = f32[20,16,128]{2,1,0:T(8,128)} copy(f32[20,16,128]{2,1,0:T(8,128)S(1)} %get-tuple-element.5) | data formatting | bytes 327680

commit v3 on v2

--- a/solution.py
+++ b/solution.py
@@ -105,41 +105,47 @@
 
     def clear_ends(self):
         if not self.folded:
-            for ref in (self.u, self.w):
+            for ref in (self.c, self.u, self.w):
                 ref[0] = jnp.zeros_like(ref[0])
                 ref[self.slabs + 1] = jnp.zeros_like(ref[0])
 
-    def faces(self, kap, lond, latd, sea, unroll):
+    def faces(self, kap, lond, latd, sea, unroll, right=None):
         top = self.slabs - 1
-
-        def vertical(z):
-            here = sea(z)
-            self.v[z + 1] = here * sea(z + 1)
-
-        lax.fori_loop(0, top, lambda z, c: (vertical(z), c)[1], 0, unroll=min(unroll, top))
+        first = sea(0)
         if self.folded:
             low = iota(self.v.shape[1:], 1) < 64
-            self.v[self.slabs] = jnp.where(low, sea(top) * roll(sea(0), 64, 1), 0.0)
-            self.v[0] = roll(self.v[self.slabs], 64, 1)
+            face_top = jnp.where(low, sea(top) * roll(first, 64, 1), 0.0)
+            face_first = roll(face_top, 64, 1)
         else:
-            self.v[0] = jnp.zeros_like(self.v[0])
-            self.v[self.slabs] = jnp.zeros_like(self.v[0])
-
-        def horizontal(z):
-            s = sea(z)
+            face_top = face_first = jnp.zeros_like(first)
+        self.v[0] = face_first
+
+        def slab(z, s, face_below, face_above):
             lw = s * lond(z)
             tw = s * latd(z)
             east = 0.5 * (lw * roll(s, -1, 0) + s * roll(lw, -1, 0))
             north = 0.5 * (tw * roll(s, -1, 1) + s * roll(tw, -1, 1))
             west = roll(east, 1, 0)
             south = roll(north, 1, 1)
-            diag = s * kap(z) + (west + east + south + north + self.v[z] + self.v[z + 1]) + (1.0 - s)
+            diag = s * kap(z) + (west + east + south + north + face_below + face_above) + (1.0 - s)
+            scale = OMEGA / diag
+            self.v[z + 1] = face_above
             self.e[z] = east
             self.n[z] = north
             self.d[z] = diag
-            self.g[z] = OMEGA / diag
-
-        self.each(horizontal, unroll)
+            self.g[z] = scale
+            if right is not None:
+                self.c[z + 1] = scale * right(z)
+
+        def step(z, carry):
+            s, face_below = carry
+            s_above = sea(z + 1)
+            face_above = s * s_above
+            slab(z, s, face_below, face_above)
+            return s_above, face_above
+
+        s, face_below = lax.fori_loop(0, top, step, (first, face_first), unroll=min(unroll, top))
+        slab(top, s, face_below, face_top)
 
     def stencil(self, src, unroll, use, rows=slice(None)):
         def step(z, carry):
@@ -162,20 +168,13 @@
 
     def sweep(self, src, dst, unroll, rows=slice(None)):
         def use(z, u, total):
-            dst[z + 1, rows] = (1.0 - OMEGA) * u + self.c[z, rows] + self.g[z, rows] * total
+            dst[z + 1, rows] = (1.0 - OMEGA) * u + self.c[z + 1, rows] + self.g[z, rows] * total
 
         self.stencil(src, unroll, use, rows)
         self.wrap(dst, rows)
 
-    def start(self, unroll):
-        def body(z):
-            self.u[z + 1] = self.c[z]
-
-        self.each(body, unroll)
-        self.wrap(self.u)
-
     def remain(self, src, unroll, put):
-        self.stencil(src, unroll, lambda z, u, total: put(z, self.d[z] * (1.25 * self.c[z] - u) + total))
+        self.stencil(src, unroll, lambda z, u, total: put(z, self.d[z] * (1.25 * self.c[z + 1] - u) + total))
 
 
 def pack_edge(slabs, width, base, count):
@@ -342,24 +341,29 @@
         made += [copy(ns.at[0], rns.at[0], 0, 1), copy(ns.at[1], rns.at[1], 0, -1)]
         return made
 
-    def merge_1(f, own, rpk, rns, rnc, put):
+    def merge_1(f, own, rpk, rns, rnc, put, first):
         lane = iota((8, 128), 1)
         blank = jnp.zeros((4, 128), F32)
 
-        def edge(side, i, at):
-            if i == 0:
-                return rns[side, at]
-            if i == 1:
-                return jnp.concatenate([rnc[side, 0, at], blank], axis=0)
-            return jnp.concatenate([blank, rnc[side, 1, at]], axis=0)
+        def edges(z, pieces):
+            south = jnp.where(has_s, roll(pieces[0], -32 * (z // 5), 1), 0.0)
+            north = jnp.where(has_n, roll(pieces[1], 96 - 32 * (z // 5), 1), 0.0)
+            return south, north
 
         for z in range(NZ):
-            k, shift = (z, 32) if z < HZ else (z - HZ, -32)
-            middle = (own(z), roll(rpk[0, f * HZ + k], shift, 1), roll(rpk[1, f * HZ + k], shift, 1))
-            for i, start in ((0, 8), (1, 16), (2, 0)):
-                south = jnp.where(has_s, roll(edge(0, i, f * 5 + z % 5), -32 * (z // 5), 1), 0.0)
-                north = jnp.where(has_n, roll(edge(1, i, f * 5 + z % 5), 96 - 32 * (z // 5), 1), 0.0)
-                put(z, start, jnp.where(lane < 32, south, jnp.where(lane < 96, middle[i], north)))
+            at = f * 5 + z % 5
+            if first:
+                k, shift = (z, 32) if z < HZ else (z - HZ, -32)
+                south, north = edges(z, (rns[0, at], rns[1, at]))
+                put(z, 8, jnp.where(lane < 32, south, jnp.where(lane < 96, own(z), north)))
+                put(z, 16, roll(rpk[0, f * HZ + k], shift, 1))
+                put(z, 0, roll(rpk[1, f * HZ + k], shift, 1))
+            else:
+                for i, start in ((0, 16), (1, 0)):
+                    pieces = [rnc[side, i, at] for side in range(2)]
+                    pieces = [jnp.concatenate([p, blank] if i == 0 else [blank, p], axis=0) for p in pieces]
+                    south, north = edges(z, pieces)
+                    put(z, start, jnp.where(lane < 32, south, jnp.where(lane < 96, own(z)[start:start + 8], north)))
 
     own1 = [
         down_0(kappa[...]),
@@ -470,17 +474,11 @@
     def sea0(z):
         return (raw0[1, z] > 0.0).astype(F32)
 
-    lev0.faces(lambda z: raw0[0, z], lambda z: raw0[1, z], lambda z: raw0[2, z], sea0, UNROLL)
+    lev0.faces(lambda z: raw0[0, z], lambda z: raw0[1, z], lambda z: raw0[2, z], sea0, UNROLL, lambda z: raw0[3, z])
     lev0.clear_ends()
 
 
-    def first0(z):
-        c = lev0.g[z] * raw0[3, z]
-        lev0.c[z] = c
-        lev0.u[z + 1] = c
-
-    lev0.each(first0, UNROLL)
-    lev0.sweep(lev0.u, lev0.w, UNROLL)
+    lev0.sweep(lev0.c, lev0.w, UNROLL)
 
     def remain0(z, u, total):
         r = raw0[3, z] - (lev0.d[z] * u - total)
@@ -490,21 +488,39 @@
     b1 = down_0(t0[...])
 
     arrive(sent_p1)
-    for f in range(3):
-        def put1(z, start, x):
+
+    def put1(f):
+        def put(z, start, x):
             raw1[f, z, start:start + 8, :] = x
 
-        merge_1(f, lambda z: raw1[f, z, 8:16, :], p_rpk, p_rns, p_rnc, put1)
+        return put
 
     def sea_1(z):
         return (raw1[1, z] > 0.0).astype(F32)
 
-    lev1.faces(lambda z: raw1[0, z], lambda z: raw1[1, z], lambda z: raw1[2, z], sea_1, UNROLL)
-    lev1.clear_ends()
-    c1 = lev1.g[:, 8:16, :] * b1
+    for f in range(3):
+        merge_1(f, lambda z: raw1[f, z, 8:16, :], p_rpk, p_rns, p_rnc, put1(f), True)
+    middle = slice(8, 16)
+    c1 = []
+    for z in range(NZ):
+        s, lw, tw = sea_1(z), raw1[1, z], raw1[2, z, middle, :]
+        here = s[middle]
+        east = 0.5 * (lw * roll(s, -1, 0) + s * roll(lw, -1, 0))
+        north = 0.5 * (tw * roll(here, -1, 1) + here * roll(tw, -1, 1))
+        faces = roll(east, 1, 0)[middle] + east[middle] + roll(north, 1, 1) + north
+        for other in (z - 1, z + 1):
+            if 0 <= other < NZ:
+                faces = faces + here * sea_1(other)[middle]
+        c1.append(OMEGA / (here * raw1[0, z, middle, :] + faces + (1.0 - here)) * b1[z])
+    c1 = jnp.stack(c1)
     q1[...] = c1
     pack_1(c1, 0, b_pk, b_ns, b_nc)
     sent_b = send_1(b_pk, b_ns, b_nc, b_rpk, b_rns, b_rnc)
+
+    for f in range(3):
+        merge_1(f, lambda z: raw1[f, z], None, p_rns, p_rnc, put1(f), False)
+    lev1.faces(lambda z: raw1[0, z], lambda z: raw1[1, z], lambda z: raw1[2, z], sea_1, UNROLL)
+    lev1.clear_ends()
 
     edge_n = jnp.zeros((16, 128), F32)
     edge_s = jnp.zeros((16, 128), F32)
@@ -553,11 +569,11 @@
     sent_hz = send_z(h_blk, h_z)
 
     def put1c(z, start, x):
-        lev1.c[z, start:start + 8, :] = x
-        lev1.u[z + 1, start:start + 8, :] = x
-
-    merge_1(0, lambda z: q1[z], b_rpk, b_rns, b_rnc, put1c)
-    lev1.sweep(lev1.u, lev1.w, UNROLL)
+        lev1.c[z + 1, start:start + 8, :] = x
+
+    merge_1(0, lambda z: q1[z], b_rpk, b_rns, b_rnc, put1c, True)
+    merge_1(0, lambda z: lev1.c[z + 1], None, b_rns, b_rnc, put1c, False)
+    lev1.sweep(lev1.c, lev1.w, UNROLL)
 
     def remain1(z, r):
         q1[z] = r[8:16]
@@ -575,19 +591,19 @@
     sent_o = send_edges(o_ew, o_ns, o_rew, o_rns, o_rd)
     for s in range(7):
         piece = f_p if s == 3 else f_rp.at[s]
-        lev2.c[:, 4 * s:4 * s + 4, :] = piece[...]
-    lev2.c[:, 28:32, :] = jnp.zeros((HZ, 4, 128), F32)
-    lev2.start(UNROLL)
-    lev2.sweep(lev2.u, lev2.w, UNROLL)
+        lev2.c[1:HZ + 1, 4 * s:4 * s + 4, :] = piece[...]
+    lev2.c[1:HZ + 1, 28:32, :] = jnp.zeros((HZ, 4, 128), F32)
+    lev2.wrap(lev2.c)
+    lev2.sweep(lev2.c, lev2.w, UNROLL)
 
     def remain2(z, r):
         t4[z] = r
 
     lev2.remain(lev2.w, UNROLL, remain2)
 
-    lev3.c[...] = lev3.g[...] * down_2(t4[...])
-    lev3.start(UNROLL)
-    lev3.sweep(lev3.u, lev3.w, UNROLL)
+    lev3.c[1:HZ + 1] = lev3.g[...] * down_2(t4[...])
+    lev3.wrap(lev3.c)
+    lev3.sweep(lev3.c, lev3.w, UNROLL)
 
     def remain3(z, r):
         t3[z, 0:16, :] = r
@@ -623,26 +639,38 @@
 
     lev4.faces(lambda z: raw4[0, z], lambda z: raw4[1, z], lambda z: raw4[2, z], sea_4, UNROLL)
 
+    arrive(sent_o)
+
+    def put_rows0(z):
+        lev0.w[z + 1, 16:20, 0:128] = o_rew[0, z]
+        lev0.w[z + 1, 20:24, 0:128] = o_rew[1, z]
+
+    def put_side0(z, x):
+        lev0.w[z + 1, :, 128:256] = x
+
+    merge_edges(0, 0, o_rns, o_rd, put_rows0, put_side0)
     arrive(sent_kp)
     for z in range(HZ):
         for i in range(2):
             at = 8 * i + z if z < 8 else 16 + 2 * i + z - 8
-            lev4.c[z, pl.ds(i, 16, stride=2), :] = k_ev[pl.ds(at, 16, stride=24), :]
+            lev4.c[z + 1, pl.ds(i, 16, stride=2), :] = k_ev[pl.ds(at, 16, stride=24), :]
     for z in range(HZ):
-        lev4.c[z] = lev4.g[z] * lev4.c[z]
-    lev4.start(UNROLL)
+        lev4.c[z + 1] = lev4.g[z] * lev4.c[z + 1]
+    lev4.wrap(lev4.c)
+    lev4.sweep(lev4.c, lev4.u, UNROLL)
 
     def two(step, carry):
         lev4.sweep(lev4.u, lev4.w, UNROLL)
         lev4.sweep(lev4.w, lev4.u, UNROLL)
         return carry
 
-    lax.fori_loop(0, 7, two, 0)
-    middle = slice(8, 24)
-    for src, dst in ((lev4.u, lev4.w), (lev4.w, lev4.u)) * 2 + ((lev4.u, lev4.w),):
-        lev4.sweep(src, dst, UNROLL, middle)
-
-    up = mm(lev4.w[1:HZ + 1, 13:21, :].reshape(HZ * 8, 128), prolong_3()).reshape(HZ, 8, 128)
+    lax.fori_loop(0, 6, two, 0)
+    lev4.sweep(lev4.u, lev4.w, UNROLL)
+    centre = slice(8, 24)
+    for src, dst in ((lev4.w, lev4.u), (lev4.u, lev4.w)) * 2 + ((lev4.w, lev4.u),):
+        lev4.sweep(src, dst, UNROLL, centre)
+
+    up = mm(lev4.u[1:HZ + 1, 13:21, :].reshape(HZ * 8, 128), prolong_3()).reshape(HZ, 8, 128)
     for start in range(2):
         t3[:, pl.ds(start, 8, stride=2), :] = up
 
@@ -683,16 +711,6 @@
     lev1.sweep(lev1.w, lev1.u, UNROLL)
     lev1.sweep(lev1.u, lev1.w, UNROLL)
 
-    arrive(sent_o)
-
-    def put_rows0(z):
-        lev0.w[z + 1, 16:20, 0:128] = o_rew[0, z]
-        lev0.w[z + 1, 20:24, 0:128] = o_rew[1, z]
-
-    def put_side0(z, x):
-        lev0.w[z + 1, :, 128:256] = x
-
-    merge_edges(0, 0, o_rns, o_rd, put_rows0, put_side0)
     for z in range(NZ):
         t1[z, 0:8, :] = lev1.w[z + 1, 8:16, :]
         t1[z, 8:10, :] = lev1.w[z + 1, 16:18, :]
@@ -729,7 +747,7 @@
     def vmem(count):
         return pltpu.VMEM((count, rows, lanes), F32)
 
-    return [vmem(slabs), vmem(slabs), vmem(slabs + 1), vmem(slabs), vmem(slabs), vmem(slabs), vmem(slabs + 2), vmem(slabs + 2)]
+    return [vmem(slabs), vmem(slabs), vmem(slabs + 1), vmem(slabs), vmem(slabs), vmem(slabs + 2), vmem(slabs + 2), vmem(slabs + 2)]
 
 
 def shards(source, kappa_sq, lon_diff, lat_diff, sea_mask):

time: 53.3 us -> 53.3 us (level)
  no operation moved by 1% of the time
where the time goes in v3:
time: 53.3 us; the launch traced here: 53.2 us
  Pallas kernels  51.2 us (96%)
  local copies, waits for them, and re-layouts  1.33 us (2%)
  between operations  0.64 us (1%)
    pallas_call x1, Pallas kernels, shards(): pl.pallas_call(body, out_shape=(shape, shape), in_specs=[anywhere] * 5, o...  51.2 us
    unnamed x2, local copies, waits for them, and re-layouts  1.33 us

profile of v3, /device:TPU:1, one launch (start us, length us, event | category | flops | bytes accessed | tf_op | source)
XLA Modules:
  0.0 53.2 jit_solution(12153279565614016786)
XLA Ops:
  0.6 51.2 %shard_map.68 = (f32[20,16,128]{2,1,0:T(8,128)S(1)}, f32[20,16,128]{2,1,0:T(8,128)S(1)}) custom-call(f32[20,16,128]{2,1,0:T(8,128)} %source_in.1, f32[20,16,128]{2,1,0:T(8,128)} %kappa_in.1, f32[20,16,128]{2,1,0:T(8,128)} %lon_in.1, f32[20,16,128]{2,1,0:T(8,128)} %lat_in.1, s32[20,16,128]{2,1,0:T(8,128)} %mask_in.1), custom_call_target="tpu_custom_call" | custom-call | tf_op jit(solution)/shard_map/pallas_call | solution.py:781
  51.8 0.7 %copy.9 = f32[20,16,128]{2,1,0:T(8,128)} copy(f32[20,16,128]{2,1,0:T(8,128)S(1)} %get-tuple-element.4) | data formatting | bytes 327680
  52.5 0.7 %copy.10 = f32[20,16,128]{2,1,0:T(8,128)} copy(f32[20,16,128]{2,1,0:T(8,128)S(1)} %get-tuple-element.5) | data formatting | bytes 327680

commit v4 on v3

--- a/solution.py
+++ b/solution.py
@@ -10,7 +10,7 @@
 NTX = 32
 NTY = 16
 OMEGA = 0.8
-UNROLL = 20
+UNROLL = 5
 MESH = pl.DeviceIdType.MESH
 F32 = jnp.float32
 
@@ -83,6 +83,18 @@
         return (m == 32 + (rel >> 1)) & (rel < 132) & (rel >= -4)
 
     return one_hot((128, 256), hit)
+
+
+def spin(x, shift):
+    return pltpu.roll(x, shift, 1)
+
+
+def repeat(count, body, unroll=1):
+    def step(i, carry):
+        body(i)
+        return carry
+
+    lax.fori_loop(0, count, step, 0, unroll=unroll)
 
 
 class Level:
@@ -188,7 +200,7 @@
 def body(
     source_in, kappa_in, lon_in, lat_in, mask_in,
     sol, resid,
-    source, kappa, lon_diff, lat_diff, mask, in_sem,
+    source, mask, raw_in, own1, h_tmp, up0, in_sem,
     raw0, src0, l0, raw1, l1, raw2, l2, raw3, l3, raw4, l4, t0, t1, t2, t3, t4, q1,
     a_ew, a_ns, a_rew, a_rns, a_rd,
     b_pk, b_ns, b_nc, b_rpk, b_rns, b_rnc,
@@ -239,7 +251,7 @@
     fetched = [
         pltpu.make_async_copy(src, dst, in_sem.at[i])
         for i, (src, dst) in enumerate((
-            (mask_in, mask), (lon_in, lon_diff), (lat_in, lat_diff), (kappa_in, kappa), (source_in, source)
+            (mask_in, mask), (lon_in, raw_in.at[1]), (lat_in, raw_in.at[2]), (kappa_in, raw_in.at[0]), (source_in, source)
         ))
     ]
     for made in fetched:
@@ -257,28 +269,40 @@
 
     lane16 = iota((16, 128), 1)
     place = ((1, 0), (0, 0), (0, 60), (1, 60))
-    edge_n = [jnp.zeros((16, 128), F32)] * 4
-    edge_s = [jnp.zeros((16, 128), F32)] * 4
-    own0 = (
-        lambda z: kappa[z],
-        lambda z: mask[z].astype(F32) * lon_diff[z],
-        lambda z: mask[z].astype(F32) * lat_diff[z],
-        lambda z: source[z],
-    )
+    edge_n = [None] * 4
+    edge_s = [None] * 4
+
+    def own0(f, z):
+        if f == 3:
+            return source[z]
+        if f == 0:
+            return raw_in[0, z]
+        if f == 1:
+            raw_in[3, z] = mask[z].astype(F32)
+        return raw_in[3, z] * raw_in[f, z]
+
     for f, needed in ((1, (0, 1)), (2, (2,)), (0, (3,)), (3, (4,))):
         for i in needed:
             fetched[i].wait()
-        for z in range(NZ):
-            x = own0[f](z)
-            raw0[f, z, 0:16, 0:128] = x
-            a_ew[0, f * NZ + z] = x[0:2]
-            a_ew[1, f * NZ + z] = x[14:16]
-            if f == 1:
-                a_ew[0, 4 * NZ + z // 2, z % 2:z % 2 + 1] = x[2:3]
-                a_ew[1, 4 * NZ + z // 2, z % 2:z % 2 + 1] = x[13:14]
-            start = place[f][1] + 3 * z
-            edge_n[f] = jnp.where(lane16 >= start, roll(x, start - 125, 1), edge_n[f])
-            edge_s[f] = jnp.where(lane16 >= start, roll(x, start, 1), edge_s[f])
+
+        def prepare(pair, carry):
+            north, south = carry
+            for i in range(2):
+                z = 2 * pair + i
+                x = own0(f, z)
+                raw0[f, z, 0:16, 0:128] = x
+                a_ew[0, f * NZ + z] = x[0:2]
+                a_ew[1, f * NZ + z] = x[14:16]
+                if f == 1:
+                    a_ew[0, 4 * NZ + pair, i:i + 1] = x[2:3]
+                    a_ew[1, 4 * NZ + pair, i:i + 1] = x[13:14]
+                start = place[f][1] + 3 * z
+                north = jnp.where(lane16 >= start, spin(x, start + 3), north)
+                south = jnp.where(lane16 >= start, spin(x, start), south)
+            return north, south
+
+        blank16 = jnp.zeros((16, 128), F32)
+        edge_n[f], edge_s[f] = lax.fori_loop(0, HZ, prepare, (blank16, blank16), unroll=2)
     for pair, (f, g) in enumerate(((1, 2), (0, 3))):
         a_ns[0, pair] = jnp.where(lane16 < 60, edge_n[f], edge_n[g])
         a_ns[1, pair] = jnp.where(lane16 < 60, edge_s[f], edge_s[g])
@@ -296,23 +320,34 @@
 
     has_s, has_n = my > 0, my < NTY - 1
 
-    def merge_edges(f, base, rns, rd, put_rows, put_side):
+    def merge_edges(fields, rns, rd, put_rows, put_side):
         sub = iota((8, 128), 0)
-        south = jnp.concatenate([rns[0, f], jnp.where(sub < 4, rd[1, f], rd[0, f])], axis=0)
-        north = jnp.concatenate([rns[1, f], jnp.where(sub < 4, rd[3, f], rd[2, f])], axis=0)
         lane = iota((24, 128), 1)
-        south = jnp.where(has_s, south, 0.0)
-        north = jnp.where(has_n, north, 0.0)
-        for z in range(NZ):
-            put_rows(z)
-            start = base + 3 * z
-            side = jnp.where(lane < 3, roll(north, -start, 1), roll(south, 125 - start, 1))
-            put_side(z, jnp.where((lane < 3) | (lane >= 125), side, 0.0))
+        sides = []
+        for f, pair, base in fields:
+            south = jnp.concatenate([rns[0, pair], jnp.where(sub < 4, rd[1, pair], rd[0, pair])], axis=0)
+            north = jnp.concatenate([rns[1, pair], jnp.where(sub < 4, rd[3, pair], rd[2, pair])], axis=0)
+            sides.append((jnp.where(has_s, south, 0.0), jnp.where(has_n, north, 0.0)))
+
+        def two(half):
+            for i in range(2):
+                z = 2 * half + i
+                for (f, pair, base), (south, north) in zip(fields, sides):
+                    put_rows(f, z, half, i)
+                    start = base + 3 * z
+                    back = lax.rem(128 - start, 128)
+                    side = jnp.where(lane < 3, spin(north, back), spin(south, 125 - start))
+                    put_side(f, z, jnp.where((lane < 3) | (lane >= 125), side, 0.0))
+
+        repeat(HZ, two)
 
     sent_a = send_edges(a_ew, a_ns, a_rew, a_rns, a_rd)
-    for f in range(4):
-        for z in range(NZ):
+
+    def clear(z):
+        for f in range(4):
             raw0[f, z, 16:24, 0:128] = jnp.zeros((8, 128), F32)
+
+    repeat(NZ, clear, 4)
 
     m0 = restrict_0()
 
@@ -322,15 +357,18 @@
 
     def pack_1(x, f, pk, ns, nc):
         lane = iota((8, 128), 1)
-        for k in range(HZ):
-            pk[f * HZ + k] = jnp.where(lane < 64, roll(x[k], -32, 1), roll(x[k + HZ], 32, 1))
-        for k in range(5):
-            group = [x[k + 5 * j] for j in range(4)]
+
+        def step(k):
+            group = [x(k + 5 * j) for j in range(4)]
+            for j in range(2):
+                pk[f * HZ + 5 * j + k] = jnp.where(lane < 64, roll(group[j], -32, 1), roll(group[j + 2], 32, 1))
             for side, base in ((0, 64), (1, 32)):
                 edge = pack_edge(group, 32, base, 4)
                 ns[side, f * 5 + k] = edge
                 nc[side, 0, f * 5 + k] = edge[0:4]
                 nc[side, 1, f * 5 + k] = edge[4:8]
+
+        repeat(5, step)
 
     def send_1(pk, ns, nc, rpk, rns, rnc):
         made = [copy(nc.at[0, 1], rnc.at[0, 1], 1, 1)]
@@ -345,32 +383,45 @@
         lane = iota((8, 128), 1)
         blank = jnp.zeros((4, 128), F32)
 
-        def edges(z, pieces):
-            south = jnp.where(has_s, roll(pieces[0], -32 * (z // 5), 1), 0.0)
-            north = jnp.where(has_n, roll(pieces[1], 96 - 32 * (z // 5), 1), 0.0)
+        def edges(j, pieces):
+            south = jnp.where(has_s, roll(pieces[0], -32 * j, 1), 0.0)
+            north = jnp.where(has_n, roll(pieces[1], 96 - 32 * j, 1), 0.0)
             return south, north
 
-        for z in range(NZ):
-            at = f * 5 + z % 5
-            if first:
-                k, shift = (z, 32) if z < HZ else (z - HZ, -32)
-                south, north = edges(z, (rns[0, at], rns[1, at]))
-                put(z, 8, jnp.where(lane < 32, south, jnp.where(lane < 96, own(z), north)))
-                put(z, 16, roll(rpk[0, f * HZ + k], shift, 1))
-                put(z, 0, roll(rpk[1, f * HZ + k], shift, 1))
-            else:
-                for i, start in ((0, 16), (1, 0)):
-                    pieces = [rnc[side, i, at] for side in range(2)]
-                    pieces = [jnp.concatenate([p, blank] if i == 0 else [blank, p], axis=0) for p in pieces]
-                    south, north = edges(z, pieces)
-                    put(z, start, jnp.where(lane < 32, south, jnp.where(lane < 96, own(z)[start:start + 8], north)))
-
-    own1 = [
-        down_0(kappa[...]),
-        0.25 * down_0(lon_diff[...]),
-        0.25 * down_0(lat_diff[...]),
-        (down_0(mask[...].astype(F32)) > 0.0).astype(F32),
-    ]
+        def step(k):
+            at = f * 5 + k
+            for j in range(4):
+                z = k + 5 * j
+                if first:
+                    folded, shift = f * HZ + k + 5 * (j % 2), 32 if j < 2 else -32
+                    south, north = edges(j, (rns[0, at], rns[1, at]))
+                    put(z, 8, jnp.where(lane < 32, south, jnp.where(lane < 96, own(z), north)))
+                    put(z, 16, roll(rpk[0, folded], shift, 1))
+                    put(z, 0, roll(rpk[1, folded], shift, 1))
+                else:
+                    for i, start in ((0, 16), (1, 0)):
+                        pieces = [rnc[side, i, at] for side in range(2)]
+                        pieces = [jnp.concatenate([p, blank] if i == 0 else [blank, p], axis=0) for p in pieces]
+                        south, north = edges(j, pieces)
+                        put(z, start, jnp.where(lane < 32, south, jnp.where(lane < 96, own(z)[start:start + 8], north)))
+
+        repeat(5, step)
+
+    def coarsen_1(f):
+        own1[f] = down_0(raw_in[f])
+
+    repeat(4, coarsen_1)
+
+    def weigh_1(z):
+        sea = (own1[3, z] > 0.0).astype(F32)
+        own1[3, z] = sea
+        raw1[0, z, 8:16, :] = own1[0, z]
+        for f in (1, 2):
+            x = 0.25 * own1[f, z]
+            own1[f, z] = x
+            raw1[f, z, 8:16, :] = sea * x
+
+    repeat(NZ, weigh_1, 4)
 
     m1 = restrict_1()
 
@@ -379,21 +430,26 @@
         t2[...] = mm(pair, m1).reshape(HZ, 8, 128)
         return t2[:, pl.ds(0, 4, stride=2), :] + t2[:, pl.ds(1, 4, stride=2), :]
 
-    own2 = [
-        down_1(own1[0]),
-        0.25 * down_1(own1[1]),
-        0.25 * down_1(own1[2]),
-        (down_1(own1[3]) > 0.0).astype(F32),
-    ]
-    for f in range(4):
-        g_p[f * HZ:(f + 1) * HZ] = own2[f]
-        for k in range(5):
-            q_p[f * 5 + k] = own2[f][k] + roll(own2[f][k + 5], 32, 1)
+    def coarsen_2(f):
+        g_p[pl.ds(f * HZ, HZ)] = down_1(own1[f])
+
+    repeat(4, coarsen_2)
+
+    def finish_2(k):
+        for f in range(4):
+            pair = []
+            for z in (k, k + 5):
+                x = g_p[f * HZ + z]
+                x = x if f == 0 else (x > 0.0).astype(F32) if f == 3 else 0.25 * x
+                g_p[f * HZ + z] = x
+                pair.append(x)
+            q_p[f * 5 + k] = pair[0] + roll(pair[1], 32, 1)
+
+    repeat(5, finish_2)
     sent_q = [copy(q_p, q_rp.at[0], 0, 1), copy(q_p, q_rp.at[1], 0, -1)]
 
-    for f, x in enumerate((own1[0], own1[3] * own1[1], own1[3] * own1[2])):
-        pack_1(x, f, p_pk, p_ns, p_nc)
-        raw1[f, :, 8:16, :] = x
+    for f in range(3):
+        pack_1(lambda z: raw1[f, z, 8:16, :], f, p_pk, p_ns, p_nc)
     sent_p1 = send_1(p_pk, p_ns, p_nc, p_rpk, p_rns, p_rnc)
 
     def send_z(blk, slots):
@@ -443,32 +499,34 @@
         put(pl.ds(1, 16, stride=2), jnp.where(odd, roll(other, -1, 0), other))
 
     arrive(sent_a)
-    for f in range(4):
-        def put_rows(z):
-            raw0[f, z, 16:18, 0:128] = a_rew[0, f * NZ + z]
-            raw0[f, z, 22:24, 0:128] = a_rew[1, f * NZ + z]
-            if f == 1:
-                pick = slice(z % 2, z % 2 + 1)
-                raw0[f, z, 18:19, 0:128] = a_rew[0, 4 * NZ + z // 2, pick]
-                raw0[f, z, 21:22, 0:128] = a_rew[1, 4 * NZ + z // 2, pick]
-
-        def put_side(z, x):
-            raw0[f, z, :, 128:256] = x
-
-        merge_edges(place[f][0], place[f][1], a_rns, a_rd, put_rows, put_side)
+
+    def put_rows(f, z, half, i):
+        raw0[f, z, 16:18, 0:128] = a_rew[0, f * NZ + z]
+        raw0[f, z, 22:24, 0:128] = a_rew[1, f * NZ + z]
+        if f == 1:
+            raw0[f, z, 18:19, 0:128] = a_rew[0, 4 * NZ + half, i:i + 1]
+            raw0[f, z, 21:22, 0:128] = a_rew[1, 4 * NZ + half, i:i + 1]
+
+    def put_side(f, z, x):
+        raw0[f, z, :, 128:256] = x
+
+    merge_edges([(f,) + place[f] for f in range(4)], a_rns, a_rd, put_rows, put_side)
 
     def send_2(p, rp):
         return [copy(p, rp.at[3 - d], d, 0) for d in (3, -3, 2, -2, 1, -1)]
 
     arrive(sent_q)
     part = iota((4, 128), 1) & 63
-    for f in range(4):
-        for k in range(HZ):
-            south = roll(q_rp[0, f * 5 + k % 5], -32 if k < 5 else -64, 1)
-            north = roll(q_rp[1, f * 5 + k % 5], 32 if k < 5 else 0, 1)
-            south = jnp.where(has_s, south, 0.0)
-            north = jnp.where(has_n, north, 0.0)
-            g_p[f * HZ + k] = jnp.where(part < 16, south, jnp.where(part < 48, g_p[f * HZ + k], north))
+
+    def extend_2(k):
+        for f in range(4):
+            for j in range(2):
+                south = jnp.where(has_s, roll(q_rp[0, f * 5 + k], -32 - 32 * j, 1), 0.0)
+                north = jnp.where(has_n, roll(q_rp[1, f * 5 + k], 32 - 32 * j, 1), 0.0)
+                at = f * HZ + 5 * j + k
+                g_p[at] = jnp.where(part < 16, south, jnp.where(part < 48, g_p[at], north))
+
+    repeat(5, extend_2)
     sent_p2 = send_2(g_p, g_rp)
 
     def sea0(z):
@@ -485,7 +543,7 @@
         t0[z] = r[0:16, 0:128]
 
     lev0.stencil(lev0.w, UNROLL, remain0)
-    b1 = down_0(t0[...])
+    q1[...] = down_0(t0[...])
 
     arrive(sent_p1)
 
@@ -501,20 +559,21 @@
     for f in range(3):
         merge_1(f, lambda z: raw1[f, z, 8:16, :], p_rpk, p_rns, p_rnc, put1(f), True)
     middle = slice(8, 16)
-    c1 = []
-    for z in range(NZ):
+
+    def own_right(z, carry):
+        here, below = carry
         s, lw, tw = sea_1(z), raw1[1, z], raw1[2, z, middle, :]
-        here = s[middle]
         east = 0.5 * (lw * roll(s, -1, 0) + s * roll(lw, -1, 0))
         north = 0.5 * (tw * roll(here, -1, 1) + here * roll(tw, -1, 1))
-        faces = roll(east, 1, 0)[middle] + east[middle] + roll(north, 1, 1) + north
-        for other in (z - 1, z + 1):
-            if 0 <= other < NZ:
-                faces = faces + here * sea_1(other)[middle]
-        c1.append(OMEGA / (here * raw1[0, z, middle, :] + faces + (1.0 - here)) * b1[z])
-    c1 = jnp.stack(c1)
-    q1[...] = c1
-    pack_1(c1, 0, b_pk, b_ns, b_nc)
+        above = jnp.where(z < NZ - 1, sea_1(jnp.minimum(z + 1, NZ - 1))[middle], 0.0)
+        face_above = here * above
+        faces = roll(east, 1, 0)[middle] + east[middle] + roll(north, 1, 1) + north + below + face_above
+        q1[z] = OMEGA / (here * raw1[0, z, middle, :] + faces + (1.0 - here)) * q1[z]
+        return above, face_above
+
+    first = sea_1(0)[middle]
+    lax.fori_loop(0, NZ, own_right, (first, jnp.zeros_like(first)), unroll=UNROLL)
+    pack_1(lambda z: q1[z], 0, b_pk, b_ns, b_nc)
     sent_b = send_1(b_pk, b_ns, b_nc, b_rpk, b_rns, b_rnc)
 
     for f in range(3):
@@ -522,14 +581,16 @@
     lev1.faces(lambda z: raw1[0, z], lambda z: raw1[1, z], lambda z: raw1[2, z], sea_1, UNROLL)
     lev1.clear_ends()
 
-    edge_n = jnp.zeros((16, 128), F32)
-    edge_s = jnp.zeros((16, 128), F32)
-    for z in range(NZ):
+    def smooth_edges(z, carry):
+        north, south = carry
         x = lev0.w[z + 1, 0:16, 0:128]
         o_ew[0, z] = x[0:4]
         o_ew[1, z] = x[12:16]
-        edge_n = jnp.where(lane16 >= 3 * z, roll(x, 3 * z - 125, 1), edge_n)
-        edge_s = jnp.where(lane16 >= 3 * z, roll(x, 3 * z, 1), edge_s)
+        north = jnp.where(lane16 >= 3 * z, spin(x, 3 * z + 3), north)
+        south = jnp.where(lane16 >= 3 * z, spin(x, 3 * z), south)
+        return north, south
+
+    edge_n, edge_s = lax.fori_loop(0, NZ, smooth_edges, (blank16, blank16), unroll=4)
     o_ns[0, 0] = edge_n
     o_ns[1, 0] = edge_s
 
@@ -539,18 +600,26 @@
         pair = jnp.concatenate([x[0:HZ], x[HZ:NZ]], axis=2).reshape(HZ * 16, 256)
         return jnp.sum(mm(pair, mall).reshape(HZ, 16, 128), axis=1)
 
-    sea4 = (down_all(mask[...].astype(F32)) > 0.0).astype(F32)
-    h_blk[0:10, :] = down_all(kappa[...])
-    h_blk[10:20, :] = sea4 * (down_all(lon_diff[...]) * (1.0 / 256))
-    h_blk[20:30, :] = sea4 * (down_all(lat_diff[...]) * (1.0 / 256))
+    def coarsen_all(f):
+        h_tmp[f] = down_all(raw_in[f])
+
+    repeat(4, coarsen_all)
+    sea4 = (h_tmp[3] > 0.0).astype(F32)
+    h_blk[0:10, :] = h_tmp[0]
+    h_blk[10:20, :] = sea4 * h_tmp[1] * (1.0 / 256)
+    h_blk[20:30, :] = sea4 * h_tmp[2] * (1.0 / 256)
     h_blk[30:32, :] = jnp.zeros((2, 128), F32)
 
     arrive(sent_p2)
-    for f in range(4):
-        for s in range(7):
-            piece = g_p if s == 3 else g_rp.at[s]
-            raw2[f, :, 4 * s:4 * s + 4, :] = piece[f * HZ:(f + 1) * HZ]
-        raw2[f, :, 28:32, :] = jnp.zeros((HZ, 4, 128), F32)
+
+    def window_2(k):
+        for f in range(4):
+            for s in range(7):
+                piece = g_p if s == 3 else g_rp.at[s]
+                raw2[f, k, 4 * s:4 * s + 4, :] = piece[f * HZ + k]
+            raw2[f, k, 28:32, :] = jnp.zeros((4, 128), F32)
+
+    repeat(HZ, window_2)
     lev2.faces(lambda z: raw2[0, z], lambda z: raw2[1, z], lambda z: raw2[2, z], lambda z: raw2[3, z], UNROLL)
 
     m2 = restrict_2()
@@ -559,10 +628,17 @@
         t3[...] = mm(x.reshape(HZ * 32, 128), m2).reshape(HZ, 32, 128)
         return t3[:, pl.ds(0, 16, stride=2), :] + t3[:, pl.ds(1, 16, stride=2), :]
 
-    raw3[0] = down_2(raw2[0])
-    raw3[1] = 0.25 * down_2(raw2[1])
-    raw3[2] = 0.25 * down_2(raw2[2])
-    raw3[3] = (down_2(raw2[3]) > 0.0).astype(F32)
+    def coarsen_3(f):
+        raw3[f] = down_2(raw2[f])
+
+    repeat(4, coarsen_3)
+
+    def finish_3(k):
+        for f in (1, 2):
+            raw3[f, k] = 0.25 * raw3[f, k]
+        raw3[3, k] = (raw3[3, k] > 0.0).astype(F32)
+
+    repeat(HZ, finish_3, 5)
     lev3.faces(lambda z: raw3[0, z], lambda z: raw3[1, z], lambda z: raw3[2, z], lambda z: raw3[3, z], UNROLL)
 
     arrive(sent_b)
@@ -641,14 +717,14 @@
 
     arrive(sent_o)
 
-    def put_rows0(z):
+    def put_rows0(f, z, half, i):
         lev0.w[z + 1, 16:20, 0:128] = o_rew[0, z]
         lev0.w[z + 1, 20:24, 0:128] = o_rew[1, z]
 
-    def put_side0(z, x):
+    def put_side0(f, z, x):
         lev0.w[z + 1, :, 128:256] = x
 
-    merge_edges(0, 0, o_rns, o_rd, put_rows0, put_side0)
+    merge_edges([(0, 0, 0)], o_rns, o_rd, put_rows0, put_side0)
     arrive(sent_kp)
     for z in range(HZ):
         for i in range(2):
@@ -660,15 +736,21 @@
     lev4.sweep(lev4.c, lev4.u, UNROLL)
 
     def two(step, carry):
-        lev4.sweep(lev4.u, lev4.w, UNROLL)
-        lev4.sweep(lev4.w, lev4.u, UNROLL)
+        lev4.sweep(lev4.u, lev4.w, HZ)
+        lev4.sweep(lev4.w, lev4.u, HZ)
         return carry
 
     lax.fori_loop(0, 6, two, 0)
     lev4.sweep(lev4.u, lev4.w, UNROLL)
     centre = slice(8, 24)
-    for src, dst in ((lev4.w, lev4.u), (lev4.u, lev4.w)) * 2 + ((lev4.w, lev4.u),):
-        lev4.sweep(src, dst, UNROLL, centre)
+    lev4.sweep(lev4.w, lev4.u, HZ, centre)
+
+    def two_centre(step, carry):
+        lev4.sweep(lev4.u, lev4.w, HZ, centre)
+        lev4.sweep(lev4.w, lev4.u, HZ, centre)
+        return carry
+
+    lax.fori_loop(0, 2, two_centre, 0)
 
     up = mm(lev4.u[1:HZ + 1, 13:21, :].reshape(HZ * 8, 128), prolong_3()).reshape(HZ, 8, 128)
     for start in range(2):
@@ -696,13 +778,14 @@
 
     t3[:, 0:16, :] = lev2.w[1:HZ + 1, 8:24, :]
     up = mm(t3[:, 0:16, :].reshape(HZ * 16, 128), prolong_1()).reshape(HZ, 16, 256)
-    for start in range(2):
-        t1[0:HZ, :, :] = up[:, :, 0:128]
-        t1[HZ:NZ, :, :] = up[:, :, 128:256]
-    for z in range(NZ):
+    t1[0:HZ, :, :] = up[:, :, 0:128]
+    t1[HZ:NZ, :, :] = up[:, :, 128:256]
+
+    def spread1(z):
         for start in range(2):
-            q = pl.ds(start, 12, stride=2)
-            raw1[0, z, q, :] = t1[z, 0:12, :]
+            raw1[0, z, pl.ds(start, 12, stride=2), :] = t1[z, 0:12, :]
+
+    repeat(NZ, spread1, 4)
 
     def add1(z):
         lev1.w[z + 1] = lev1.w[z + 1] + raw1[0, z]
@@ -711,17 +794,22 @@
     lev1.sweep(lev1.w, lev1.u, UNROLL)
     lev1.sweep(lev1.u, lev1.w, UNROLL)
 
-    for z in range(NZ):
+    def gather0(z):
         t1[z, 0:8, :] = lev1.w[z + 1, 8:16, :]
         t1[z, 8:10, :] = lev1.w[z + 1, 16:18, :]
         t1[z, 10:12, :] = lev1.w[z + 1, 6:8, :]
         t1[z, 12:16, :] = jnp.zeros((4, 128), F32)
-    up = mm(t1[...].reshape(NZ * 16, 128), prolong_0()).reshape(NZ, 16, 256)
-    for z in range(NZ):
+
+    repeat(NZ, gather0, 4)
+    up0[...] = mm(t1[...].reshape(NZ * 16, 128), prolong_0()).reshape(NZ, 16, 256)
+
+    def spread0(z):
         for half in range(2):
-            part = up[z, 0:12, 128 * half:128 * half + 128]
+            part = up0[z, 0:12, 128 * half:128 * half + 128]
             for start in range(2):
                 raw1[half, z, pl.ds(start, 12, stride=2), :] = part
+
+    repeat(NZ, spread0, 4)
 
     def add0(z):
         for half in range(2):
@@ -755,8 +843,8 @@
         return pltpu.VMEM(shape, F32)
 
     scratch = [
-        vmem(NZ, 16, 128), vmem(NZ, 16, 128), vmem(NZ, 16, 128), vmem(NZ, 16, 128),
-        pltpu.VMEM((NZ, 16, 128), jnp.int32), pltpu.SemaphoreType.DMA((5,)),
+        vmem(NZ, 16, 128), pltpu.VMEM((NZ, 16, 128), jnp.int32),
+        vmem(4, NZ, 16, 128), vmem(4, NZ, 8, 128), vmem(4, HZ, 128), vmem(NZ, 16, 256), pltpu.SemaphoreType.DMA((5,)),
         vmem(4, NZ, 24, 256), vmem(8, 128), level_scratch(NZ, 24, 256),
         vmem(3, NZ, 24, 128), level_scratch(NZ, 24, 128),
         vmem(4, HZ, 32, 128), level_scratch(HZ, 32, 128),

time: 53.3 us -> 61.6 us (1.16)
  Pallas kernels: 51.2 us -> 59.5 us
    pallas_call x1, Pallas kernels: 51.2 us -> 59.5 us  [shards(): pl.pallas_call(body, out_shape=(shape, shape), in_specs=[anywhere] * 5, o...]
where the time goes in v4:
time: 61.6 us; the launch traced here: 61.5 us
  Pallas kernels  59.5 us (97%)
  local copies, waits for them, and re-layouts  1.33 us (2%)
  between operations  0.64 us (1%)
    pallas_call x1, Pallas kernels, shards(): pl.pallas_call(body, out_shape=(shape, shape), in_specs=[anywhere] * 5, o...  59.5 us
    unnamed x2, local copies, waits for them, and re-layouts  1.33 us

profile of v4, /device:TPU:1, one launch (start us, length us, event | category | flops | bytes accessed | tf_op | source)
XLA Modules:
  0.0 61.5 jit_solution(2997388314926624055)
XLA Ops:
  0.6 59.5 %shard_map.68 = (f32[20,16,128]{2,1,0:T(8,128)S(1)}, f32[20,16,128]{2,1,0:T(8,128)S(1)}) custom-call(f32[20,16,128]{2,1,0:T(8,128)} %source_in.1, f32[20,16,128]{2,1,0:T(8,128)} %kappa_in.1, f32[20,16,128]{2,1,0:T(8,128)} %lon_in.1, f32[20,16,128]{2,1,0:T(8,128)} %lat_in.1, s32[20,16,128]{2,1,0:T(8,128)} %mask_in.1), custom_call_target="tpu_custom_call" | custom-call | tf_op jit(solution)/shard_map/pallas_call | solution.py:869
  60.1 0.7 %copy.9 = f32[20,16,128]{2,1,0:T(8,128)} copy(f32[20,16,128]{2,1,0:T(8,128)S(1)} %get-tuple-element.4) | data formatting | bytes 327680
  60.8 0.7 %copy.10 = f32[20,16,128]{2,1,0:T(8,128)} copy(f32[20,16,128]{2,1,0:T(8,128)S(1)} %get-tuple-element.5) | data formatting | bytes 327680

commit v5 on v3

--- a/solution.py
+++ b/solution.py
@@ -7,6 +7,7 @@
 
 NZ = 20
 HZ = 10
+QZ = 5
 NTX = 32
 NTY = 16
 OMEGA = 0.8
@@ -66,7 +67,11 @@
 
 
 def prolong_3():
-    return one_hot((128, 128), lambda m, n: m == (n & 64) + 16 + ((n & 63) >> 1))
+    def hit(m, n):
+        q = n & 63
+        return (m == (n & 64) + ((n & 128) >> 2) + 4 + (q >> 1)) & (q < 56)
+
+    return one_hot((128, 256), hit)
 
 
 def prolong_2():
@@ -86,9 +91,9 @@
 
 
 class Level:
-    def __init__(self, slabs, folded, refs):
+    def __init__(self, slabs, seam, refs):
         self.slabs = slabs
-        self.folded = folded
+        self.seam = seam
         self.e, self.n, self.v, self.g, self.d, self.c, self.u, self.w = refs
 
     def each(self, body, unroll):
@@ -99,12 +104,12 @@
         lax.fori_loop(0, self.slabs, step, 0, unroll=min(unroll, self.slabs))
 
     def wrap(self, ref, rows=slice(None)):
-        if self.folded:
-            ref[0, rows] = roll(ref[self.slabs, rows], 64, 1)
-            ref[self.slabs + 1, rows] = roll(ref[1, rows], 64, 1)
+        if self.seam:
+            ref[0, rows] = roll(ref[self.slabs, rows], self.seam, 1)
+            ref[self.slabs + 1, rows] = roll(ref[1, rows], -self.seam, 1)
 
     def clear_ends(self):
-        if not self.folded:
+        if not self.seam:
             for ref in (self.c, self.u, self.w):
                 ref[0] = jnp.zeros_like(ref[0])
                 ref[self.slabs + 1] = jnp.zeros_like(ref[0])
@@ -112,7 +117,7 @@
     def faces(self, kap, lond, latd, sea, unroll, right=None):
         top = self.slabs - 1
         first = sea(0)
-        if self.folded:
+        if self.seam:
             low = iota(self.v.shape[1:], 1) < 64
             face_top = jnp.where(low, sea(top) * roll(first, 64, 1), 0.0)
             face_first = roll(face_top, 64, 1)
@@ -147,7 +152,7 @@
         s, face_below = lax.fori_loop(0, top, step, (first, face_first), unroll=min(unroll, top))
         slab(top, s, face_below, face_top)
 
-    def stencil(self, src, unroll, use, rows=slice(None)):
+    def stencil(self, src, unroll, use, rows=slice(None), first=0):
         def step(z, carry):
             below, u, face_below = carry
             above = src[z + 2, rows]
@@ -164,17 +169,32 @@
             ))
             return u, above, face_above
 
-        lax.fori_loop(0, self.slabs, step, (src[0, rows], src[1, rows], self.v[0, rows]), unroll=min(unroll, self.slabs))
-
-    def sweep(self, src, dst, unroll, rows=slice(None)):
+        def start(z):
+            return src[z, rows], src[z + 1, rows], self.v[z, rows]
+
+        if self.seam:
+            for i in range(self.slabs):
+                z = (first + i) % self.slabs
+                carry = step(z, start(z) if i == 0 or z == 0 else carry)
+        else:
+            lax.fori_loop(0, self.slabs, step, start(0), unroll=min(unroll, self.slabs))
+
+    def sweep(self, src, dst, unroll, rows=slice(None), first=0):
         def use(z, u, total):
-            dst[z + 1, rows] = (1.0 - OMEGA) * u + self.c[z + 1, rows] + self.g[z, rows] * total
-
-        self.stencil(src, unroll, use, rows)
-        self.wrap(dst, rows)
-
-    def remain(self, src, unroll, put):
-        self.stencil(src, unroll, lambda z, u, total: put(z, self.d[z] * (1.25 * self.c[z + 1] - u) + total))
+            new = (1.0 - OMEGA) * u + self.c[z + 1, rows] + self.g[z, rows] * total
+            dst[z + 1, rows] = new
+            if self.seam and z == 0:
+                dst[self.slabs + 1, rows] = roll(new, -self.seam, 1)
+            if self.seam and z == self.slabs - 1:
+                dst[0, rows] = roll(new, self.seam, 1)
+
+        self.stencil(src, unroll, use, rows, first)
+
+    def remain(self, src, unroll, put, first=0):
+        def use(z, u, total):
+            put(z, self.d[z] * (1.25 * self.c[z + 1] - u) + total)
+
+        self.stencil(src, unroll, use, first=first)
 
 
 def pack_edge(slabs, width, base, count):
@@ -189,7 +209,7 @@
     source_in, kappa_in, lon_in, lat_in, mask_in,
     sol, resid,
     source, kappa, lon_diff, lat_diff, mask, in_sem,
-    raw0, src0, l0, raw1, l1, raw2, l2, raw3, l3, raw4, l4, t0, t1, t2, t3, t4, q1,
+    raw0, src0, l0, raw1, l1, raw2, l2, raw3, l3, raw4, l4, l5, t0, t1, t2, t3, t4, q1,
     a_ew, a_ns, a_rew, a_rns, a_rd,
     b_pk, b_ns, b_nc, b_rpk, b_rns, b_rnc,
     f_p, f_rp,
@@ -230,11 +250,12 @@
         for made in copies:
             made.wait_recv()
 
-    lev0 = Level(NZ, False, l0)
-    lev1 = Level(NZ, False, l1)
-    lev2 = Level(HZ, True, l2)
-    lev3 = Level(HZ, True, l3)
-    lev4 = Level(HZ, True, l4)
+    lev0 = Level(NZ, 0, l0)
+    lev1 = Level(NZ, 0, l1)
+    lev2 = Level(HZ, 64, l2)
+    lev3 = Level(HZ, 64, l3)
+    lev4 = Level(HZ, 64, l4)
+    lev5 = Level(QZ, 32, l5)
 
     fetched = [
         pltpu.make_async_copy(src, dst, in_sem.at[i])
@@ -594,21 +615,21 @@
         lev2.c[1:HZ + 1, 4 * s:4 * s + 4, :] = piece[...]
     lev2.c[1:HZ + 1, 28:32, :] = jnp.zeros((HZ, 4, 128), F32)
     lev2.wrap(lev2.c)
-    lev2.sweep(lev2.c, lev2.w, UNROLL)
+    lev2.sweep(lev2.c, lev2.w, UNROLL, first=1)
 
     def remain2(z, r):
         t4[z] = r
 
-    lev2.remain(lev2.w, UNROLL, remain2)
+    lev2.remain(lev2.w, UNROLL, remain2, 2)
 
     lev3.c[1:HZ + 1] = lev3.g[...] * down_2(t4[...])
     lev3.wrap(lev3.c)
-    lev3.sweep(lev3.c, lev3.w, UNROLL)
+    lev3.sweep(lev3.c, lev3.w, UNROLL, first=1)
 
     def remain3(z, r):
         t3[z, 0:16, :] = r
 
-    lev3.remain(lev3.w, UNROLL, remain3)
+    lev3.remain(lev3.w, UNROLL, remain3, 2)
     m3 = restrict_3()
     t3[:, 0:16, :] = mm(t3[:, 0:16, :].reshape(HZ * 16, 128), m3).reshape(HZ, 16, 128)
     for z in range(8):
@@ -638,6 +659,17 @@
         return (raw4[1, z] > 0.0).astype(F32)
 
     lev4.faces(lambda z: raw4[0, z], lambda z: raw4[1, z], lambda z: raw4[2, z], sea_4, UNROLL)
+    group = iota((32, 128), 1) & 32
+
+    def fold(lower, upper):
+        return jnp.where(group == 0, roll(lower, -12, 1), roll(upper, 20, 1))
+
+    for k in range(QZ):
+        lev5.e[k] = fold(lev4.e[k], lev4.e[k + QZ])
+        lev5.n[k] = fold(lev4.n[k], lev4.n[k + QZ])
+        lev5.g[k] = fold(lev4.g[k], lev4.g[k + QZ])
+        lev5.v[k + 1] = fold(lev4.v[k + 1], lev4.v[k + QZ + 1])
+    lev5.v[0] = roll(lev5.v[QZ], 32, 1)
 
     arrive(sent_o)
 
@@ -657,30 +689,36 @@
     for z in range(HZ):
         lev4.c[z + 1] = lev4.g[z] * lev4.c[z + 1]
     lev4.wrap(lev4.c)
-    lev4.sweep(lev4.c, lev4.u, UNROLL)
-
-    def two(step, carry):
-        lev4.sweep(lev4.u, lev4.w, UNROLL)
-        lev4.sweep(lev4.w, lev4.u, UNROLL)
+    for k in range(QZ):
+        lev5.c[k + 1] = fold(lev4.c[k + 1], lev4.c[k + QZ + 1])
+    lev4.sweep(lev4.c, lev4.w, HZ, first=1)
+
+    def four(step, carry):
+        for i in range(2):
+            lev4.sweep(lev4.w, lev4.u, HZ, first=2 + 2 * i)
+            lev4.sweep(lev4.u, lev4.w, HZ, first=3 + 2 * i)
         return carry
 
-    lax.fori_loop(0, 6, two, 0)
-    lev4.sweep(lev4.u, lev4.w, UNROLL)
-    centre = slice(8, 24)
-    for src, dst in ((lev4.w, lev4.u), (lev4.u, lev4.w)) * 2 + ((lev4.w, lev4.u),):
-        lev4.sweep(src, dst, UNROLL, centre)
-
-    up = mm(lev4.u[1:HZ + 1, 13:21, :].reshape(HZ * 8, 128), prolong_3()).reshape(HZ, 8, 128)
+    lax.fori_loop(0, 2, four, 0)
+    for k in range(QZ):
+        lev5.u[k + 1] = fold(lev4.w[k + 1], lev4.w[k + QZ + 1])
+    lev5.wrap(lev5.u)
+    for i in range(10):
+        src, dst = (lev5.u, lev5.w) if i % 2 == 0 else (lev5.w, lev5.u)
+        lev5.sweep(src, dst, QZ, slice(None) if i < 5 else slice(8, 24), first=(i + 1) % QZ)
+
+    up = mm(lev5.u[1:QZ + 1, 13:21, :].reshape(QZ * 8, 128), prolong_3()).reshape(QZ, 8, 256)
     for start in range(2):
-        t3[:, pl.ds(start, 8, stride=2), :] = up
+        t3[0:QZ, pl.ds(start, 8, stride=2), :] = up[:, :, 0:128]
+        t3[QZ:HZ, pl.ds(start, 8, stride=2), :] = up[:, :, 128:256]
 
     def add3(z):
         lev3.w[z + 1] = lev3.w[z + 1] + t3[z, 0:16, :]
 
     lev3.each(add3, UNROLL)
     lev3.wrap(lev3.w)
-    lev3.sweep(lev3.w, lev3.u, UNROLL)
-    lev3.sweep(lev3.u, lev3.w, UNROLL)
+    lev3.sweep(lev3.w, lev3.u, UNROLL, first=1)
+    lev3.sweep(lev3.u, lev3.w, UNROLL, first=2)
 
     up = mm(lev3.w[1:HZ + 1].reshape(HZ * 16, 128), prolong_2()).reshape(HZ, 16, 128)
     for start in range(2):
@@ -691,8 +729,8 @@
 
     lev2.each(add2, UNROLL)
     lev2.wrap(lev2.w)
-    lev2.sweep(lev2.w, lev2.u, UNROLL)
-    lev2.sweep(lev2.u, lev2.w, UNROLL)
+    lev2.sweep(lev2.w, lev2.u, UNROLL, first=1)
+    lev2.sweep(lev2.u, lev2.w, UNROLL, first=2)
 
     t3[:, 0:16, :] = lev2.w[1:HZ + 1, 8:24, :]
     up = mm(t3[:, 0:16, :].reshape(HZ * 16, 128), prolong_1()).reshape(HZ, 16, 256)
@@ -761,7 +799,7 @@
         vmem(3, NZ, 24, 128), level_scratch(NZ, 24, 128),
         vmem(4, HZ, 32, 128), level_scratch(HZ, 32, 128),
         vmem(4, HZ, 16, 128), level_scratch(HZ, 16, 128),
-        vmem(3, HZ, 32, 128), level_scratch(HZ, 32, 128),
+        vmem(3, HZ, 32, 128), level_scratch(HZ, 32, 128), level_scratch(QZ, 32, 128),
         vmem(NZ, 16, 128), vmem(NZ, 16, 128), vmem(HZ, 8, 128), vmem(HZ, 32, 128), vmem(HZ, 32, 128), vmem(NZ, 8, 128),
         vmem(2, 4 * NZ + HZ, 2, 128), vmem(2, 2, 16, 128), vmem(2, 4 * NZ + HZ, 2, 128), vmem(2, 2, 16, 128), vmem(4, 2, 8, 128),
         vmem(HZ, 8, 128), vmem(2, 5, 8, 128), vmem(2, 2, 5, 4, 128),

time: 53.3 us -> 53.7 us (level)
  no operation moved by 1% of the time
where the time goes in v5:
time: 53.7 us; the launch traced here: 53.6 us
  Pallas kernels  51.6 us (96%)
  local copies, waits for them, and re-layouts  1.33 us (2%)
  between operations  0.64 us (1%)
    pallas_call x1, Pallas kernels, shards(): pl.pallas_call(body, out_shape=(shape, shape), in_specs=[anywhere] * 5, o...  51.6 us
    unnamed x2, local copies, waits for them, and re-layouts  1.33 us

profile of v5, /device:TPU:1, one launch (start us, length us, event | category | flops | bytes accessed | tf_op | source)
XLA Modules:
  0.0 53.6 jit_solution(8113261675276826055)
XLA Ops:
  0.6 51.6 %shard_map.68 = (f32[20,16,128]{2,1,0:T(8,128)S(1)}, f32[20,16,128]{2,1,0:T(8,128)S(1)}) custom-call(f32[20,16,128]{2,1,0:T(8,128)} %source_in.1, f32[20,16,128]{2,1,0:T(8,128)} %kappa_in.1, f32[20,16,128]{2,1,0:T(8,128)} %lon_in.1, f32[20,16,128]{2,1,0:T(8,128)} %lat_in.1, s32[20,16,128]{2,1,0:T(8,128)} %mask_in.1), custom_call_target="tpu_custom_call" | custom-call | tf_op jit(solution)/shard_map/pallas_call | solution.py:819
  52.2 0.7 %copy.9 = f32[20,16,128]{2,1,0:T(8,128)} copy(f32[20,16,128]{2,1,0:T(8,128)S(1)} %get-tuple-element.4) | data formatting | bytes 327680
  52.9 0.7 %copy.10 = f32[20,16,128]{2,1,0:T(8,128)} copy(f32[20,16,128]{2,1,0:T(8,128)S(1)} %get-tuple-element.5) | data formatting | bytes 327680

commit v6 on v5

--- a/solution.py
+++ b/solution.py
@@ -62,8 +62,12 @@
     return one_hot((128, 128), hit, 0.25)
 
 
-def restrict_all():
-    return one_hot((256, 128), lambda n, m: m == ((n & 128) >> 1) + 24 + ((n & 127) >> 4), 1.0 / 256)
+def restrict_24():
+    def hit(n, m):
+        q = n & 63
+        return (m == (n & 64) + 20 + (q >> 2)) & (q >= 16) & (q < 48)
+
+    return one_hot((128, 128), hit, 1.0 / 16)
 
 
 def prolong_3():
@@ -213,7 +217,7 @@
     a_ew, a_ns, a_rew, a_rns, a_rd,
     b_pk, b_ns, b_nc, b_rpk, b_rns, b_rnc,
     f_p, f_rp,
-    k_blk, k_z, k_ev,
+    k_rows, k_blk, k_z, k_ev,
     p_pk, p_ns, p_nc, p_rpk, p_rns, p_rnc, q_p, q_rp, g_p, g_rp, h_blk, h_z, h_ev, h_od,
     o_ew, o_ns, o_rew, o_rns, o_rd,
     send_sem, recv_sem,
@@ -337,9 +341,11 @@
 
     m0 = restrict_0()
 
+    def pair_rows(ref, count):
+        return ref[:, pl.ds(0, count, stride=2), :] + ref[:, pl.ds(1, count, stride=2), :]
+
     def down_0(x):
-        t1[...] = mm(x.reshape(NZ * 16, 128), m0).reshape(NZ, 16, 128)
-        return t1[:, pl.ds(0, 8, stride=2), :] + t1[:, pl.ds(1, 8, stride=2), :]
+        return mm(x.reshape(NZ * 8, 128), m0).reshape(NZ, 8, 128)
 
     def pack_1(x, f, pk, ns, nc):
         lane = iota((8, 128), 1)
@@ -362,35 +368,30 @@
         made += [copy(ns.at[0], rns.at[0], 0, 1), copy(ns.at[1], rns.at[1], 0, -1)]
         return made
 
-    def merge_1(f, own, rpk, rns, rnc, put, first):
+    def merge_1(f, own, rpk, rns, rnc, put):
         lane = iota((8, 128), 1)
         blank = jnp.zeros((4, 128), F32)
 
-        def edges(z, pieces):
-            south = jnp.where(has_s, roll(pieces[0], -32 * (z // 5), 1), 0.0)
-            north = jnp.where(has_n, roll(pieces[1], 96 - 32 * (z // 5), 1), 0.0)
-            return south, north
+        def edge(side, i, at):
+            if i == 0:
+                return rns[side, at]
+            if i == 1:
+                return jnp.concatenate([rnc[side, 0, at], blank], axis=0)
+            return jnp.concatenate([blank, rnc[side, 1, at]], axis=0)
 
         for z in range(NZ):
-            at = f * 5 + z % 5
-            if first:
-                k, shift = (z, 32) if z < HZ else (z - HZ, -32)
-                south, north = edges(z, (rns[0, at], rns[1, at]))
-                put(z, 8, jnp.where(lane < 32, south, jnp.where(lane < 96, own(z), north)))
-                put(z, 16, roll(rpk[0, f * HZ + k], shift, 1))
-                put(z, 0, roll(rpk[1, f * HZ + k], shift, 1))
-            else:
-                for i, start in ((0, 16), (1, 0)):
-                    pieces = [rnc[side, i, at] for side in range(2)]
-                    pieces = [jnp.concatenate([p, blank] if i == 0 else [blank, p], axis=0) for p in pieces]
-                    south, north = edges(z, pieces)
-                    put(z, start, jnp.where(lane < 32, south, jnp.where(lane < 96, own(z)[start:start + 8], north)))
+            k, shift = (z, 32) if z < HZ else (z - HZ, -32)
+            middle = (own(z), roll(rpk[0, f * HZ + k], shift, 1), roll(rpk[1, f * HZ + k], shift, 1))
+            for i, start in ((0, 8), (1, 16), (2, 0)):
+                south = jnp.where(has_s, roll(edge(0, i, f * 5 + z % 5), -32 * (z // 5), 1), 0.0)
+                north = jnp.where(has_n, roll(edge(1, i, f * 5 + z % 5), 96 - 32 * (z // 5), 1), 0.0)
+                put(z, start, jnp.where(lane < 32, south, jnp.where(lane < 96, middle[i], north)))
 
     own1 = [
-        down_0(kappa[...]),
-        0.25 * down_0(lon_diff[...]),
-        0.25 * down_0(lat_diff[...]),
-        (down_0(mask[...].astype(F32)) > 0.0).astype(F32),
+        down_0(pair_rows(kappa, 8)),
+        0.25 * down_0(pair_rows(lon_diff, 8)),
+        0.25 * down_0(pair_rows(lat_diff, 8)),
+        (down_0(pair_rows(mask, 8).astype(F32)) > 0.0).astype(F32),
     ]
 
     m1 = restrict_1()
@@ -400,12 +401,13 @@
         t2[...] = mm(pair, m1).reshape(HZ, 8, 128)
         return t2[:, pl.ds(0, 4, stride=2), :] + t2[:, pl.ds(1, 4, stride=2), :]
 
-    own2 = [
-        down_1(own1[0]),
-        0.25 * down_1(own1[1]),
-        0.25 * down_1(own1[2]),
-        (down_1(own1[3]) > 0.0).astype(F32),
-    ]
+    own2 = []
+    rows4 = []
+    for f, scale in enumerate((1.0, 0.25, 0.25, 1.0)):
+        x = down_1(own1[f])
+        own2.append((x > 0.0).astype(F32) if f == 3 else scale * x)
+        flat = t2.reshape(HZ * 8, 128)
+        rows4.append(sum(flat[pl.ds(i, HZ, stride=8), :] for i in range(8)))
     for f in range(4):
         g_p[f * HZ:(f + 1) * HZ] = own2[f]
         for k in range(5):
@@ -506,42 +508,24 @@
         t0[z] = r[0:16, 0:128]
 
     lev0.stencil(lev0.w, UNROLL, remain0)
-    b1 = down_0(t0[...])
+    b1 = down_0(pair_rows(t0, 8))
 
     arrive(sent_p1)
-
-    def put1(f):
-        def put(z, start, x):
-            raw1[f, z, start:start + 8, :] = x
-
-        return put
 
     def sea_1(z):
         return (raw1[1, z] > 0.0).astype(F32)
 
     for f in range(3):
-        merge_1(f, lambda z: raw1[f, z, 8:16, :], p_rpk, p_rns, p_rnc, put1(f), True)
-    middle = slice(8, 16)
-    c1 = []
-    for z in range(NZ):
-        s, lw, tw = sea_1(z), raw1[1, z], raw1[2, z, middle, :]
-        here = s[middle]
-        east = 0.5 * (lw * roll(s, -1, 0) + s * roll(lw, -1, 0))
-        north = 0.5 * (tw * roll(here, -1, 1) + here * roll(tw, -1, 1))
-        faces = roll(east, 1, 0)[middle] + east[middle] + roll(north, 1, 1) + north
-        for other in (z - 1, z + 1):
-            if 0 <= other < NZ:
-                faces = faces + here * sea_1(other)[middle]
-        c1.append(OMEGA / (here * raw1[0, z, middle, :] + faces + (1.0 - here)) * b1[z])
-    c1 = jnp.stack(c1)
+        def put1(z, start, x):
+            raw1[f, z, start:start + 8, :] = x
+
+        merge_1(f, lambda z: raw1[f, z, 8:16, :], p_rpk, p_rns, p_rnc, put1)
+    lev1.faces(lambda z: raw1[0, z], lambda z: raw1[1, z], lambda z: raw1[2, z], sea_1, UNROLL)
+    lev1.clear_ends()
+    c1 = lev1.g[:, 8:16, :] * b1
     q1[...] = c1
     pack_1(c1, 0, b_pk, b_ns, b_nc)
     sent_b = send_1(b_pk, b_ns, b_nc, b_rpk, b_rns, b_rnc)
-
-    for f in range(3):
-        merge_1(f, lambda z: raw1[f, z], None, p_rns, p_rnc, put1(f), False)
-    lev1.faces(lambda z: raw1[0, z], lambda z: raw1[1, z], lambda z: raw1[2, z], sea_1, UNROLL)
-    lev1.clear_ends()
 
     edge_n = jnp.zeros((16, 128), F32)
     edge_s = jnp.zeros((16, 128), F32)
@@ -554,16 +538,12 @@
     o_ns[0, 0] = edge_n
     o_ns[1, 0] = edge_s
 
-    mall = restrict_all()
-
-    def down_all(x):
-        pair = jnp.concatenate([x[0:HZ], x[HZ:NZ]], axis=2).reshape(HZ * 16, 256)
-        return jnp.sum(mm(pair, mall).reshape(HZ, 16, 128), axis=1)
-
-    sea4 = (down_all(mask[...].astype(F32)) > 0.0).astype(F32)
-    h_blk[0:10, :] = down_all(kappa[...])
-    h_blk[10:20, :] = sea4 * (down_all(lon_diff[...]) * (1.0 / 256))
-    h_blk[20:30, :] = sea4 * (down_all(lat_diff[...]) * (1.0 / 256))
+    padding = jnp.zeros((16 - HZ, 128), F32)
+    every = mm(jnp.concatenate([part for x in rows4 for part in (x, padding)], axis=0), restrict_24())
+    sea4 = (every[48:58] > 0.0).astype(F32)
+    h_blk[0:10, :] = every[0:10]
+    h_blk[10:20, :] = sea4 * every[16:26] * (1.0 / 64)
+    h_blk[20:30, :] = sea4 * every[32:42] * (1.0 / 64)
     h_blk[30:32, :] = jnp.zeros((2, 128), F32)
 
     arrive(sent_p2)
@@ -576,14 +556,13 @@
 
     m2 = restrict_2()
 
-    def down_2(x):
-        t3[...] = mm(x.reshape(HZ * 32, 128), m2).reshape(HZ, 32, 128)
-        return t3[:, pl.ds(0, 16, stride=2), :] + t3[:, pl.ds(1, 16, stride=2), :]
-
-    raw3[0] = down_2(raw2[0])
-    raw3[1] = 0.25 * down_2(raw2[1])
-    raw3[2] = 0.25 * down_2(raw2[2])
-    raw3[3] = (down_2(raw2[3]) > 0.0).astype(F32)
+    def down_2(ref):
+        return mm(pair_rows(ref, 16).reshape(HZ * 16, 128), m2).reshape(HZ, 16, 128)
+
+    raw3[0] = down_2(raw2.at[0])
+    raw3[1] = 0.25 * down_2(raw2.at[1])
+    raw3[2] = 0.25 * down_2(raw2.at[2])
+    raw3[3] = (down_2(raw2.at[3]) > 0.0).astype(F32)
     lev3.faces(lambda z: raw3[0, z], lambda z: raw3[1, z], lambda z: raw3[2, z], lambda z: raw3[3, z], UNROLL)
 
     arrive(sent_b)
@@ -592,8 +571,7 @@
     def put1c(z, start, x):
         lev1.c[z + 1, start:start + 8, :] = x
 
-    merge_1(0, lambda z: q1[z], b_rpk, b_rns, b_rnc, put1c, True)
-    merge_1(0, lambda z: lev1.c[z + 1], None, b_rns, b_rnc, put1c, False)
+    merge_1(0, lambda z: q1[z], b_rpk, b_rns, b_rnc, put1c)
     lev1.sweep(lev1.c, lev1.w, UNROLL)
 
     def remain1(z, r):
@@ -622,23 +600,19 @@
 
     lev2.remain(lev2.w, UNROLL, remain2, 2)
 
-    lev3.c[1:HZ + 1] = lev3.g[...] * down_2(t4[...])
+    lev3.c[1:HZ + 1] = lev3.g[...] * down_2(t4)
     lev3.wrap(lev3.c)
     lev3.sweep(lev3.c, lev3.w, UNROLL, first=1)
 
     def remain3(z, r):
-        t3[z, 0:16, :] = r
+        k_rows[16 * z:16 * z + 16, :] = r
 
     lev3.remain(lev3.w, UNROLL, remain3, 2)
-    m3 = restrict_3()
-    t3[:, 0:16, :] = mm(t3[:, 0:16, :].reshape(HZ * 16, 128), m3).reshape(HZ, 16, 128)
-    for z in range(8):
-        row = t3[z, 6:7, :] + t3[z, 7:8, :] + roll(t3[z, 8:9, :] + t3[z, 9:10, :], 8, 1)
-        if z < 4:
-            at = 6 if z < 2 else 8
-            last = t3[8 + z % 2, at:at + 1, :] + t3[8 + z % 2, at + 1:at + 2, :]
-            row = row + roll(last, 16, 1)
-        k_blk[z:z + 1, :] = row
+    own_cell = k_rows[pl.ds(6, HZ, stride=16), :] + k_rows[pl.ds(7, HZ, stride=16), :]
+    east_cell = k_rows[pl.ds(8, HZ, stride=16), :] + k_rows[pl.ds(9, HZ, stride=16), :]
+    cells = mm(jnp.concatenate([own_cell, padding, east_cell, padding], axis=0), restrict_3())
+    last = jnp.concatenate([cells[8:10], cells[24:26], jnp.zeros((4, 128), F32)], axis=0)
+    k_blk[...] = cells[0:8] + roll(cells[16:24], 8, 1) + roll(last, 16, 1)
     sent_kz = send_z(k_blk, k_z)
 
     arrive(sent_hp)
@@ -805,7 +779,7 @@
         vmem(HZ, 8, 128), vmem(2, 5, 8, 128), vmem(2, 2, 5, 4, 128),
         vmem(2, HZ, 8, 128), vmem(2, 5, 8, 128), vmem(2, 2, 5, 4, 128),
         vmem(HZ, 4, 128), vmem(7, HZ, 4, 128),
-        vmem(8, 128), vmem(7, 8, 128), vmem(16 * 24, 128),
+        vmem(HZ * 16, 128), vmem(8, 128), vmem(7, 8, 128), vmem(16 * 24, 128),
         vmem(3 * HZ, 8, 128), vmem(2, 15, 8, 128), vmem(2, 2, 15, 4, 128),
         vmem(2, 3 * HZ, 8, 128), vmem(2, 15, 8, 128), vmem(2, 2, 15, 4, 128),
         vmem(20, 4, 128), vmem(2, 20, 4, 128),

time: 53.7 us -> 53.6 us (level)
  no operation moved by 1% of the time
where the time goes in v6:
time: 53.6 us; the launch traced here: 53.4 us
  Pallas kernels  51.5 us (96%)
  local copies, waits for them, and re-layouts  1.33 us (2%)
  between operations  0.64 us (1%)
    pallas_call x1, Pallas kernels, shards(): pl.pallas_call(body, out_shape=(shape, shape), in_specs=[anywhere] * 5, o...  51.5 us
    unnamed x2, local copies, waits for them, and re-layouts  1.33 us

profile of v6, /device:TPU:1, one launch (start us, length us, event | category | flops | bytes accessed | tf_op | source)
XLA Modules:
  0.0 53.4 jit_solution(12231499951698565486)
XLA Ops:
  0.6 51.5 %shard_map.68 = (f32[20,16,128]{2,1,0:T(8,128)S(1)}, f32[20,16,128]{2,1,0:T(8,128)S(1)}) custom-call(f32[20,16,128]{2,1,0:T(8,128)} %source_in.1, f32[20,16,128]{2,1,0:T(8,128)} %kappa_in.1, f32[20,16,128]{2,1,0:T(8,128)} %lon_in.1, f32[20,16,128]{2,1,0:T(8,128)} %lat_in.1, s32[20,16,128]{2,1,0:T(8,128)} %mask_in.1), custom_call_target="tpu_custom_call" | custom-call | tf_op jit(solution)/shard_map/pallas_call | solution.py:793
  52.1 0.7 %copy.9 = f32[20,16,128]{2,1,0:T(8,128)} copy(f32[20,16,128]{2,1,0:T(8,128)S(1)} %get-tuple-element.4) | data formatting | bytes 327680
  52.8 0.7 %copy.10 = f32[20,16,128]{2,1,0:T(8,128)} copy(f32[20,16,128]{2,1,0:T(8,128)S(1)} %get-tuple-element.5) | data formatting | bytes 327680

commit v7 on v6

--- a/solution.py
+++ b/solution.py
@@ -527,6 +527,51 @@
     pack_1(c1, 0, b_pk, b_ns, b_nc)
     sent_b = send_1(b_pk, b_ns, b_nc, b_rpk, b_rns, b_rnc)
 
+    padding = jnp.zeros((16 - HZ, 128), F32)
+    every = mm(jnp.concatenate([part for x in rows4 for part in (x, padding)], axis=0), restrict_24())
+    sea4 = (every[48:58] > 0.0).astype(F32)
+    h_blk[0:10, :] = every[0:10]
+    h_blk[10:20, :] = sea4 * every[16:26] * (1.0 / 64)
+    h_blk[20:30, :] = sea4 * every[32:42] * (1.0 / 64)
+    h_blk[30:32, :] = jnp.zeros((2, 128), F32)
+
+    arrive(sent_p2)
+    for f in range(4):
+        for s in range(7):
+            piece = g_p if s == 3 else g_rp.at[s]
+            raw2[f, :, 4 * s:4 * s + 4, :] = piece[f * HZ:(f + 1) * HZ]
+        raw2[f, :, 28:32, :] = jnp.zeros((HZ, 4, 128), F32)
+    lev2.faces(lambda z: raw2[0, z], lambda z: raw2[1, z], lambda z: raw2[2, z], lambda z: raw2[3, z], UNROLL)
+
+    arrive(sent_b)
+    sent_hz = send_z(h_blk, h_z)
+
+    def put1c(z, start, x):
+        lev1.c[z + 1, start:start + 8, :] = x
+
+    merge_1(0, lambda z: q1[z], b_rpk, b_rns, b_rnc, put1c)
+    lev1.sweep(lev1.c, lev1.w, UNROLL)
+
+    def remain1(z, r):
+        q1[z] = r[8:16]
+
+    lev1.remain(lev1.w, UNROLL, remain1)
+    b2 = down_1(q1[...])
+
+    f_p[...] = lev2.g[:, 12:16, :] * b2
+    sent_c = send_2(f_p, f_rp)
+
+    m2 = restrict_2()
+
+    def down_2(ref):
+        return mm(pair_rows(ref, 16).reshape(HZ * 16, 128), m2).reshape(HZ, 16, 128)
+
+    raw3[0] = down_2(raw2.at[0])
+    raw3[1] = 0.25 * down_2(raw2.at[1])
+    raw3[2] = 0.25 * down_2(raw2.at[2])
+    raw3[3] = (down_2(raw2.at[3]) > 0.0).astype(F32)
+    lev3.faces(lambda z: raw3[0, z], lambda z: raw3[1, z], lambda z: raw3[2, z], lambda z: raw3[3, z], UNROLL)
+
     edge_n = jnp.zeros((16, 128), F32)
     edge_s = jnp.zeros((16, 128), F32)
     for z in range(NZ):
@@ -538,56 +583,12 @@
     o_ns[0, 0] = edge_n
     o_ns[1, 0] = edge_s
 
-    padding = jnp.zeros((16 - HZ, 128), F32)
-    every = mm(jnp.concatenate([part for x in rows4 for part in (x, padding)], axis=0), restrict_24())
-    sea4 = (every[48:58] > 0.0).astype(F32)
-    h_blk[0:10, :] = every[0:10]
-    h_blk[10:20, :] = sea4 * every[16:26] * (1.0 / 64)
-    h_blk[20:30, :] = sea4 * every[32:42] * (1.0 / 64)
-    h_blk[30:32, :] = jnp.zeros((2, 128), F32)
-
-    arrive(sent_p2)
-    for f in range(4):
-        for s in range(7):
-            piece = g_p if s == 3 else g_rp.at[s]
-            raw2[f, :, 4 * s:4 * s + 4, :] = piece[f * HZ:(f + 1) * HZ]
-        raw2[f, :, 28:32, :] = jnp.zeros((HZ, 4, 128), F32)
-    lev2.faces(lambda z: raw2[0, z], lambda z: raw2[1, z], lambda z: raw2[2, z], lambda z: raw2[3, z], UNROLL)
-
-    m2 = restrict_2()
-
-    def down_2(ref):
-        return mm(pair_rows(ref, 16).reshape(HZ * 16, 128), m2).reshape(HZ, 16, 128)
-
-    raw3[0] = down_2(raw2.at[0])
-    raw3[1] = 0.25 * down_2(raw2.at[1])
-    raw3[2] = 0.25 * down_2(raw2.at[2])
-    raw3[3] = (down_2(raw2.at[3]) > 0.0).astype(F32)
-    lev3.faces(lambda z: raw3[0, z], lambda z: raw3[1, z], lambda z: raw3[2, z], lambda z: raw3[3, z], UNROLL)
-
-    arrive(sent_b)
-    sent_hz = send_z(h_blk, h_z)
-
-    def put1c(z, start, x):
-        lev1.c[z + 1, start:start + 8, :] = x
-
-    merge_1(0, lambda z: q1[z], b_rpk, b_rns, b_rnc, put1c)
-    lev1.sweep(lev1.c, lev1.w, UNROLL)
-
-    def remain1(z, r):
-        q1[z] = r[8:16]
-
-    lev1.remain(lev1.w, UNROLL, remain1)
-    b2 = down_1(q1[...])
-
-    f_p[...] = lev2.g[:, 12:16, :] * b2
-    sent_c = send_2(f_p, f_rp)
-
     arrive(sent_hz)
     row_h = window_row(h_z, 32)
+
     arrive(sent_c)
+    sent_o = send_edges(o_ew, o_ns, o_rew, o_rns, o_rd)
     sent_hp = send_plane(row_h, h_ev, 32)
-    sent_o = send_edges(o_ew, o_ns, o_rew, o_rns, o_rd)
     for s in range(7):
         piece = f_p if s == 3 else f_rp.at[s]
         lev2.c[1:HZ + 1, 4 * s:4 * s + 4, :] = piece[...]
@@ -615,6 +616,16 @@
     k_blk[...] = cells[0:8] + roll(cells[16:24], 8, 1) + roll(last, 16, 1)
     sent_kz = send_z(k_blk, k_z)
 
+    arrive(sent_o)
+
+    def put_rows0(z):
+        lev0.w[z + 1, 16:20, 0:128] = o_rew[0, z]
+        lev0.w[z + 1, 20:24, 0:128] = o_rew[1, z]
+
+    def put_side0(z, x):
+        lev0.w[z + 1, :, 128:256] = x
+
+    merge_edges(0, 0, o_rns, o_rd, put_rows0, put_side0)
     arrive(sent_hp)
     sent_hs = send_sibling(h_ev, h_od)
 
@@ -645,16 +656,6 @@
         lev5.v[k + 1] = fold(lev4.v[k + 1], lev4.v[k + QZ + 1])
     lev5.v[0] = roll(lev5.v[QZ], 32, 1)
 
-    arrive(sent_o)
-
-    def put_rows0(z):
-        lev0.w[z + 1, 16:20, 0:128] = o_rew[0, z]
-        lev0.w[z + 1, 20:24, 0:128] = o_rew[1, z]
-
-    def put_side0(z, x):
-        lev0.w[z + 1, :, 128:256] = x
-
-    merge_edges(0, 0, o_rns, o_rd, put_rows0, put_side0)
     arrive(sent_kp)
     for z in range(HZ):
         for i in range(2):

time: 53.6 us -> 53.8 us (level)
  no operation moved by 1% of the time
where the time goes in v7:
time: 53.8 us; the launch traced here: 53.6 us
  Pallas kernels  51.6 us (96%)
  local copies, waits for them, and re-layouts  1.33 us (2%)
  between operations  0.64 us (1%)
    pallas_call x1, Pallas kernels, shards(): pl.pallas_call(body, out_shape=(shape, shape), in_specs=[anywhere] * 5, o...  51.6 us
    unnamed x2, local copies, waits for them, and re-layouts  1.33 us

profile of v7, /device:TPU:1, one launch (start us, length us, event | category | flops | bytes accessed | tf_op | source)
XLA Modules:
  0.0 53.6 jit_solution(12258861264071026101)
XLA Ops:
  0.6 51.6 %shard_map.68 = (f32[20,16,128]{2,1,0:T(8,128)S(1)}, f32[20,16,128]{2,1,0:T(8,128)S(1)}) custom-call(f32[20,16,128]{2,1,0:T(8,128)} %source_in.1, f32[20,16,128]{2,1,0:T(8,128)} %kappa_in.1, f32[20,16,128]{2,1,0:T(8,128)} %lon_in.1, f32[20,16,128]{2,1,0:T(8,128)} %lat_in.1, s32[20,16,128]{2,1,0:T(8,128)} %mask_in.1), custom_call_target="tpu_custom_call" | custom-call | tf_op jit(solution)/shard_map/pallas_call | solution.py:794
  52.3 0.7 %copy.9 = f32[20,16,128]{2,1,0:T(8,128)} copy(f32[20,16,128]{2,1,0:T(8,128)S(1)} %get-tuple-element.4) | data formatting | bytes 327680
  53.0 0.7 %copy.10 = f32[20,16,128]{2,1,0:T(8,128)} copy(f32[20,16,128]{2,1,0:T(8,128)S(1)} %get-tuple-element.5) | data formatting | bytes 327680

commit v8 on v7

--- a/solution.py
+++ b/solution.py
@@ -439,7 +439,17 @@
             for i in range(3):
                 pick = (part >= 24 + 8 * i) & (part < 32 + 8 * i)
                 out[i] = out[i] + roll(jnp.where(pick, block, 0.0), 8 * (s - 3 - i), 1)
-        return jnp.concatenate(out, axis=0)
+        sub = iota((8, 128), 0)
+        lane = iota((8, 128), 1)
+        spare = (((lane + 11) & 63) < 13)
+        rows = []
+        for i in range(2):
+            ends = jnp.where(sub < 4, out[2][2 * i:2 * i + 1], out[2][2 * i + 1:2 * i + 2])
+            pieces = roll(ends, 50, 1)
+            for c in range(1, 4):
+                pieces = jnp.where((sub & 3) == c, roll(ends, 50 - 13 * c, 1), pieces)
+            rows.append(jnp.where(spare, pieces, out[i]))
+        return jnp.concatenate(rows, axis=0)
 
     def send_plane(row, ev, count):
         own = pl.ds(8 * count, count)
@@ -465,21 +475,6 @@
         other = od[pl.ds(index, 16, stride=count), :]
         put(pl.ds(1, 16, stride=2), jnp.where(odd, roll(other, -1, 0), other))
 
-    arrive(sent_a)
-    for f in range(4):
-        def put_rows(z):
-            raw0[f, z, 16:18, 0:128] = a_rew[0, f * NZ + z]
-            raw0[f, z, 22:24, 0:128] = a_rew[1, f * NZ + z]
-            if f == 1:
-                pick = slice(z % 2, z % 2 + 1)
-                raw0[f, z, 18:19, 0:128] = a_rew[0, 4 * NZ + z // 2, pick]
-                raw0[f, z, 21:22, 0:128] = a_rew[1, 4 * NZ + z // 2, pick]
-
-        def put_side(z, x):
-            raw0[f, z, :, 128:256] = x
-
-        merge_edges(place[f][0], place[f][1], a_rns, a_rd, put_rows, put_side)
-
     def send_2(p, rp):
         return [copy(p, rp.at[3 - d], d, 0) for d in (3, -3, 2, -2, 1, -1)]
 
@@ -494,6 +489,21 @@
             g_p[f * HZ + k] = jnp.where(part < 16, south, jnp.where(part < 48, g_p[f * HZ + k], north))
     sent_p2 = send_2(g_p, g_rp)
 
+    arrive(sent_a)
+    for f in range(4):
+        def put_rows(z):
+            raw0[f, z, 16:18, 0:128] = a_rew[0, f * NZ + z]
+            raw0[f, z, 22:24, 0:128] = a_rew[1, f * NZ + z]
+            if f == 1:
+                pick = slice(z % 2, z % 2 + 1)
+                raw0[f, z, 18:19, 0:128] = a_rew[0, 4 * NZ + z // 2, pick]
+                raw0[f, z, 21:22, 0:128] = a_rew[1, 4 * NZ + z // 2, pick]
+
+        def put_side(z, x):
+            raw0[f, z, :, 128:256] = x
+
+        merge_edges(place[f][0], place[f][1], a_rns, a_rd, put_rows, put_side)
+
     def sea0(z):
         return (raw0[1, z] > 0.0).astype(F32)
 
@@ -630,7 +640,7 @@
     sent_hs = send_sibling(h_ev, h_od)
 
     arrive(sent_kz)
-    sent_kp = send_plane(folded_window_row(k_z), k_ev, 24)
+    sent_kp = send_plane(folded_window_row(k_z), k_ev, 16)
 
     arrive(sent_hs)
     for f in range(3):
@@ -657,10 +667,17 @@
     lev5.v[0] = roll(lev5.v[QZ], 32, 1)
 
     arrive(sent_kp)
-    for z in range(HZ):
-        for i in range(2):
-            at = 8 * i + z if z < 8 else 16 + 2 * i + z - 8
-            lev4.c[z + 1, pl.ds(i, 16, stride=2), :] = k_ev[pl.ds(at, 16, stride=24), :]
+    place13 = ((iota((16, 128), 1) & 63) - 3)
+    for i in range(2):
+        rows = pl.ds(i, 16, stride=2)
+        for z in range(8):
+            lev4.c[z + 1, rows, :] = k_ev[pl.ds(8 * i + z, 16, stride=16), :]
+        for z in range(8, HZ):
+            found = jnp.zeros((16, 128), F32)
+            for c in range(4):
+                piece = roll(k_ev[pl.ds(8 * i + 4 * (z - 8) + c, 16, stride=16), :], 13 * c - 50, 1)
+                found = jnp.where((place13 >= 13 * c) & (place13 < 13 * c + 13), piece, found)
+            lev4.c[z + 1, rows, :] = found
     for z in range(HZ):
         lev4.c[z + 1] = lev4.g[z] * lev4.c[z + 1]
     lev4.wrap(lev4.c)
@@ -780,7 +797,7 @@
         vmem(HZ, 8, 128), vmem(2, 5, 8, 128), vmem(2, 2, 5, 4, 128),
         vmem(2, HZ, 8, 128), vmem(2, 5, 8, 128), vmem(2, 2, 5, 4, 128),
         vmem(HZ, 4, 128), vmem(7, HZ, 4, 128),
-        vmem(HZ * 16, 128), vmem(8, 128), vmem(7, 8, 128), vmem(16 * 24, 128),
+        vmem(HZ * 16, 128), vmem(8, 128), vmem(7, 8, 128), vmem(16 * 16, 128),
         vmem(3 * HZ, 8, 128), vmem(2, 15, 8, 128), vmem(2, 2, 15, 4, 128),
         vmem(2, 3 * HZ, 8, 128), vmem(2, 15, 8, 128), vmem(2, 2, 15, 4, 128),
         vmem(20, 4, 128), vmem(2, 20, 4, 128),

time: 53.8 us -> 53.8 us (level)
  no operation moved by 1% of the time
where the time goes in v8:
time: 53.8 us; the launch traced here: 53.7 us
  Pallas kernels  51.7 us (96%)
  local copies, waits for them, and re-layouts  1.33 us (2%)
  between operations  0.64 us (1%)
    pallas_call x1, Pallas kernels, shards(): pl.pallas_call(body, out_shape=(shape, shape), in_specs=[anywhere] * 5, o...  51.7 us
    unnamed x2, local copies, waits for them, and re-layouts  1.33 us

profile of v8, /device:TPU:1, one launch (start us, length us, event | category | flops | bytes accessed | tf_op | source)
XLA Modules:
  0.0 53.7 jit_solution(3471620831656356883)
XLA Ops:
  0.6 51.7 %shard_map.68 = (f32[20,16,128]{2,1,0:T(8,128)S(1)}, f32[20,16,128]{2,1,0:T(8,128)S(1)}) custom-call(f32[20,16,128]{2,1,0:T(8,128)} %source_in.1, f32[20,16,128]{2,1,0:T(8,128)} %kappa_in.1, f32[20,16,128]{2,1,0:T(8,128)} %lon_in.1, f32[20,16,128]{2,1,0:T(8,128)} %lat_in.1, s32[20,16,128]{2,1,0:T(8,128)} %mask_in.1), custom_call_target="tpu_custom_call" | custom-call | tf_op jit(solution)/shard_map/pallas_call | solution.py:811
  52.3 0.7 %copy.9 = f32[20,16,128]{2,1,0:T(8,128)} copy(f32[20,16,128]{2,1,0:T(8,128)S(1)} %get-tuple-element.4) | data formatting | bytes 327680
  53.0 0.7 %copy.10 = f32[20,16,128]{2,1,0:T(8,128)} copy(f32[20,16,128]{2,1,0:T(8,128)S(1)} %get-tuple-element.5) | data formatting | bytes 327680

commit v9 on v8

--- a/solution.py
+++ b/solution.py
@@ -423,6 +423,15 @@
         slots[3] = blk[...]
         return [copy(blk, slots.at[3 - d], 0, d) for d in (3, -3, 2, -2, 1, -1)]
 
+    padding = jnp.zeros((16 - HZ, 128), F32)
+    every = mm(jnp.concatenate([part for x in rows4 for part in (x, padding)], axis=0), restrict_24())
+    sea4 = (every[48:58] > 0.0).astype(F32)
+    h_blk[0:10, :] = every[0:10]
+    h_blk[10:20, :] = sea4 * every[16:26] * (1.0 / 64)
+    h_blk[20:30, :] = sea4 * every[32:42] * (1.0 / 64)
+    h_blk[30:32, :] = jnp.zeros((2, 128), F32)
+    sent_hz = send_z(h_blk, h_z)
+
     def window_row(slots, count):
         row = jnp.zeros((count, 128), F32)
         for s in range(7):
@@ -537,13 +546,8 @@
     pack_1(c1, 0, b_pk, b_ns, b_nc)
     sent_b = send_1(b_pk, b_ns, b_nc, b_rpk, b_rns, b_rnc)
 
-    padding = jnp.zeros((16 - HZ, 128), F32)
-    every = mm(jnp.concatenate([part for x in rows4 for part in (x, padding)], axis=0), restrict_24())
-    sea4 = (every[48:58] > 0.0).astype(F32)
-    h_blk[0:10, :] = every[0:10]
-    h_blk[10:20, :] = sea4 * every[16:26] * (1.0 / 64)
-    h_blk[20:30, :] = sea4 * every[32:42] * (1.0 / 64)
-    h_blk[30:32, :] = jnp.zeros((2, 128), F32)
+    arrive(sent_hz)
+    sent_hp = send_plane(window_row(h_z, 32), h_ev, 32)
 
     arrive(sent_p2)
     for f in range(4):
@@ -554,7 +558,6 @@
     lev2.faces(lambda z: raw2[0, z], lambda z: raw2[1, z], lambda z: raw2[2, z], lambda z: raw2[3, z], UNROLL)
 
     arrive(sent_b)
-    sent_hz = send_z(h_blk, h_z)
 
     def put1c(z, start, x):
         lev1.c[z + 1, start:start + 8, :] = x
@@ -593,12 +596,9 @@
     o_ns[0, 0] = edge_n
     o_ns[1, 0] = edge_s
 
-    arrive(sent_hz)
-    row_h = window_row(h_z, 32)
 
     arrive(sent_c)
     sent_o = send_edges(o_ew, o_ns, o_rew, o_rns, o_rd)
-    sent_hp = send_plane(row_h, h_ev, 32)
     for s in range(7):
         piece = f_p if s == 3 else f_rp.at[s]
         lev2.c[1:HZ + 1, 4 * s:4 * s + 4, :] = piece[...]
@@ -626,6 +626,9 @@
     k_blk[...] = cells[0:8] + roll(cells[16:24], 8, 1) + roll(last, 16, 1)
     sent_kz = send_z(k_blk, k_z)
 
+    arrive(sent_hp)
+    sent_hs = send_sibling(h_ev, h_od)
+
     arrive(sent_o)
 
     def put_rows0(z):
@@ -636,9 +639,6 @@
         lev0.w[z + 1, :, 128:256] = x
 
     merge_edges(0, 0, o_rns, o_rd, put_rows0, put_side0)
-    arrive(sent_hp)
-    sent_hs = send_sibling(h_ev, h_od)
-
     arrive(sent_kz)
     sent_kp = send_plane(folded_window_row(k_z), k_ev, 16)
 

time: 53.8 us -> 54 us (level)
  no operation moved by 1% of the time
where the time goes in v9:
time: 54 us; the launch traced here: 53.8 us
  Pallas kernels  51.8 us (96%)
  local copies, waits for them, and re-layouts  1.33 us (2%)
  between operations  0.64 us (1%)
    pallas_call x1, Pallas kernels, shards(): pl.pallas_call(body, out_shape=(shape, shape), in_specs=[anywhere] * 5, o...  51.8 us
    unnamed x2, local copies, waits for them, and re-layouts  1.33 us

profile of v9, /device:TPU:1, one launch (start us, length us, event | category | flops | bytes accessed | tf_op | source)
XLA Modules:
  0.0 53.8 jit_solution(14337792545925600504)
XLA Ops:
  0.6 51.8 %shard_map.68 = (f32[20,16,128]{2,1,0:T(8,128)S(1)}, f32[20,16,128]{2,1,0:T(8,128)S(1)}) custom-call(f32[20,16,128]{2,1,0:T(8,128)} %source_in.1, f32[20,16,128]{2,1,0:T(8,128)} %kappa_in.1, f32[20,16,128]{2,1,0:T(8,128)} %lon_in.1, f32[20,16,128]{2,1,0:T(8,128)} %lat_in.1, s32[20,16,128]{2,1,0:T(8,128)} %mask_in.1), custom_call_target="tpu_custom_call" | custom-call | tf_op jit(solution)/shard_map/pallas_call | solution.py:811
  52.4 0.7 %copy.9 = f32[20,16,128]{2,1,0:T(8,128)} copy(f32[20,16,128]{2,1,0:T(8,128)S(1)} %get-tuple-element.4) | data formatting | bytes 327680
  53.1 0.7 %copy.10 = f32[20,16,128]{2,1,0:T(8,128)} copy(f32[20,16,128]{2,1,0:T(8,128)S(1)} %get-tuple-element.5) | data formatting | bytes 327680

commit v10 on v2

--- a/solution.py
+++ b/solution.py
@@ -137,7 +137,8 @@
             self.e[z] = east
             self.n[z] = north
             self.d[z] = diag
-            self.g[z] = OMEGA / diag
+            guess = pl.reciprocal(diag, approx=True)
+            self.g[z] = guess * (2.0 * OMEGA - OMEGA * (diag * guess))
 
         self.each(horizontal, unroll)
 
@@ -246,8 +247,8 @@
     for made in fetched:
         made.start()
 
-    peers = [(2 * k, 0) for k in range(1, 16)] + [(1, 0), (-1, 0), (3, 0), (-3, 0)]
-    peers += [(0, d) for d in (1, 2, 3, -1, -2, -3)] + list(DIAGONALS)
+    peers = list(DIAGONALS) + [(1, 0), (-1, 0), (0, 1), (0, -1)]
+    peers += [(3, 0), (-3, 0)] + [(0, d) for d in (2, 3, -2, -3)] + [(2 * k, 0) for k in range(1, 16)]
     barrier = pltpu.get_barrier_semaphore()
     for dx, dy in peers:
         pl.semaphore_signal(

time: 53.3 us -> 53.5 us (level)
  no operation moved by 1% of the time
where the time goes in v10:
time: 53.5 us; the launch traced here: 53.4 us
  Pallas kernels  51.4 us (96%)
  local copies, waits for them, and re-layouts  1.33 us (2%)
  between operations  0.64 us (1%)
    pallas_call x1, Pallas kernels, shards(): pl.pallas_call(body, out_shape=(shape, shape), in_specs=[anywhere] * 5, o...  51.4 us
    unnamed x2, local copies, waits for them, and re-layouts  1.33 us

profile of v10, /device:TPU:1, one launch (start us, length us, event | category | flops | bytes accessed | tf_op | source)
XLA Modules:
  0.0 53.4 jit_solution(12351900459193952922)
XLA Ops:
  0.6 51.4 %shard_map.68 = (f32[20,16,128]{2,1,0:T(8,128)S(1)}, f32[20,16,128]{2,1,0:T(8,128)S(1)}) custom-call(f32[20,16,128]{2,1,0:T(8,128)} %source_in.1, f32[20,16,128]{2,1,0:T(8,128)} %kappa_in.1, f32[20,16,128]{2,1,0:T(8,128)} %lon_in.1, f32[20,16,128]{2,1,0:T(8,128)} %lat_in.1, s32[20,16,128]{2,1,0:T(8,128)} %mask_in.1), custom_call_target="tpu_custom_call" | custom-call | tf_op jit(solution)/shard_map/pallas_call | solution.py:764
  52.0 0.7 %copy.9 = f32[20,16,128]{2,1,0:T(8,128)} copy(f32[20,16,128]{2,1,0:T(8,128)S(1)} %get-tuple-element.4) | data formatting | bytes 327680
  52.7 0.7 %copy.10 = f32[20,16,128]{2,1,0:T(8,128)} copy(f32[20,16,128]{2,1,0:T(8,128)S(1)} %get-tuple-element.5) | data formatting | bytes 327680

commit v11 on v2

--- a/solution.py
+++ b/solution.py
@@ -725,6 +725,17 @@
         made.wait_send()
 
 
+def deliver(sol_in, resid_in, sol_out, resid_out, sem):
+    copies = [
+        pltpu.make_async_copy(sol_in, sol_out, sem.at[0]),
+        pltpu.make_async_copy(resid_in, resid_out, sem.at[1]),
+    ]
+    for made in copies:
+        made.start()
+    for made in copies:
+        made.wait()
+
+
 def level_scratch(slabs, rows, lanes):
     def vmem(count):
         return pltpu.VMEM((count, rows, lanes), F32)
@@ -760,7 +771,7 @@
     ]
     shape = jax.ShapeDtypeStruct(source.shape, F32)
     anywhere = pl.BlockSpec(memory_space=pl.ANY)
-    return pl.pallas_call(
+    found = pl.pallas_call(
         body,
         out_shape=(shape, shape),
         in_specs=[anywhere] * 5,
@@ -770,6 +781,13 @@
             collective_id=0, has_side_effects=True, vmem_limit_bytes=54848 * 1024
         ),
     )(source, kappa_sq, lon_diff, lat_diff, sea_mask)
+    return pl.pallas_call(
+        deliver,
+        out_shape=(shape, shape),
+        in_specs=[pl.BlockSpec(memory_space=pltpu.VMEM)] * 2,
+        out_specs=[anywhere] * 2,
+        scratch_shapes=[pltpu.SemaphoreType.DMA((2,))],
+    )(*found)
 
 def solution(mesh):
     spec = P(None, "tx", "ty")

time: 53.3 us -> 55.1 us (1.034)
  Pallas kernels: 51.2 us -> 53 us
    pallas_call x0 -> x1, Pallas kernels: none -> 1.73 us  [shards(): pl.pallas_call(deliver, out_shape=(shape, shape), in_specs=[pl.BlockSpec(...]
    unnamed x2 -> x4, local copies, waits for them, and re-layouts: 1.33 us -> 1.32 us
where the time goes in v11:
time: 55.1 us; the launch traced here: 54.9 us
  Pallas kernels  53 us (96%)
  local copies, waits for them, and re-layouts  1.32 us (2%)
  between operations  0.65 us (1%)
    pallas_call x1, Pallas kernels, shards(): pl.pallas_call(body, out_shape=(shape, shape), in_specs=[anywhere] * 5, o...  51.2 us
    pallas_call x1, Pallas kernels, shards(): pl.pallas_call(deliver, out_shape=(shape, shape), in_specs=[pl.BlockSpec(...  1.73 us
    unnamed x4, local copies, waits for them, and re-layouts  1.32 us

profile of v11, /device:TPU:1, one launch (start us, length us, event | category | flops | bytes accessed | tf_op | source)
XLA Modules:
  0.0 54.9 jit_solution(1113807840365606110)
XLA Ops:
  0.6 51.2 %shard_map.68 = (f32[20,16,128]{2,1,0:T(8,128)S(1)}, f32[20,16,128]{2,1,0:T(8,128)S(1)}) custom-call(f32[20,16,128]{2,1,0:T(8,128)} %source_in.1, f32[20,16,128]{2,1,0:T(8,128)} %kappa_in.1, f32[20,16,128]{2,1,0:T(8,128)} %lon_in.1, f32[20,16,128]{2,1,0:T(8,128)} %lat_in.1, s32[20,16,128]{2,1,0:T(8,128)} %mask_in.1), custom_call_target="tpu_custom_call" | custom-call | tf_op jit(solution)/shard_map/pallas_call | solution.py:774
  51.9 0.0 copy-start
  51.9 0.6 %copy-done = f32[20,16,128]{2,1,0:T(8,128)} copy-done((f32[20,16,128]{2,1,0:T(8,128)}, f32[20,16,128]{2,1,0:T(8,128)S(1)}, u32[]{:S(2)}) %copy-start) | copy-done | bytes 163864
  52.5 0.0 copy-start.1
  52.5 0.7 %copy-done.1 = f32[20,16,128]{2,1,0:T(8,128)} copy-done((f32[20,16,128]{2,1,0:T(8,128)}, f32[20,16,128]{2,1,0:T(8,128)S(1)}, u32[]{:S(2)}) %copy-start.1) | copy-done | bytes 163864
  53.2 1.7 %shard_map.69 = (f32[20,16,128]{2,1,0:T(8,128)}, f32[20,16,128]{2,1,0:T(8,128)}) custom-call(f32[20,16,128]{2,1,0:T(8,128)} %copy-done, f32[20,16,128]{2,1,0:T(8,128)} %copy-done.1), custom_call_target="tpu_custom_call" | custom-call | tf_op jit(solution)/shard_map/pallas_call | solution.py:784
Async XLA Ops:
  51.9 0.7 %copy-start = (f32[20,16,128]{2,1,0:T(8,128)}, f32[20,16,128]{2,1,0:T(8,128)S(1)}, u32[]{:S(2)}) copy-start(f32[20,16,128]{2,1,0:T(8,128)S(1)} %get-tuple-element.4.sol_in) | copy-start | bytes 491524
  52.5 0.7 %copy-start.1 = (f32[20,16,128]{2,1,0:T(8,128)}, f32[20,16,128]{2,1,0:T(8,128)S(1)}, u32[]{:S(2)}) copy-start(f32[20,16,128]{2,1,0:T(8,128)S(1)} %get-tuple-element.5.resid_in) | copy-start | bytes 491524
